TPU v7x, 32 devices: a whole 2x2x4 slice. The times are simulated.
32 devices in a mesh: rep: 2 (over y), col: 4 (over z), row: 2 (over x), sub: 2 (over core).
Axes of the slice: x: 2, y: 2, z: 4, core: 2. Of those that a mesh axis runs over, the one named last changes fastest.
Arguments:
- node_query: bfloat16 [512, 256], P(('rep', 'row')), parts along dimension 0, may hold values from -6 to 6
- query_angles: float32 [3, 512], P(None, ('rep', 'row')), parts along dimension 1, may hold values from -3.140625 to 3.140625
- query_trans: float32 [3, 512], P(None, ('rep', 'row')), parts along dimension 1, may hold values from -12 to 26
- query_chain: int32 [512], P(('rep', 'row')), parts along dimension 0, may hold values from 0 to 3
- node_key: bfloat16 [2048, 256], P(('rep', 'col', 'row', 'sub')), parts along dimension 0, may hold values from -6 to 6
- key_angles: float32 [3, 2048], P(None, ('rep', 'col')), parts along dimension 1, may hold values from -3.140625 to 3.140625
- key_trans: float32 [3, 2048], P(None, ('rep', 'col')), parts along dimension 1, may hold values from -12 to 12
- key_chain: int32 [2048], P(('rep', 'col')), parts along dimension 0, may hold values from 0 to 3, never falling along the last dimension, each value on 1 to 512 neighbouring positions
- pair_features: bfloat16 [128, 512, 1024], P('sub', ('rep', 'row'), 'col'), parts along dimension 1, may hold values from -6 to 6
- pair_mask: int32 [512, 1024], P(('rep', 'row'), 'col'), parts along dimension 0, may hold values 0 or 1
- query_weight: bfloat16 [256, 336], P(None, 'sub'), may hold values from -0.375 to 0.375
- key_weight: bfloat16 [256, 816], P(None, 'sub'), may hold values from -0.375 to 0.375
- bias_weight: bfloat16 [128, 12], P(None, 'sub'), may hold values from -0.5 to 0.5
- point_gain: float32 [12], P('sub'), may hold values from 0.25 to 2
- chain_gain: float32 [12], P('sub'), may hold values from -2 to 2
- out_weight: bfloat16 [2112, 256], P('sub'), may hold values from -0.125 to 0.125
- first_gain: float32 [256], replicated, may hold values from 0.5 to 1.5
- second_gain: float32 [256], replicated, may hold values from 0.5 to 1.5
- gate_weight: bfloat16 [256, 1024], replicated, may hold values from -0.375 to 0.375
- up_weight: bfloat16 [256, 1024], replicated, may hold values from -0.375 to 0.375
- down_weight: bfloat16 [1024, 256], replicated, may hold values from -0.1875 to 0.1875
- edge_query_weight: bfloat16 [256, 256], replicated, may hold values from -0.375 to 0.375
- edge_key_weight: bfloat16 [256, 256], replicated, may hold values from -0.375 to 0.375
- edge_in_weight: bfloat16 [128, 256], replicated, may hold values from -0.5 to 0.5
- edge_out_weight: bfloat16 [256, 128], replicated, may hold values from -0.375 to 0.375
Outputs:
- updated_nodes: bfloat16 [512, 256], P(('rep', 'row')), parts along dimension 0
- updated_pairs: bfloat16 [128, 512, 1024], P('sub', ('rep', 'row'), 'col'), parts along dimension 1
There are 2 independent parts, one for each index of `rep`. A program takes and returns all parts, laid end to end along the dimension named above; an argument that names none is the same for every part. Nothing has to cross between parts.
All inputs are finite; a program needn't handle non-finite values. No bound on the sum of `pair_mask` on one device may be relied on, other than what follows from the above.
Results may differ from a plain program's by a relative error of at most 0.006.
Values may be sent and summed in bfloat16 or wider, within the bound.
No kernel may reach another device: no remote copies, remote signals or barrier semaphores. Data moves between devices by JAX's collectives and lax.ppermute only.
A program may use at most 128 MiB of HBM per device.

v0:
```python
import math

import jax
import jax.numpy as jnp
from jax import lax
from jax.sharding import PartitionSpec as P

CH = 16
PQ = 4
PV = 8


linear_scale = math.sqrt(1.0 / 3.0)
masked_score = -1000000000.0
norm_epsilon = 1e-05


def rotations(angles):
    cos_yaw = jnp.cos(angles[0])
    sin_yaw = jnp.sin(angles[0])
    cos_pitch = jnp.cos(angles[1])
    sin_pitch = jnp.sin(angles[1])
    cos_roll = jnp.cos(angles[2])
    sin_roll = jnp.sin(angles[2])
    first_row = jnp.stack(
        [
            cos_yaw * cos_pitch,
            cos_yaw * sin_pitch * sin_roll - sin_yaw * cos_roll,
            cos_yaw * sin_pitch * cos_roll + sin_yaw * sin_roll,
        ],
        0,
    )
    second_row = jnp.stack(
        [
            sin_yaw * cos_pitch,
            sin_yaw * sin_pitch * sin_roll + cos_yaw * cos_roll,
            sin_yaw * sin_pitch * cos_roll - cos_yaw * sin_roll,
        ],
        0,
    )
    third_row = jnp.stack([-sin_pitch, cos_pitch * sin_roll, cos_pitch * cos_roll], 0)
    return jnp.stack([first_row, second_row, third_row], 0)


def layer_norm(values, gain):
    centred = values - jnp.mean(values, axis=-1, keepdims=True)
    variance = jnp.mean(centred * centred, axis=-1, keepdims=True)
    return centred * lax.rsqrt(variance + norm_epsilon) * gain


def product(left, right):
    return jnp.dot(left, right, preferred_element_type=jnp.float32)


def leading_product(left, right):
    return lax.dot_general(
        left, right, (((0,), (0,)), ((), ())), preferred_element_type=jnp.float32
    )


def row_window(values, begin, count, axis):
    return lax.dynamic_slice_in_dim(values, begin, count, axis)


def finish_nodes(
    sums,
    totals,
    node_rows,
    angle_rows,
    trans_rows,
    out_weight,
    first_gain,
    second_gain,
    gate_weight,
    up_weight,
    down_weight,
):
    row_count, heads = totals.shape
    attended = sums / totals[:, :, None]
    global_points = (
        attended[:, :, CH : CH + 3 * PV].reshape(row_count, heads, 3, PV)
        - trans_rows.T[:, None, :, None]
    )
    local_points = jnp.einsum(
        "bai,ihbp->ihap", rotations(angle_rows), global_points, precision=lax.Precision.HIGHEST
    )
    point_norms = jnp.sqrt(1.0 + jnp.sum(local_points * local_points, axis=2))
    features = jnp.concatenate(
        [
            attended[:, :, :CH],
            local_points.reshape(row_count, heads, 3 * PV),
            point_norms,
            attended[:, :, CH + 3 * PV :],
        ],
        axis=2,
    )
    features = features.reshape(row_count, heads * features.shape[2]).astype(jnp.bfloat16)
    projected = lax.psum(product(features, out_weight), "sub")
    first_nodes = layer_norm(node_rows.astype(jnp.float32) + projected, first_gain)
    first_rounded = first_nodes.astype(jnp.bfloat16)
    hidden = (
        jax.nn.silu(product(first_rounded, gate_weight)) * product(first_rounded, up_weight)
    ).astype(jnp.bfloat16)
    return layer_norm(first_nodes + product(hidden, down_weight), second_gain).astype(jnp.bfloat16)


def attend(
    node_rows,
    angle_rows,
    trans_rows,
    chain_rows,
    mask_rows,
    key_rows,
    key_angles,
    key_trans,
    key_chain,
    tile_pairs,
    query_weight,
    key_weight,
    bias_weight,
    point_gain,
    chain_gain,
):
    highest = lax.Precision.HIGHEST
    heads = point_gain.shape[0]
    query_count, key_count = mask_rows.shape
    query_proj = product(node_rows, query_weight).reshape(query_count, heads, CH + 3 * PQ)
    query_vectors = query_proj[:, :, :CH].astype(jnp.bfloat16)
    query_points = (
        jnp.einsum(
            "abi,ihbp->ihap",
            rotations(angle_rows),
            query_proj[:, :, CH:].reshape(query_count, heads, 3, PQ),
            precision=highest,
        )
        + trans_rows.T[:, None, :, None]
    )
    query_points = query_points.reshape(query_count, heads, 3 * PQ)
    key_proj = product(key_rows, key_weight).reshape(key_count, heads, 2 * CH + 3 * PQ + 3 * PV)
    key_vectors = key_proj[:, :, :CH].astype(jnp.bfloat16)
    value_vectors = key_proj[:, :, CH : 2 * CH].astype(jnp.bfloat16)
    key_frames = rotations(key_angles)
    key_points = (
        jnp.einsum(
            "abi,ihbp->ihap",
            key_frames,
            key_proj[:, :, 2 * CH : 2 * CH + 3 * PQ].reshape(key_count, heads, 3, PQ),
            precision=highest,
        )
        + key_trans.T[:, None, :, None]
    )
    key_points = key_points.reshape(key_count, heads, 3 * PQ)
    value_points = (
        jnp.einsum(
            "abi,ihbp->ihap",
            key_frames,
            key_proj[:, :, 2 * CH + 3 * PQ :].reshape(key_count, heads, 3, PV),
            precision=highest,
        )
        + key_trans.T[:, None, :, None]
    )
    value_points = value_points.reshape(key_count, heads, 3 * PV)
    bias = leading_product(bias_weight, tile_pairs)
    inner = jnp.einsum(
        "ihc,jhc->hij", query_vectors, key_vectors, preferred_element_type=jnp.float32
    ) / math.sqrt(CH)
    cross = jnp.einsum("ihd,jhd->hij", query_points, key_points, precision=highest)
    query_squares = jnp.sum(query_points * query_points, axis=2).T
    key_squares = jnp.sum(key_points * key_points, axis=2).T
    distance = query_squares[:, :, None] + key_squares[:, None, :] - 2.0 * cross
    same_chain = (chain_rows[:, None] == key_chain[None, :]).astype(jnp.float32)
    point_scale = point_gain * (math.sqrt(2.0 / (9.0 * PQ)) / 2.0)
    scores = linear_scale * (
        inner
        + bias
        + chain_gain[:, None, None] * same_chain[None]
        - point_scale[:, None, None] * distance
    )
    scores = jnp.where(mask_rows[None] == 1, scores, masked_score)
    row_max = lax.pmax(jnp.max(scores, axis=2), "col")
    weights = jnp.exp(scores - row_max[:, :, None])
    totals = jnp.sum(weights, axis=2).T
    rounded_weights = weights.astype(jnp.bfloat16)
    vector_part = jnp.einsum(
        "hij,jhc->ihc", rounded_weights, value_vectors, preferred_element_type=jnp.float32
    )
    point_part = jnp.einsum("hij,jhd->ihd", weights, value_points, precision=highest)
    pair_part = lax.dot_general(
        rounded_weights,
        tile_pairs,
        (((2,), (2,)), ((1,), (1,))),
        preferred_element_type=jnp.float32,
    )
    sums = jnp.concatenate([vector_part, point_part, pair_part], axis=2)
    return (totals, sums)


def node_section(
    totals,
    sums,
    node_rows,
    angle_rows,
    trans_rows,
    out_weight,
    first_gain,
    second_gain,
    gate_weight,
    up_weight,
    down_weight,
):
    row_count = node_rows.shape[0]
    share = row_count // lax.axis_size("col")
    begin = lax.axis_index("col") * share
    total_share, sum_share = (
        lax.psum_scatter(totals, "col", scatter_dimension=0, tiled=True),
        lax.psum_scatter(sums, "col", scatter_dimension=0, tiled=True),
    )
    node_share = finish_nodes(
        sum_share,
        total_share,
        row_window(node_rows, begin, share, 0),
        row_window(angle_rows, begin, share, 1),
        row_window(trans_rows, begin, share, 1),
        out_weight,
        first_gain,
        second_gain,
        gate_weight,
        up_weight,
        down_weight,
    )
    return lax.all_gather(node_share, "col", axis=0, tiled=True)


def shards(
    node_query,
    query_angles,
    query_trans,
    query_chain,
    node_key,
    key_angles,
    key_trans,
    key_chain,
    pair_features,
    pair_mask,
    query_weight,
    key_weight,
    bias_weight,
    point_gain,
    chain_gain,
    out_weight,
    first_gain,
    second_gain,
    gate_weight,
    up_weight,
    down_weight,
    edge_query_weight,
    edge_key_weight,
    edge_in_weight,
    edge_out_weight,
):
    key_rows = lax.all_gather(node_key, ("row", "sub"), axis=0, tiled=True)
    query_count = pair_mask.shape[0]
    full_pairs = lax.all_gather(pair_features, "sub", axis=0, tiled=True)
    totals, sums = attend(
        node_query,
        query_angles,
        query_trans,
        query_chain,
        pair_mask,
        key_rows,
        key_angles,
        key_trans,
        key_chain,
        full_pairs,
        query_weight,
        key_weight,
        bias_weight,
        point_gain,
        chain_gain,
    )
    new_nodes = node_section(
        totals,
        sums,
        node_query,
        query_angles,
        query_trans,
        out_weight,
        first_gain,
        second_gain,
        gate_weight,
        up_weight,
        down_weight,
    )
    channel_share = pair_features.shape[0]
    edge_queries = product(new_nodes, edge_query_weight)
    edge_keys = product(key_rows, edge_key_weight)
    out_columns = row_window(
        edge_out_weight, lax.axis_index("sub") * channel_share, channel_share, 1
    )
    block = math.gcd(query_count, 32)

    def edge_step(index, result):
        begin = index * block
        pair_block = row_window(full_pairs, begin, block, 1)
        own_block = row_window(pair_features, begin, block, 1)
        edge_pre = leading_product(edge_in_weight, pair_block)
        edge_pre = (
            edge_pre
            + row_window(edge_queries, begin, block, 0).T[:, :, None]
            + edge_keys.T[:, None, :]
        )
        edge_hidden = jnp.maximum(edge_pre, 0.0).astype(jnp.bfloat16)
        edge_out = leading_product(out_columns, edge_hidden)
        fresh = (own_block.astype(jnp.float32) + edge_out).astype(jnp.bfloat16)
        return lax.dynamic_update_slice_in_dim(result, fresh, begin, 1)

    updated_pairs = lax.fori_loop(0, query_count // block, edge_step, jnp.zeros_like(pair_features))
    return (new_nodes, updated_pairs)


def solution(mesh):
    return jax.shard_map(
        shards,
        mesh=mesh,
        in_specs=(
            P(("rep", "row"), None),
            P(None, ("rep", "row")),
            P(None, ("rep", "row")),
            P(("rep", "row")),
            P(("rep", "col", "row", "sub"), None),
            P(None, ("rep", "col")),
            P(None, ("rep", "col")),
            P(("rep", "col")),
            P("sub", ("rep", "row"), "col"),
            P(("rep", "row"), "col"),
            P(None, "sub"),
            P(None, "sub"),
            P(None, "sub"),
            P("sub"),
            P("sub"),
            P("sub", None),
            P(),
            P(),
            P(),
            P(),
            P(),
            P(),
            P(),
            P(),
            P(),
        ),
        out_specs=(P(("rep", "row"), None), P("sub", ("rep", "row"), "col")),
        check_vma=False,
    )
```

profile of v0, /device:TPU:0, one launch (start us, length us, event | category | flops | bytes accessed | tf_op | source)
XLA Modules:
  0.0 185.6 jit_solution(11751437756029664675)
XLA Ops:
  7.2 6.6 %copy.185 = bf16[64,128,256]{2,0,1:T(8,128)(2,1)} copy(bf16[64,128,256]{2,1,0:T(8,128)(2,1)} %param.35) | data formatting | bytes 8388608 | tf_op args[8]
  13.9 0.6 copy-done.15
  14.6 6.5 %all_gather.9 = bf16[256,256]{1,0:T(8,128)(2,1)S(1)} all-gather(bf16[64,256]{1,0:T(8,128)(2,1)S(1)} %copy-done.15), channel_id=1, replica_groups=mesh['rep'=2,'col'=4,'row'=2,'sub'=2] {'row','sub'}, dimensions={0}, use_global_device_ids=true | all-gather | bytes 163840 | tf_op jit(solution)/shard_map/all_gather | solution.py:261
  21.4 0.8 convert.20
  22.2 0.7 copy.189
  23.5 0.9 copy.215
  24.9 0.6 copy.187
  25.5 4.0 %multiply_reduce_fusion.1 = (f32[128,6]{1,0:T(8,128)}, f32[128,6,3,4]{1,2,3,0:T(4,128)S(1)}) fusion(f32[128,3]{1,0:T(8,128)} %copy.189, f32[128,6,3,4]{1,2,3,0:T(4,128)S(1)} %copy.187, f32[3,3,128,1]{1,0,3,2:T(4,128)} %copy.215), kind=kOutput, calls=%fused_computation.39 | convolution fusion | flops 358656 | bytes 82944 | tf_op jit(solution)/shard_map/abi,ihbp->ihap/dot_general | solution.py:130
  29.5 1.5 copy.190
  31.0 0.4 copy.195
  31.4 0.6 reshape.108
  32.0 1.9 %copy.191 = f32[256,6,3,4]{1,2,3,0:T(4,128)} copy(f32[256,6,3,4]{0,3,2,1:T(4,128)S(1)} %reshape.107) | data formatting | bytes 147456 | tf_op jit(solution)/shard_map/reshape | solution.py:147
  33.9 6.3 %multiply_reduce_fusion = (f32[256,6]{1,0:T(8,128)S(1)}, f32[256,6,3,4]{1,2,3,0:T(4,128)S(1)}) fusion(f32[256,3]{1,0:T(8,128)S(1)} %copy.193, f32[256,6,3,4]{1,2,3,0:T(4,128)} %copy.191, f32[3,3,256,1]{1,0,3,2:T(4,128)S(1)} %copy.216), kind=kOutput, calls=%fused_computation.19 | convolution fusion | flops 717312 | bytes 165888 | tf_op jit(solution)/shard_map/abi,ihbp->ihap/dot_general | solution.py:144
  40.1 0.7 copy.194
  40.8 0.8 copy.196
  41.6 0.9 slice_bitcast_fusion
  42.6 2.7 %copy.197 = f32[256,6,3,8]{3,2,1,0:T(4,128)} copy(f32[256,6,3,8]{0,3,2,1:T(8,128)S(1)} %slice_bitcast_fusion) | data formatting | bytes 294912 | tf_op jit(solution)/shard_map/reshape | solution.py:157
  45.3 8.5 %add_bitcast_fusion = f32[256,6,3,8]{3,2,1,0:T(4,128)} fusion(f32[256,6,3,8]{3,2,1,0:T(4,128)} %copy.197, f32[3,3,256,1]{1,0,3,2:T(4,128)S(1)} %copy.216, f32[256,3]{1,0:T(8,128)S(1)} %copy.193), kind=kOutput, calls=%fused_computation.18 | convolution fusion | flops 1363968 | bytes 307200 | tf_op jit(solution)/shard_map/abi,ihbp->ihap/dot_general | solution.py:154
  53.8 3.0 %copy.200 = f32[256,6,3,8]{0,3,2,1:T(8,128)S(1)} copy(f32[256,6,3,8]{3,2,1,0:T(4,128)} %add_bitcast_fusion) | data formatting | bytes 294912 | tf_op jit(solution)/shard_map/add | solution.py:154
  57.1 0.9 fusion.30
  58.0 4.6 %fusion.63 = f32[6,128,256]{2,0,1:T(8,128)S(1)} fusion(bf16[128,128,256]{2,0,1:T(8,128)(2,1)} %all-gather.2.cloned.1.call-done, bf16[128,6]{0,1:T(8,128)(2,1)S(1)} %copy-done.23), kind=kOutput, calls=%fused_computation.91 | convolution fusion | flops 50331648 | bytes 9176576 | tf_op jit(solution)/shard_map/dot_general | solution.py:56
  62.6 1.5 fusion.83
  64.1 12.4 %pmax.7 = f32[6,128]{1,0:T(8,128)S(1)} all-reduce(f32[6,128]{1,0:T(8,128)S(1)} %get-tuple-element.252), channel_id=1, replica_groups=mesh['rep'=2,'col'=4,'row'=2,'sub'=2] {'col'}, use_global_device_ids=true, to_apply=%region_3.4 | all-reduce | flops 768 | bytes 6144 | tf_op jit(solution)/shard_map/pmax | solution.py:180
  76.5 0.3 fusion.34
  76.8 0.9 convolution_bitcast_fusion
  77.6 1.0 convolution_bitcast_fusion.1
  78.7 0.7 copy.228
  80.0 5.7 %fusion.36 = f32[128,6,128]{2,1,0:T(8,128)S(1)} fusion(bf16[128,128,256]{2,0,1:T(8,128)(2,1)} %all-gather.2.cloned.1.call-done, bf16[6,128,256]{2,1,0:T(8,128)(2,1)S(1)} %get-tuple-element.221), kind=kOutput, calls=%fused_computation.43 | convolution fusion | flops 50331648 | bytes 9175040 | tf_op jit(solution)/shard_map/dot_general | solution.py:188
  85.7 1.6 pad_maximum_fusion
  88.0 8.8 %reduce-scatter.7.cloned.1.call-done = f32[32,6]{1,0:T(8,128)} async-done(((f32[128,6]{1,0:T(8,128)}), f32[32,6]{1,0:T(8,128)}) %reduce-scatter.7.cloned.1.call-update) | async-done | bytes 784
  96.8 0.8 copy.229
  97.6 27.6 %reduce-scatter.5.cloned.1.call-done = f32[32,6,168]{2,1,0:T(8,128)} async-done(((f32[128,6,168]{2,1,0:T(8,128)}), f32[32,6,168]{2,1,0:T(8,128)}) %reduce-scatter.5.cloned.1.call-update) | async-done | bytes 129040 | tf_op jit(solution)/shard_map/reduce_scatter | solution.py:216
  125.2 1.2 copy.204
  126.7 1.0 convert_bitcast_fusion
  128.4 3.4 %psum.7 = f32[32,256]{1,0:T(8,128)S(1)} all-reduce(f32[32,256]{1,0:T(8,128)S(1)} %fusion.89), channel_id=1, replica_groups=mesh['rep'=2,'col'=4,'row'=2,'sub'=2] {'sub'}, use_global_device_ids=true, to_apply=%region_8.9 | all-reduce | flops 8192 | bytes 65536 | tf_op jit(solution)/shard_map/psum | solution.py:98
  132.4 1.6 fusion.84
  134.2 13.1 %all_gather.11 = bf16[128,256]{1,0:T(8,128)(2,1)S(1)} all-gather(bf16[32,256]{1,0:T(8,128)(2,1)S(1)} %multiply_convert_fusion), channel_id=1, replica_groups=mesh['rep'=2,'col'=4,'row'=2,'sub'=2] {'col'}, dimensions={0}, use_global_device_ids=true | all-gather | bytes 81920 | tf_op jit(solution)/shard_map/all_gather | solution.py:231
  147.5 2.5 %broadcast_in_dim.20.clone = bf16[64,128,256]{2,1,0:T(8,128)(2,1)} broadcast(bf16[]{:T(256)} %constant.79.clone.1), dimensions={} | broadcast | bytes 4194306 | tf_op jit(solution)/shard_map/broadcast_in_dim | solution.py:317
  150.1 28.4 %while.13 = (s32[]{:T(128)}, bf16[64,128,256]{2,1,0:T(8,128)(2,1)}, bf16[64,128,256]{2,0,1:T(8,128)(2,1)}, bf16[128,128,256]{2,0,1:T(8,128)(2,1)}, bf16[128,256]...) while((s32[]{:T(128)}, bf16[64,128,256]{2,1,0:T(8,128)(2,1)}, ...), condition=%wide.region_14.15_spmd, body=%wide.region_13.14_spmd.sunk | while | flops 815267840 | bytes 6751403 | solution.py:317
  150.1 5.5 %fusion.127 = bf16[64,32,256]{2,0,1:T(8,128)(2,1)S(1)} fusion(f32[256,256]{0,1:T(8,128)S(1)} %bitcast.137, f32[256,32]{0,1:T(8,128)S(1)} %dynamic-slice_bitcast_fusion.3, bf16[128,128,256]{2,0,1:T(8,128)(2,1)} %get-tuple-element.340, s32[]{:T(128)S(6)} %select_n.27, bf16[64,128,256]{2,0,1:T(8,128)(2,1)} %get-tuple-element.339, ...), kind=kOutput, calls=%fused_computation.10.clone.1 | convolution fusion | flops 815267840 | bytes 4588544 | tf_op jit(solution)/shard_map/while/body/eval_jaxpr/dot_general | solution.py:56
  155.6 1.6 copy_dynamic-update-slice_fusion.2
  157.2 5.5 %fusion.127 = bf16[64,32,256]{2,0,1:T(8,128)(2,1)S(1)} fusion(f32[256,256]{0,1:T(8,128)S(1)} %bitcast.137, f32[256,32]{0,1:T(8,128)S(1)} %dynamic-slice_bitcast_fusion.3, bf16[128,128,256]{2,0,1:T(8,128)(2,1)} %get-tuple-element.340, s32[]{:T(128)S(6)} %select_n.27, bf16[64,128,256]{2,0,1:T(8,128)(2,1)} %get-tuple-element.339, ...), kind=kOutput, calls=%fused_computation.10.clone.1 | convolution fusion | flops 815267840 | bytes 4588544 | tf_op jit(solution)/shard_map/while/body/eval_jaxpr/dot_general | solution.py:56
  162.7 1.6 copy_dynamic-update-slice_fusion.2
  164.3 5.5 %fusion.127 = bf16[64,32,256]{2,0,1:T(8,128)(2,1)S(1)} fusion(f32[256,256]{0,1:T(8,128)S(1)} %bitcast.137, f32[256,32]{0,1:T(8,128)S(1)} %dynamic-slice_bitcast_fusion.3, bf16[128,128,256]{2,0,1:T(8,128)(2,1)} %get-tuple-element.340, s32[]{:T(128)S(6)} %select_n.27, bf16[64,128,256]{2,0,1:T(8,128)(2,1)} %get-tuple-element.339, ...), kind=kOutput, calls=%fused_computation.10.clone.1 | convolution fusion | flops 815267840 | bytes 4588544 | tf_op jit(solution)/shard_map/while/body/eval_jaxpr/dot_general | solution.py:56
  169.8 1.6 copy_dynamic-update-slice_fusion.2
  171.4 5.5 %fusion.127 = bf16[64,32,256]{2,0,1:T(8,128)(2,1)S(1)} fusion(f32[256,256]{0,1:T(8,128)S(1)} %bitcast.137, f32[256,32]{0,1:T(8,128)S(1)} %dynamic-slice_bitcast_fusion.3, bf16[128,128,256]{2,0,1:T(8,128)(2,1)} %get-tuple-element.340, s32[]{:T(128)S(6)} %select_n.27, bf16[64,128,256]{2,0,1:T(8,128)(2,1)} %get-tuple-element.339, ...), kind=kOutput, calls=%fused_computation.10.clone.1 | convolution fusion | flops 815267840 | bytes 4588544 | tf_op jit(solution)/shard_map/while/body/eval_jaxpr/dot_general | solution.py:56
  176.9 1.6 copy_dynamic-update-slice_fusion.2
  178.5 0.6 copy.248
  (130 shorter events, 4.8 us)
Async XLA Ops:
  7.2 121.0 %copy-start = (bf16[1056,256]{1,0:T(8,128)(2,1)S(1)}, bf16[1056,256]{1,0:T(8,128)(2,1)}, u32[]{:S(2)}) copy-start(bf16[1056,256]{1,0:T(8,128)(2,1)} %param.42) | copy-start | bytes 1622020
  7.2 50.9 %all-gather.2.cloned.1.call-start = ((), (), s32[]{:S(2)}) async-start(), calls=%async_computation.2 | async-start | bytes 12582912 | tf_op jit(solution)/shard_map/all_gather | solution.py:263
  13.8 0.8 copy-start.15
  13.8 7.2 %copy-start.5 = (bf16[256,408]{0,1:T(8,128)(2,1)S(1)}, bf16[256,408]{0,1:T(8,128)(2,1)}, u32[]{:S(2)}) copy-start(bf16[256,408]{0,1:T(8,128)(2,1)} %param.38) | copy-start | bytes 626692
  13.8 8.4 %copy-start.20 = (f32[3,128]{1,0:T(4,128)S(1)}, f32[3,128]{1,0:T(4,128)}, u32[]{:S(2)}) copy-start(f32[3,128]{1,0:T(4,128)} %param.29) | copy-start | bytes 4612
  13.8 9.1 %copy-start.6 = (bf16[128,256]{1,0:T(8,128)(2,1)S(1)}, bf16[128,256]{1,0:T(8,128)(2,1)}, u32[]{:S(2)}) copy-start(bf16[128,256]{1,0:T(8,128)(2,1)} %param.27) | copy-start | bytes 196612
  13.8 9.1 %copy-start.12 = (bf16[256,168]{0,1:T(8,128)(2,1)S(1)}, bf16[256,168]{0,1:T(8,128)(2,1)}, u32[]{:S(2)}) copy-start(bf16[256,168]{0,1:T(8,128)(2,1)} %param.37) | copy-start | bytes 258052
  13.8 9.3 %copy-start.22 = (f32[3,256]{1,0:T(4,128)S(1)}, f32[3,256]{1,0:T(4,128)}, u32[]{:S(2)}) copy-start(f32[3,256]{1,0:T(4,128)} %param.33) | copy-start | bytes 9220
  13.8 9.5 %copy-start.17 = (f32[3,128]{1,0:T(4,128)S(1)}, f32[3,128]{1,0:T(4,128)}, u32[]{:S(2)}) copy-start(f32[3,128]{1,0:T(4,128)} %param.28) | copy-start | bytes 4612
  13.8 10.5 %copy-start.19 = (f32[3,256]{1,0:T(4,128)S(1)}, f32[3,256]{1,0:T(4,128)}, u32[]{:S(2)}) copy-start(f32[3,256]{1,0:T(4,128)} %param.32) | copy-start | bytes 9220
  13.9 82.9 %reduce-scatter.7.cloned.1.call-start = ((), (), s32[]{:S(2)}) async-start(), calls=%async_computation.4 | async-start | bytes 81920
  21.3 3.6 %copy-start.1 = (f32[256,6,68]{0,2,1:T(8,128)}, f32[256,6,68]{0,2,1:T(8,128)S(1)}, u32[]{:S(2)}) copy-start(f32[256,6,68]{0,2,1:T(8,128)S(1)} %reshape.104) | copy-start | bytes 1253380
  23.1 1.8 copy-start.3
  45.2 11.6 %copy-start.18 = (f32[3,128]{1,0:T(4,128)S(1)}, f32[3,128]{1,0:T(4,128)}, u32[]{:S(2)}) copy-start(f32[3,128]{1,0:T(4,128)} %param.28) | copy-start | bytes 4612
  45.2 11.6 %copy-start.21 = (f32[3,128]{1,0:T(4,128)S(1)}, f32[3,128]{1,0:T(4,128)}, u32[]{:S(2)}) copy-start(f32[3,128]{1,0:T(4,128)} %param.29) | copy-start | bytes 4612
  45.2 11.7 %copy-start.31 = (f32[6]{0:T(128)S(1)}, f32[6]{0:T(128)}, u32[]{:S(2)}) copy-start(f32[6]{0:T(128)} %param.40) | copy-start | bytes 76
  45.3 11.7 %copy-start.9 = (s32[128,256]{1,0:T(8,128)S(1)}, s32[128,256]{1,0:T(8,128)}, u32[]{:S(2)}) copy-start(s32[128,256]{1,0:T(8,128)} %param.36) | copy-start | bytes 393220
  45.3 11.7 %copy-start.24 = (s32[256]{0:T(256)S(1)}, s32[256]{0:T(256)}, u32[]{:S(2)}) copy-start(s32[256]{0:T(256)} %param.34) | copy-start | bytes 3076
  45.3 11.7 %copy-start.27 = (s32[128]{0:T(128)S(1)}, s32[128]{0:T(128)}, u32[]{:S(2)}) copy-start(s32[128]{0:T(128)} %param.30) | copy-start | bytes 1540
  45.3 11.8 %copy-start.8 = (f32[128,6,12]{0,2,1:T(8,128)S(1)}, f32[128,6,12]{0,2,1:T(8,128)}, u32[]{:S(2)}) copy-start(f32[128,6,12]{0,2,1:T(8,128)} %reshape.108) | copy-start | bytes 110596
  45.3 11.8 %copy-start.14 = (f32[6,256]{1,0:T(8,128)S(1)}, f32[6,256]{1,0:T(8,128)}, u32[]{:S(2)}) copy-start(f32[6,256]{1,0:T(8,128)} %copy.194) | copy-start | bytes 18436
  45.3 11.8 %copy-start.16 = (f32[6,128]{1,0:T(8,128)S(1)}, f32[6,128]{1,0:T(8,128)}, u32[]{:S(2)}) copy-start(f32[6,128]{1,0:T(8,128)} %copy.190) | copy-start | bytes 9220
  45.3 12.7 %copy-start.23 = (bf16[128,6]{0,1:T(8,128)(2,1)S(1)}, bf16[128,6]{0,1:T(8,128)(2,1)}, u32[]{:S(2)}) copy-start(bf16[128,6]{0,1:T(8,128)(2,1)} %param.39) | copy-start | bytes 4612
  58.0 4.6 %copy-start.4 = (f32[128,6,28]{0,2,1:T(8,128)S(1)}, f32[128,6,28]{0,2,1:T(8,128)}, u32[]{:S(2)}) copy-start(f32[128,6,28]{0,2,1:T(8,128)} %copy-done.3) | copy-start | bytes 258052
  58.0 4.6 %copy-start.28 = (f32[6]{0:T(128)S(1)}, f32[6]{0:T(128)}, u32[]{:S(2)}) copy-start(f32[6]{0:T(128)} %param.41) | copy-start | bytes 76
  79.4 45.8 %reduce-scatter.5.cloned.1.call-start = ((), (), s32[]{:S(2)}) async-start(), calls=%async_computation.3 | async-start | bytes 1310720 | tf_op jit(solution)/shard_map/reduce_scatter | solution.py:216
  80.0 7.7 %copy-start.13 = (bf16[256,128]{1,0:T(8,128)(2,1)S(1)}, bf16[256,128]{1,0:T(8,128)(2,1)}, u32[]{:S(2)}) copy-start(bf16[256,128]{1,0:T(8,128)(2,1)} %param.51) | copy-start | bytes 196612
  80.0 7.8 %copy-start.11 = (bf16[256,256]{1,0:T(8,128)(2,1)S(1)}, bf16[256,256]{1,0:T(8,128)(2,1)}, u32[]{:S(2)}) copy-start(bf16[256,256]{1,0:T(8,128)(2,1)} %param.49) | copy-start | bytes 393220
  87.3 44.5 %copy-start.7 = (bf16[128,256]{1,0:T(8,128)(2,1)S(1)}, bf16[128,256]{1,0:T(8,128)(2,1)}, u32[]{:S(2)}) copy-start(bf16[128,256]{1,0:T(8,128)(2,1)} %param.27) | copy-start | bytes 196612
  87.3 44.9 %copy-start.2 = (bf16[256,1024]{1,0:T(8,128)(2,1)S(1)}, bf16[256,1024]{1,0:T(8,128)(2,1)}, u32[]{:S(2)}) copy-start(bf16[256,1024]{1,0:T(8,128)(2,1)} %param.45) | copy-start | bytes 1572868
  87.3 44.9 %copy-start.25 = (f32[256]{0:T(256)S(1)}, f32[256]{0:T(256)}, u32[]{:S(2)}) copy-start(f32[256]{0:T(256)} %param.43) | copy-start | bytes 3076
  87.3 45.1 %copy-start.29 = (bf16[1024,256]{1,0:T(8,128)(2,1)S(1)}, bf16[1024,256]{1,0:T(8,128)(2,1)}, u32[]{:S(2)}) copy-start(bf16[1024,256]{1,0:T(8,128)(2,1)} %param.47) | copy-start | bytes 1572868
  87.8 46.3 %copy-start.26 = (f32[256]{0:T(256)S(1)}, f32[256]{0:T(256)}, u32[]{:S(2)}) copy-start(f32[256]{0:T(256)} %param.44) | copy-start | bytes 3076
  88.0 59.3 %copy-start.10 = (bf16[256,256]{1,0:T(8,128)(2,1)S(1)}, bf16[256,256]{1,0:T(8,128)(2,1)}, u32[]{:S(2)}) copy-start(bf16[256,256]{1,0:T(8,128)(2,1)} %param.48) | copy-start | bytes 393220
  128.0 22.0 %copy-start.30 = (bf16[128,256]{1,0:T(8,128)(2,1)S(1)}, bf16[128,256]{1,0:T(8,128)(2,1)}, u32[]{:S(2)}) copy-start(bf16[128,256]{1,0:T(8,128)(2,1)} %param.50) | copy-start | bytes 196612
Sparse Core Ops, SparseCore 0:
  14.0 22.5 all-gather.1
  79.6 17.2 reduce-scatter.6
  99.8 25.3 reduce-scatter.4
where the time goes:
time: 186 us
  matrix products  59.1 us (32%)
  waiting for transfers between devices  36.4 us (20%)
  local copies, waits for them, and re-layouts  35.9 us (19%)
  blocking collectives  35.4 us (19%)
  between operations  14.5 us (8%)
  other arithmetic  4.1 us (2%)
    reduce_scatter x1, waiting for transfers between devices, node_section(): lax.psum_scatter(sums, 'col', scatter_dimension=0, tiled=True)  27.6 us
    dot_general x5, matrix products, leading_product(): lax.dot_general(left, right, (((0,), (0,)), ((), ())), preferred_element_...  26.7 us
    all_gather x1, blocking collectives, node_section(): return lax.all_gather(node_share, 'col', axis=0, tiled=True)  13.1 us
    pmax x1, blocking collectives, attend(): row_max = lax.pmax(jnp.max(scores, axis=2), 'col')  12.4 us
    unnamed x69, local copies, waits for them, and re-layouts  9.61 us
    unnamed x4, waiting for transfers between devices  8.82 us
    dot_general x1, matrix products, attend(): jnp.einsum('abi,ihbp->ihap', key_frames, key_proj[:, :, 2 * CH + 3 * PQ:]...  8.52 us
    all_gather x1, blocking collectives, shards(): key_rows = lax.all_gather(node_key, ('row', 'sub'), axis=0, tiled=True)  6.47 us
  transfers between devices with their start and end apart: 3, of which 2 were waited for; matrix products, arithmetic and copies ran while one was open for 25% of the time, Pallas kernels for 0%

commit v1 on v0

v1 whole, which is shorter than its diff:
```python
import functools
import math

import jax
import jax.numpy as jnp
from jax import lax
from jax.experimental import pallas as pl
from jax.experimental.pallas import tpu as pltpu
from jax.sharding import PartitionSpec as P

CH = 16
PQ = 4
PV = 8
QCOLS = CH + 3 * PQ
KCOLS = 2 * CH + 3 * PQ + 3 * PV
FEATURES = CH + 4 * PV
SLOT = 64
ROWS = 16

linear_scale = math.sqrt(1.0 / 3.0)
masked_score = -1000000000.0
norm_epsilon = 1e-05
point_factor = math.sqrt(2.0 / (9.0 * PQ)) / 2.0

f32 = jnp.float32
bf16 = jnp.bfloat16


def params(mib):
    return pltpu.CompilerParams(vmem_limit_bytes=mib * 2**20)


def dot(left, right):
    return jnp.dot(left, right, preferred_element_type=f32)


def dot_nt(left, right):
    return lax.dot_general(left, right, (((1,), (1,)), ((), ())), preferred_element_type=f32)


def dot_tn(left, right):
    return lax.dot_general(left, right, (((0,), (0,)), ((), ())), preferred_element_type=f32)


def dot_tt(left, right):
    return lax.dot_general(left, right, (((0,), (1,)), ((), ())), preferred_element_type=f32)


def iota(shape, axis):
    return lax.broadcasted_iota(jnp.int32, shape, axis)


def rounded(values):
    return values.astype(bf16).astype(f32)


def rotation_rows(angles):
    cos, sin = jnp.cos(angles), jnp.sin(angles)
    cy, cp, cr = cos[0:1], cos[1:2], cos[2:3]
    sy, sp, sr = sin[0:1], sin[1:2], sin[2:3]
    return [
        [cy * cp, cy * sp * sr - sy * cr, cy * sp * cr + sy * sr],
        [sy * cp, sy * sp * sr + cy * cr, sy * sp * cr - cy * sr],
        [-sp, cp * sr, cp * cr],
    ]


def whole(array):
    return pl.BlockSpec(array.shape, lambda *_: (0,) * array.ndim)


SMEM = pl.BlockSpec(memory_space=pltpu.SMEM)


def project_kernel(
    blocks,
    place,
    point_own,
    point_other,
    chain_own,
    chain_other,
    query_nodes,
    query_angles,
    query_trans,
    query_chain,
    key_angles,
    key_trans,
    key_chain,
    query_weight_own,
    query_weight_other,
    key_weight_own,
    key_weight_other,
    bias_own,
    bias_other,
    edge_key_weight,
    *rest,
):
    key_blocks = rest[:blocks]
    scores, values, bias_spread, query_frames, edge_keys = rest[blocks : blocks + 5]
    keys, key_proj, query_proj, key_side, query_side, query_rows = rest[blocks + 5 :]
    sub, mine = place[0], place[1]
    local_heads = query_weight_own.shape[1] // QCOLS
    query_count, key_count = query_nodes.shape[0], keys.shape[0]
    half = scores.shape[1]
    share = key_blocks[0].shape[0]
    for step in range(blocks):
        source = lax.rem(mine - step + blocks, blocks)
        keys[pl.ds(pl.multiple_of(source * share, share), share), :] = key_blocks[step][...]
    nodes = keys[...]
    key_proj[0] = dot_tt(key_weight_own[...], nodes)
    key_proj[1] = dot_tt(key_weight_other[...], nodes)
    query_proj[0] = dot_tt(query_weight_own[...], query_nodes[...])
    query_proj[1] = dot_tt(query_weight_other[...], query_nodes[...])
    edge_keys[...] = dot_tt(edge_key_weight[...], nodes)

    channels = bias_own.shape[0] // 2
    spread = channels * ROWS
    for at, offset in enumerate((sub * channels, (1 - sub) * channels)):
        select = (iota((2 * channels, spread), 0) == offset + iota((2 * channels, spread), 1) // ROWS)
        select = select.astype(f32).astype(bf16)
        diagonal = iota((1, ROWS, spread), 1) == iota((1, ROWS, spread), 2) % ROWS
        for which, weight in enumerate((bias_own, bias_other)):
            row = dot_tn(weight[...], select)
            block = jnp.where(diagonal, row[:, None, :], 0.0).reshape(local_heads * ROWS, spread)
            begin = which * local_heads * ROWS
            bias_spread[begin : begin + local_heads * ROWS, at * spread : (at + 1) * spread] = block.astype(bf16)

    key_frames = rotation_rows(key_angles[...])
    query_rotation = rotation_rows(query_angles[...])
    frame_rows = [query_rotation[a][b] for a in range(3) for b in range(3)]
    frame_rows += [query_trans[a : a + 1, :] for a in range(3)]
    frame_rows += [query_chain[...].astype(f32)] + [jnp.zeros((1, query_count), f32)] * 3
    query_frames[...] = jnp.concatenate(frame_rows, axis=0).T
    centre = jnp.mean(query_trans[...], axis=1, keepdims=True)

    key_side[...] = jnp.zeros_like(key_side)
    query_side[...] = jnp.zeros_like(query_side)
    key_squares = []
    for head in range(2 * local_heads):
        which, at = divmod(head, local_heads)
        scale = (point_own if which == 0 else point_other)[at] * point_factor
        begin = at * KCOLS
        key_side[head, 0:CH] = rounded(key_proj[which, begin : begin + CH])
        values[head, 0:CH] = key_proj[which, begin + CH : begin + 2 * CH].astype(bf16)
        begin += 2 * CH
        local = [key_proj[which, begin + PQ * b : begin + PQ * (b + 1)] for b in range(3)]
        squares = jnp.zeros((1, key_count), f32)
        for a in range(3):
            moved = sum(key_frames[a][b] * local[b] for b in range(3)) + (
                key_trans[a : a + 1, :] - centre[a : a + 1]
            )
            squares = squares + jnp.sum(moved * moved, axis=0, keepdims=True)
            high = rounded(moved)
            key_side[head, CH + PQ * a : CH + PQ * (a + 1)] = high
            key_side[head, CH + PQ * (3 + a) : CH + PQ * (4 + a)] = moved - high
            key_side[head, CH + PQ * (6 + a) : CH + PQ * (7 + a)] = high
        key_squares.append(squares)
        begin += 3 * PQ
        local = [key_proj[which, begin + PV * b : begin + PV * (b + 1)] for b in range(3)]
        highs, lows = [], []
        for a in range(3):
            moved = sum(key_frames[a][b] * local[b] for b in range(3)) + key_trans[a : a + 1, :]
            highs.append(rounded(moved))
            lows.append(moved - highs[-1])
        values[head, CH : CH + 3 * PV] = jnp.concatenate(highs, axis=0).astype(bf16)
        values[head, CH + 3 * PV : CH + 6 * PV] = jnp.concatenate(lows, axis=0).astype(bf16)
        begin = at * QCOLS
        query_side[head, 0:CH] = rounded(query_proj[which, begin : begin + CH]) * (1.0 / math.sqrt(CH))
        begin += CH
        local = [query_proj[which, begin + PQ * b : begin + PQ * (b + 1)] for b in range(3)]
        squares = jnp.zeros((1, query_count), f32)
        for a in range(3):
            moved = sum(query_rotation[a][b] * local[b] for b in range(3)) + (
                query_trans[a : a + 1, :] - centre[a : a + 1]
            )
            squares = squares + jnp.sum(moved * moved, axis=0, keepdims=True)
            moved = moved * (2.0 * scale)
            high = rounded(moved)
            query_side[head, CH + PQ * a : CH + PQ * (a + 1)] = high
            query_side[head, CH + PQ * (3 + a) : CH + PQ * (4 + a)] = high
            query_side[head, CH + PQ * (6 + a) : CH + PQ * (7 + a)] = moved - high
        query_side[head, SLOT - 1 : SLOT] = squares * (-scale)
    for head in range(2 * local_heads):
        query_rows[head] = query_side[head].T
    begin = pl.multiple_of(sub * half, half)
    chains = query_frames[pl.ds(begin, half), 12:13]
    same = (chains == key_chain[...].astype(f32)).astype(f32)
    for head in range(2 * local_heads):
        which, at = divmod(head, local_heads)
        scale = (point_own if which == 0 else point_other)[at] * point_factor
        chain_gain = (chain_own if which == 0 else chain_other)[at]
        left = query_rows[head, pl.ds(begin, half), :]
        score = dot(left.astype(bf16), key_side[head].astype(bf16))
        score = score + left[:, SLOT - 1 : SLOT] - scale * key_squares[head] + chain_gain * same
        scores[head] = linear_scale * score


def project(
    place, gains, query_side, key_side, query_weights, key_weights, bias_weights, edge_key_weight, key_blocks, half
):
    query_count = query_side[0].shape[0]
    key_count = key_side[0].shape[1]
    local_heads = gains[0].shape[0]
    heads = 2 * local_heads
    channels, hidden = bias_weights[0].shape[0], edge_key_weight.shape[1]
    operands = [*query_side, *key_side, *query_weights, *key_weights, *bias_weights, edge_key_weight, *key_blocks]
    return pl.pallas_call(
        functools.partial(project_kernel, len(key_blocks)),
        in_specs=[SMEM] * 5 + [whole(a) for a in operands],
        out_shape=(
            jax.ShapeDtypeStruct((heads, half, key_count), f32),
            jax.ShapeDtypeStruct((heads, SLOT, key_count), bf16),
            jax.ShapeDtypeStruct((heads * ROWS, channels * ROWS), bf16),
            jax.ShapeDtypeStruct((query_count, 16), f32),
            jax.ShapeDtypeStruct((hidden, key_count), f32),
        ),
        scratch_shapes=[
            pltpu.VMEM((key_count, query_side[0].shape[1]), bf16),
            pltpu.VMEM((2, local_heads * KCOLS, key_count), f32),
            pltpu.VMEM((2, local_heads * QCOLS, query_count), f32),
            pltpu.VMEM((heads, SLOT, key_count), f32),
            pltpu.VMEM((heads, SLOT, query_count), f32),
            pltpu.VMEM((heads, query_count, SLOT), f32),
        ],
        compiler_params=params(32),
        name="project",
    )(place, *gains, *operands)


def attend_kernel(
    place,
    own_pairs,
    other_pairs,
    base_scores,
    mask,
    values,
    bias_spread,
    frames,
    part,
    weight_high,
    weight_low,
    peaks,
    sums,
    gather_own,
    gather_other,
):
    step = pl.program_id(0)
    sub = place[0]
    heads, _, keys = base_scores.shape
    channels = own_pairs.shape[0]
    spread = channels * ROWS
    lanes = 2 * channels

    @pl.when(step == 0)
    def _():
        source = iota((spread, lanes), 0) // ROWS
        target = iota((spread, lanes), 1)
        gather_own[...] = (target == source + sub * channels).astype(f32).astype(bf16)
        gather_other[...] = (target == source + (1 - sub) * channels).astype(f32).astype(bf16)

    own = own_pairs[...].reshape(spread, keys)
    other = other_pairs[...].reshape(spread, keys)
    bias = dot(bias_spread[:, :spread], own) + dot(bias_spread[:, spread:], other)
    score = base_scores[...] + linear_scale * bias.reshape(heads, ROWS, keys)
    score = jnp.where(mask[...][None] == 1, score, masked_score)
    peak = jnp.max(score, axis=2, keepdims=True)
    weight = jnp.exp(score - peak)
    total = jnp.sum(weight, axis=2, keepdims=True)
    high = weight.astype(bf16)
    begin = pl.multiple_of(step * ROWS, ROWS)
    weight_high[:, pl.ds(begin, ROWS), :] = high
    weight_low[:, pl.ds(begin, ROWS), :] = (weight - high.astype(f32)).astype(bf16)
    peaks[:, pl.ds(begin, ROWS), :] = jnp.broadcast_to(peak, (heads, ROWS, lanes))
    sums[:, pl.ds(begin, ROWS), :] = jnp.broadcast_to(total, (heads, ROWS, lanes))
    flat = high.reshape(heads * ROWS, keys)
    scale = (1.0 / total).reshape(heads * ROWS, 1)
    diagonal = iota((heads * ROWS, spread), 0) % ROWS == iota((heads * ROWS, spread), 1) % ROWS
    own_part = jnp.where(diagonal, dot_nt(flat, own) * scale, 0.0).astype(bf16)
    other_part = jnp.where(diagonal, dot_nt(flat, other) * scale, 0.0).astype(bf16)
    pairs = dot(own_part, gather_own[...]) + dot(other_part, gather_other[...])
    part[0:heads, pl.ds(begin, ROWS), :] = pairs.reshape(heads, ROWS, lanes).astype(bf16)

    @pl.when(step == pl.num_programs(0) - 1)
    def _():
        half = frames.shape[0]
        lane = iota((half, 2 * SLOT), 1)
        first = lane < SLOT
        slot = lane % SLOT
        plane = (slot - CH) // PV
        inside = (slot >= CH) & (slot < CH + 3 * PV)

        def on_planes(columns):
            out = jnp.zeros((half, 2 * SLOT), f32)
            for b, column in columns:
                out = jnp.where(inside & (plane == b), frames[:, column : column + 1], out)
            return out

        shift = on_planes([(a, 9 + a) for a in range(3)])
        turns = [
            (d, on_planes([(b, 3 * (b - d) + b) for b in range(3) if 0 <= b - d < 3])) for d in range(-2, 3)
        ]
        for pair in range(heads // 2):
            a, b = 2 * pair, 2 * pair + 1
            left = jnp.concatenate([weight_high[a], weight_low[a], weight_high[b], weight_low[b]], axis=0)
            right = jnp.concatenate([values[a], values[b]], axis=0)
            out = dot_nt(left, right)
            upper = jnp.where(first, out[0:half], out[2 * half : 3 * half])
            lower = jnp.where(first, out[half : 2 * half], out[3 * half :])
            peak_pair = jnp.where(first, peaks[a], peaks[b])
            sum_pair = jnp.where(first, sums[a], sums[b])
            inverse = 1.0 / sum_pair
            points = (upper + lower + pltpu.roll(upper, 2 * SLOT - 3 * PV, 1)) * inverse - shift
            turned = jnp.zeros((half, 2 * SLOT), f32)
            for d, factor in turns:
                turned = turned + factor * (pltpu.roll(points, (d * PV) % (2 * SLOT), 1) if d else points)
            result = jnp.where(slot < CH, upper * inverse, turned)
            at = CH + 3 * PV
            for value in (peak_pair, sum_pair):
                for _ in range(3):
                    piece = rounded(value)
                    result = jnp.where(slot == at, piece, result)
                    value = value - piece
                    at += 1
            part[heads + pair] = jnp.where(slot < at, result, 0.0).astype(bf16)


def attend(place, own_pairs, other_pairs, base_scores, mask, values, bias_spread, frames):
    heads, half, keys = base_scores.shape
    channels = own_pairs.shape[0]
    steps = half // ROWS
    pair_block = pl.BlockSpec((channels, ROWS, keys), lambda g, p: (0, p[0] * steps + g, 0))
    return pl.pallas_call(
        attend_kernel,
        grid_spec=pltpu.PrefetchScalarGridSpec(
            num_scalar_prefetch=1,
            grid=(steps,),
            in_specs=[
                pair_block,
                pair_block,
                pl.BlockSpec((heads, ROWS, keys), lambda g, p: (0, g, 0)),
                pl.BlockSpec((ROWS, keys), lambda g, p: (p[0] * steps + g, 0)),
                whole(values),
                whole(bias_spread),
                pl.BlockSpec((half, frames.shape[1]), lambda g, p: (p[0], 0)),
            ],
            out_specs=pl.BlockSpec((heads + heads // 2, half, 2 * channels), lambda g, p: (0, 0, 0)),
            scratch_shapes=[
                pltpu.VMEM((heads, half, keys), bf16),
                pltpu.VMEM((heads, half, keys), bf16),
                pltpu.VMEM((heads, half, 2 * channels), f32),
                pltpu.VMEM((heads, half, 2 * channels), f32),
                pltpu.VMEM((channels * ROWS, 2 * channels), bf16),
                pltpu.VMEM((channels * ROWS, 2 * channels), bf16),
            ],
        ),
        out_shape=jax.ShapeDtypeStruct((heads + heads // 2, half, 2 * channels), bf16),
        compiler_params=params(40),
        name="attend",
    )(place, own_pairs, other_pairs, base_scores, mask, values, bias_spread, frames)


def norm(values, gain):
    centred = values - jnp.mean(values, axis=-1, keepdims=True)
    variance = jnp.mean(centred * centred, axis=-1, keepdims=True)
    return centred * lax.rsqrt(variance + norm_epsilon) * gain


def node_kernel(
    count,
    nodes,
    out_own,
    out_other,
    first_gain,
    second_gain,
    gate_weight,
    up_weight,
    down_weight,
    *rest,
):
    parts, result = rest[:count], rest[count]
    heads = parts[0].shape[0] * 2 // 3
    rows, lanes = parts[0].shape[1:]
    local_heads = heads // 2
    tall = local_heads * rows
    first = iota((tall, lanes), 1) < SLOT
    slot = iota((tall, lanes), 1) % SLOT
    at = CH + 3 * PV

    def broadcast(values, lane):
        return jnp.where(
            first,
            jnp.broadcast_to(values[:, lane : lane + 1], (tall, lanes)),
            jnp.broadcast_to(values[:, SLOT + lane : SLOT + lane + 1], (tall, lanes)),
        )

    extras, peaks, sums = [], [], []
    for part in parts:
        extra = part[heads:].astype(f32).reshape(tall, lanes)
        joined = extra + pltpu.roll(extra, lanes - 1, 1) + pltpu.roll(extra, lanes - 2, 1)
        extras.append(extra)
        peaks.append(broadcast(joined, at))
        sums.append(broadcast(joined, at + 3))
    peak = functools.reduce(jnp.maximum, peaks)
    shares = [s * jnp.exp(p - peak) for s, p in zip(sums, peaks)]
    total = sum(shares)
    shares = [s / total for s in shares]
    merged = sum(s * e for s, e in zip(shares, extras))
    squares = merged * merged
    norms = jnp.sqrt(
        1.0 + pltpu.roll(squares, PV, 1) + pltpu.roll(squares, 2 * PV, 1) + pltpu.roll(squares, 3 * PV, 1)
    )
    merged = jnp.where(slot < at, merged, norms).astype(bf16)
    projected = jnp.zeros((rows, nodes.shape[1]), f32)
    for head in range(heads):
        pair, odd = divmod(head, 2)
        weight = out_own if head < local_heads else out_other
        begin = (head % local_heads) * (FEATURES + lanes)
        span = slice(pair * rows, (pair + 1) * rows)
        lane = odd * SLOT
        mixed = jnp.zeros((rows, lanes), f32)
        for share, part in zip(shares, parts):
            factor = jnp.broadcast_to(share[span, lane : lane + 1], (rows, lanes))
            mixed = mixed + factor * part[head].astype(f32)
        projected = projected + dot(mixed.astype(bf16), weight[begin + FEATURES : begin + FEATURES + lanes])
        projected = projected + dot(merged[span, lane : lane + FEATURES], weight[begin : begin + FEATURES])
    first_nodes = norm(nodes[...].astype(f32) + projected, first_gain[...])
    first_rounded = first_nodes.astype(bf16)
    gate = dot(first_rounded, gate_weight[...])
    hidden = (gate / (1.0 + jnp.exp(-gate)) * dot(first_rounded, up_weight[...])).astype(bf16)
    result[...] = norm(first_nodes + dot(hidden, down_weight[...]), second_gain[...]).astype(bf16)


def update_nodes(parts, nodes, out_own, out_other, first_gain, second_gain, gate_weight, up_weight, down_weight):
    operands = [nodes, out_own, out_other, first_gain, second_gain, gate_weight, up_weight, down_weight, *parts]
    return pl.pallas_call(
        functools.partial(node_kernel, len(parts)),
        in_specs=[whole(a) for a in operands],
        out_shape=jax.ShapeDtypeStruct(nodes.shape, bf16),
        compiler_params=params(32),
        name="nodes",
    )(*operands)


def edge_kernel(
    place,
    own_pairs,
    other_pairs,
    nodes,
    edge_keys,
    in_weight,
    out_weight,
    query_weight,
    result,
    new_nodes,
    left,
    out_left,
    turned,
    hidden,
    fresh,
):
    channels, rows, keys = own_pairs.shape
    both = 2 * channels
    sub = place[0]

    @pl.when(pl.program_id(0) == 0)
    def _():
        own = pl.multiple_of(sub * channels, channels)
        other = pl.multiple_of((1 - sub) * channels, channels)
        left[:, 0:channels] = in_weight[pl.ds(own, channels), :].astype(f32).T.astype(bf16)
        left[:, channels:both] = in_weight[pl.ds(other, channels), :].astype(f32).T.astype(bf16)
        flipped = out_weight[...].astype(f32).T
        out_left[...] = jnp.where(sub == 0, flipped[0:channels], flipped[channels:]).astype(bf16)
        picks = iota((rows, 2 * rows, keys), 1) % rows == iota((rows, 2 * rows, keys), 0)
        turned[:, both:, :] = picks.astype(f32).astype(bf16)

    new_nodes[...] = nodes[0, 0]
    queries = dot_tt(query_weight[...], nodes[0, 0])
    high = queries.astype(bf16)
    left[:, both : both + rows] = high
    left[:, both + rows :] = (queries - high.astype(f32)).astype(bf16)
    turned[:, 0:channels, :] = jnp.swapaxes(own_pairs[...], 0, 1)
    turned[:, channels:both, :] = jnp.swapaxes(other_pairs[...], 0, 1)
    for row in range(rows):
        hidden[row] = jnp.maximum(dot(left[...], turned[row]) + edge_keys[...], 0.0).astype(bf16)
    for row in range(rows):
        out = dot(out_left[...], hidden[row])
        for at in range(keys // 128):
            fresh[at, pl.ds(row, channels, stride=rows), :] = out[:, at * 128 : (at + 1) * 128]
    for at in range(keys // 128):
        span = slice(at * 128, (at + 1) * 128)
        old = own_pairs[:, :, span].reshape(channels * rows, 128).astype(f32)
        result[:, :, span] = (old + fresh[at]).astype(bf16).reshape(channels, rows, 128)


def update_pairs(place, own_pairs, other_pairs, nodes, edge_keys, in_weight, out_weight, query_weight):
    channels, count, keys = own_pairs.shape
    hidden = in_weight.shape[1]
    features = nodes.shape[-1]
    steps = nodes.shape[1]
    pair_block = pl.BlockSpec((channels, ROWS, keys), lambda g, p: (0, g, 0))

    def node_block(g, p):
        return (lax.rem(g // steps + p[0], 2), lax.rem(lax.rem(g, steps) + p[1], steps), 0, 0)

    return pl.pallas_call(
        edge_kernel,
        grid_spec=pltpu.PrefetchScalarGridSpec(
            num_scalar_prefetch=1,
            grid=(count // ROWS,),
            in_specs=[
                pair_block,
                pair_block,
                pl.BlockSpec((1, 1, ROWS, features), node_block),
                whole(edge_keys),
                whole(in_weight),
                whole(out_weight),
                whole(query_weight),
            ],
            out_specs=(pair_block, pl.BlockSpec((ROWS, features), lambda g, p: (g, 0))),
            scratch_shapes=[
                pltpu.VMEM((hidden, 2 * channels + 2 * ROWS), bf16),
                pltpu.VMEM((channels, hidden), bf16),
                pltpu.VMEM((ROWS, 2 * channels + 2 * ROWS, keys), bf16),
                pltpu.VMEM((ROWS, hidden, keys), bf16),
                pltpu.VMEM((keys // 128, channels * ROWS, 128), f32),
            ],
        ),
        out_shape=(
            jax.ShapeDtypeStruct(own_pairs.shape, bf16),
            jax.ShapeDtypeStruct((count, features), bf16),
        ),
        compiler_params=params(40),
        name="edges",
    )(place, own_pairs, other_pairs, nodes, edge_keys, in_weight, out_weight, query_weight)


def shards(
    node_query,
    query_angles,
    query_trans,
    query_chain,
    node_key,
    key_angles,
    key_trans,
    key_chain,
    pair_features,
    pair_mask,
    query_weight,
    key_weight,
    bias_weight,
    point_gain,
    chain_gain,
    out_weight,
    first_gain,
    second_gain,
    gate_weight,
    up_weight,
    down_weight,
    edge_query_weight,
    edge_key_weight,
    edge_in_weight,
    edge_out_weight,
):
    subs, cols, rows = lax.axis_size("sub"), lax.axis_size("col"), lax.axis_size("row")
    sub, col = lax.axis_index("sub"), lax.axis_index("col")

    def swap(values):
        return lax.ppermute(values, "sub", [(i, (i + 1) % subs) for i in range(subs)])

    group = rows * subs
    mine = lax.axis_index(("row", "sub"))
    key_blocks = [node_key] + [
        lax.ppermute(node_key, ("row", "sub"), [(i, (i + k) % group) for i in range(group)])
        for k in range(1, group)
    ]
    other_query, other_key, other_bias = swap(query_weight), swap(key_weight), swap(bias_weight)
    other_point, other_chain = swap(point_gain), swap(chain_gain)
    other_pairs = swap(pair_features)
    other_out = swap(out_weight)

    query_count = node_query.shape[0]
    half = query_count // subs
    share = half // cols
    place = jnp.stack([sub, mine]).astype(jnp.int32)
    base_scores, values, bias_spread, frames, edge_keys = project(
        place,
        [point_gain, other_point, chain_gain, other_chain],
        [node_query, query_angles, query_trans, query_chain[None, :]],
        [key_angles, key_trans, key_chain[None, :]],
        [query_weight, other_query],
        [key_weight, other_key],
        [bias_weight, other_bias],
        edge_key_weight,
        key_blocks,
        half,
    )
    part = attend(place, pair_features, other_pairs, base_scores, pair_mask, values, bias_spread, frames)

    def piece(k):
        return lax.dynamic_slice_in_dim(part, lax.rem(col + k, cols) * share, share, 1)

    parts = [piece(0)] + [
        lax.ppermute(piece(k), "col", [(i, (i + k) % cols) for i in range(cols)]) for k in range(1, cols)
    ]
    spare = -share % ROWS
    own_nodes = lax.dynamic_slice_in_dim(node_query, sub * half + col * share, share, 0)
    if spare:
        parts = [jnp.pad(p, ((0, 0), (0, spare), (0, 0))) for p in parts]
        own_nodes = jnp.pad(own_nodes, ((0, spare), (0, 0)))
    fresh_nodes = update_nodes(
        parts,
        own_nodes,
        out_weight,
        other_out,
        first_gain[None, :],
        second_gain[None, :],
        gate_weight,
        up_weight,
        down_weight,
    )[:share]
    ring = [fresh_nodes] + [
        lax.ppermute(fresh_nodes, "col", [(i, (i - k) % cols) for i in range(cols)]) for k in range(1, cols)
    ]
    half_nodes = jnp.concatenate(ring, axis=0)
    if spare:
        half_nodes = jnp.roll(half_nodes, col * share, axis=0)
        turn = 0 * col
    else:
        turn = lax.rem(cols - col, cols) * (share // ROWS)
    both_nodes = jnp.stack([half_nodes, swap(half_nodes)])
    both_nodes = both_nodes.reshape(subs, half // ROWS, ROWS, node_query.shape[1])
    updated_pairs, updated_nodes = update_pairs(
        jnp.stack([sub, turn]).astype(jnp.int32),
        pair_features,
        other_pairs,
        both_nodes,
        edge_keys,
        edge_in_weight,
        edge_out_weight,
        edge_query_weight,
    )
    return (updated_nodes, updated_pairs)


def solution(mesh):
    return jax.shard_map(
        shards,
        mesh=mesh,
        in_specs=(
            P(("rep", "row"), None),
            P(None, ("rep", "row")),
            P(None, ("rep", "row")),
            P(("rep", "row")),
            P(("rep", "col", "row", "sub"), None),
            P(None, ("rep", "col")),
            P(None, ("rep", "col")),
            P(("rep", "col")),
            P("sub", ("rep", "row"), "col"),
            P(("rep", "row"), "col"),
            P(None, "sub"),
            P(None, "sub"),
            P(None, "sub"),
            P("sub"),
            P("sub"),
            P("sub", None),
            P(),
            P(),
            P(),
            P(),
            P(),
            P(),
            P(),
            P(),
            P(),
        ),
        out_specs=(P(("rep", "row"), None), P("sub", ("rep", "row"), "col")),
        check_vma=False,
    )
```

time: 186 us -> 79.1 us (0.43)
  matrix products: 59.1 us -> 0 us
  blocking collectives: 35.4 us -> 0 us
  Pallas kernels: 0 us -> 28.3 us
  waiting for transfers between devices: 36.4 us -> 17.2 us
  local copies, waits for them, and re-layouts: 35.9 us -> 16.8 us
  starting transfers between devices: 0.12 us -> 15.1 us
  between operations: 14.5 us -> 0.85 us
  other arithmetic: 4.1 us -> 0.16 us
    dot_general x21 -> x0, matrix products: 59.1 us -> none  [the longest x5 26.7 us: leading_product(): lax.dot_general(left, right, (((0,), (0,)), ((), ())), preferred_element_...]
    pallas_call x0 -> x4, Pallas kernels: none -> 28.3 us  [the longest x1 16.1 us: update_pairs(): pl.pallas_call(edge_kernel, grid_spec=pltpu.PrefetchScalarGridSpec(num_sc...]
    reduce_scatter x1 -> x0, waiting for transfers between devices: 27.6 us -> none  [node_section(): lax.psum_scatter(sums, 'col', scatter_dimension=0, tiled=True)]
    all_gather x2 -> x0, blocking collectives: 19.6 us -> none  [the longest x1 13.1 us: node_section(): return lax.all_gather(node_share, 'col', axis=0, tiled=True)]
    ppermute x0 -> x17, waiting for transfers between devices: none -> 17.2 us  [the longest x3 6.58 us: shards(): lax.ppermute(piece(k), 'col', [(i, (i + k) % cols) for i in range(cols)])]
    ppermute x0 -> x17, starting transfers between devices: none -> 15.1 us  [the longest x3 4.74 us: shards(): lax.ppermute(fresh_nodes, 'col', [(i, (i - k) % cols) for i in range(cols)])]
    pmax x1 -> x0, blocking collectives: 12.4 us -> none  [attend(): row_max = lax.pmax(jnp.max(scores, axis=2), 'col')]
    unnamed x4 -> x0, waiting for transfers between devices: 8.82 us -> none
  transfers between devices with their start and end apart: 3 -> 17, of which waited for: 2 -> 11; matrix products, arithmetic and copies ran while one was open for 25% -> 5% of each run, Pallas kernels for 0% -> 13%
where the time goes in v1:
time: 79.1 us; the launch traced here: 78.4 us
  Pallas kernels  28.3 us (36%)
  waiting for transfers between devices  17.2 us (22%)
  local copies, waits for them, and re-layouts  16.8 us (21%)
  starting transfers between devices  15.1 us (19%)
  between operations  0.85 us (1%)
    pallas_call x1, Pallas kernels, update_pairs(): pl.pallas_call(edge_kernel, grid_spec=pltpu.PrefetchScalarGridSpec(num_sc...  16.1 us
    unnamed x49, local copies, waits for them, and re-layouts  16.1 us
    pallas_call x1, Pallas kernels, attend(): pl.pallas_call(attend_kernel, grid_spec=pltpu.PrefetchScalarGridSpec(num_...  8.38 us
    ppermute x3, waiting for transfers between devices, shards(): lax.ppermute(piece(k), 'col', [(i, (i + k) % cols) for i in range(cols)])  6.58 us
    ppermute x8, waiting for transfers between devices, swap(): lax.ppermute(values, 'sub', [(i, (i + 1) % subs) for i in range(subs)])  6.33 us
    ppermute x3, starting transfers between devices, shards(): lax.ppermute(fresh_nodes, 'col', [(i, (i - k) % cols) for i in range(cols)])  4.74 us
    ppermute x3, starting transfers between devices, shards(): lax.ppermute(piece(k), 'col', [(i, (i + k) % cols) for i in range(cols)])  4.67 us
    ppermute x3, starting transfers between devices, shards(): lax.ppermute(node_key, ('row', 'sub'), [(i, (i + k) % group) for i in ran...  3.93 us
  transfers between devices with their start and end apart: 17, of which 11 were waited for; matrix products, arithmetic and copies ran while one was open for 5% of the time, Pallas kernels for 13%

profile of v1, /device:TPU:0, one launch (start us, length us, event | category | flops | bytes accessed | tf_op | source)
XLA Modules:
  0.0 78.4 jit_solution(6094807535296361170)
XLA Ops:
  0.6 0.5 collective-permute-start
  1.1 0.1 collective-permute-start.1
  1.2 1.1 %copy.31.key_weight_own = bf16[256,408]{1,0:T(8,128)(2,1)S(1)} copy(bf16[256,408]{0,1:T(8,128)(2,1)} %param.36) | data formatting | bytes 417792 | tf_op args[11]
  2.3 0.5 collective-permute-start.5
  2.8 0.8 %copy.32.bias_own = bf16[128,6]{1,0:T(8,128)(2,1)S(1)} copy(bf16[128,6]{0,1:T(8,128)(2,1)} %param.37) | data formatting | bytes 3072 | tf_op args[12]
  3.6 0.1 collective-permute-start.6
  3.7 0.4 collective-permute-start.2
  4.2 4.0 %collective-permute-done.2.point_other = f32[6]{0:T(128)S(1)} collective-permute-done((f32[6]{0:T(128)}, f32[6]{0:T(128)S(1)}, u32[]{:S(2)}, u32[]{:S(2)}) %collective-permute-start.2) | collective-permute-done | bytes 56 | tf_op jit(solution)/shard_map/ppermute | solution.py:568
  8.1 0.1 collective-permute-start.3
  8.3 1.1 %collective-permute-done.3.chain_other = f32[6]{0:T(128)S(1)} collective-permute-done((f32[6]{0:T(128)}, f32[6]{0:T(128)S(1)}, u32[]{:S(2)}, u32[]{:S(2)}) %collective-permute-start.3) | collective-permute-done | bytes 56 | tf_op jit(solution)/shard_map/ppermute | solution.py:568
  9.4 3.1 %collective-permute-start.8 = (bf16[64,256]{1,0:T(8,128)(2,1)}, bf16[64,256]{1,0:T(8,128)(2,1)S(1)}, u32[]{:S(2)}, u32[]{:S(2)}) collective-permute-start(bf16[64,256]{1,0:T(8,128)(2,1)} %rest_0_.1), channel_id=1, source_target_pairs={{0,2},{1,3},{2,0},{3,1},{4,6},{5,7},{6,4},{7,5},{8,10},{9,11},{10,... | collective-permute-start | bytes 98312 | tf_op jit(solution)/shard_map/ppermute | solution.py:573
  12.6 1.0 %copy.30.query_weight_own = bf16[256,168]{1,0:T(8,128)(2,1)S(1)} copy(bf16[256,168]{0,1:T(8,128)(2,1)} %param.35) | data formatting | bytes 172032 | tf_op args[10]
  13.6 1.1 %collective-permute-done.8.rest_2_ = bf16[64,256]{1,0:T(8,128)(2,1)S(1)} collective-permute-done((bf16[64,256]{1,0:T(8,128)(2,1)}, bf16[64,256]{1,0:T(8,128)(2,1)S(1)}, u32[]{:S(2)}, u32[]{:S(2)}) %collective-permute-start.8) | collective-permute-done | bytes 32800 | tf_op jit(solution)/shard_map/ppermute | solution.py:573
  14.6 0.8 collective-permute-start.9
  15.4 0.7 collective-permute-done.7.rest_1_
  16.1 0.1 pad_add_fusion.1.place
  16.2 1.2 %collective-permute-done.9.rest_3_ = bf16[64,256]{1,0:T(8,128)(2,1)S(1)} collective-permute-done((bf16[64,256]{1,0:T(8,128)(2,1)}, bf16[64,256]{1,0:T(8,128)(2,1)S(1)}, u32[]{:S(2)}, u32[]{:S(2)}) %collective-permute-start.9) | collective-permute-done | bytes 32800 | tf_op jit(solution)/shard_map/ppermute | solution.py:573
  17.3 0.1 collective-permute-done.4.query_weight_other
  17.4 0.9 %copy-done.8 = bf16[256,256]{1,0:T(8,128)(2,1)S(1)} copy-done((bf16[256,256]{1,0:T(8,128)(2,1)S(1)}, bf16[256,256]{1,0:T(8,128)(2,1)}, u32[]{:S(2)}) %copy-start.8) | copy-done | bytes 131096
  18.3 0.8 %copy-done.9 = bf16[128,256]{1,0:T(8,128)(2,1)S(1)} copy-done((bf16[128,256]{1,0:T(8,128)(2,1)S(1)}, bf16[128,256]{1,0:T(8,128)(2,1)}, u32[]{:S(2)}) %copy-start.9) | copy-done | bytes 65560
  19.2 0.8 copy-done.12
  19.9 0.7 copy-done.13
  20.6 0.7 copy-done.14
  21.3 0.7 copy-done.15
  22.0 0.7 copy-done.16
  22.7 0.7 copy-done.19
  23.4 0.7 copy-done.20
  24.0 0.7 copy-done.21
  24.7 0.7 copy-done.22
  25.3 2.1 %project.1 = (f32[12,64,256]{2,1,0:T(8,128)S(1)}, bf16[12,64,256]{2,1,0:T(8,128)(2,1)S(1)}, bf16[192,2048]{1,0:T(8,128)(2,1)S(1)}, f32[128,16]{1,0:T(8,128)S(1)}, f32[256,256]{1,0:T(8,128)S(1)}) custom-call(s32[2]{0:T(128)S(1)} %pad_add_fusion.1.place, f32[6]{0:T(128)S(1)} %copy-done.20, f32[6]{0:T(128)S(1)} %collective-permute-done.2.point_other, ...), custom_call_target="tpu_custom_call" | custom-call | tf_op jit(solution)/shard_map/project/pallas_call | solution.py:207
  27.4 2.2 %copy-done = bf16[64,128,256]{2,1,0:T(8,128)(2,1)S(1)} copy-done((bf16[64,128,256]{2,1,0:T(8,128)(2,1)S(1)}, bf16[64,128,256]{2,1,0:T(8,128)(2,1)}, u32[]{:S(2)}) %copy-start) | copy-done | bytes 4194328
  29.6 0.9 %copy-done.6 = s32[128,256]{1,0:T(8,128)S(1)} copy-done((s32[128,256]{1,0:T(8,128)S(1)}, s32[128,256]{1,0:T(8,128)}, u32[]{:S(2)}) %copy-start.6) | copy-done | bytes 131096
  30.6 8.4 %attend.1 = bf16[18,64,128]{2,1,0:T(8,128)(2,1)S(1)} custom-call(s32[2]{0:T(128)S(1)} %pad_add_fusion.1.place, bf16[64,128,256]{2,1,0:T(8,128)(2,1)S(1)} %copy-done, bf16[64,128,256]{2,1,0:T(8,128)(2,1)} %collective-permute-done.other_pairs, f32[12,64,256]{2,1,0:T(8,128)S(1)} %get-tuple-element.9.base_scores, s32[128,256]{1,0:T(8,128)S(1)} %copy-done.6, ...), custom_call_target="tpu_custom_call" | custom-call | tf_op jit(solution)/shard_map/attend/pallas_call | solution.py:332
  39.0 0.1 constant_dynamic-slice_fusion
  39.0 3.7 %collective-permute-start.12 = (bf16[18,16,128]{2,1,0:T(8,128)(2,1)S(1)}, bf16[18,16,128]{2,1,0:T(8,128)(2,1)S(1)}, u32[]{:S(2)}, u32[]{:S(2)}) collective-permute-start(bf16[18,16,128]{2,1,0:T(8,128)(2,1)S(1)} %get-tuple-element.16), channel_id=1, source_target_pairs={{0,12},{4,0},{8,4},{12,8},{1,13},{5,1},{9,5},{13,9},{2,14},{6,2},{... | collective-permute-start | bytes 221192 | tf_op jit(solution)/shard_map/ppermute | solution.py:603
  42.7 1.0 %collective-permute-start.10 = (bf16[18,16,128]{2,1,0:T(8,128)(2,1)S(1)}, bf16[18,16,128]{2,1,0:T(8,128)(2,1)S(1)}, u32[]{:S(2)}, u32[]{:S(2)}) collective-permute-start(bf16[18,16,128]{2,1,0:T(8,128)(2,1)S(1)} %get-tuple-element.18), channel_id=1, source_target_pairs={{0,4},{4,8},{8,12},{12,0},{1,5},{5,9},{9,13},{13,1},{2,6},{6,10},{... | collective-permute-start | bytes 221192 | tf_op jit(solution)/shard_map/ppermute | solution.py:603
  43.7 0.7 constant_dynamic-slice_fusion.4.nodes
  44.4 0.6 collective-permute-done.12.rest_3_
  45.0 6.0 %collective-permute-done.11.rest_2_ = bf16[18,16,128]{2,1,0:T(8,128)(2,1)S(1)} collective-permute-done((bf16[18,16,128]{2,1,0:T(8,128)(2,1)S(1)}, bf16[18,16,128]{2,1,0:T(8,128)(2,1)S(1)}, u32[]{:S(2)}, u32[]{:S(2)}) %collective-permute-start.11) | collective-permute-done | bytes 73760 | tf_op jit(solution)/shard_map/ppermute | solution.py:603
  51.0 1.8 %nodes.1 = bf16[16,256]{1,0:T(8,128)(2,1)S(1)} custom-call(bf16[16,256]{1,0:T(8,128)(2,1)S(1)} %constant_dynamic-slice_fusion.4.nodes, bf16[1056,256]{1,0:T(8,128)(2,1)S(1)} %copy-done.2, bf16[1056,256]{1,0:T(8,128)(2,1)S(1)} %collective-permute-done.1.out_other, f32[1,256]{1,0:T(1,128)S(1)} %bitcast.9, f32[1,256]{1,0:T(1,128)S(1)} %bitcast.10, ...), custom_call_target="tpu_custom_call" | custom-call | tf_op jit(solution)/shard_map/nodes/pallas_call | solution.py:435
  52.8 1.9 %collective-permute-start.14 = (bf16[16,256]{1,0:T(8,128)(2,1)S(1)}, bf16[16,256]{1,0:T(8,128)(2,1)S(1)}, u32[]{:S(2)}, u32[]{:S(2)}) collective-permute-start(bf16[16,256]{1,0:T(8,128)(2,1)S(1)} %nodes.1), channel_id=1, source_target_pairs={{0,8},{4,12},{8,0},{12,4},{1,9},{5,13},{9,1},{13,5},{2,10},{6,14},... | collective-permute-start | bytes 24584 | tf_op jit(solution)/shard_map/ppermute | solution.py:622
  54.7 2.9 %collective-permute-start.13 = (bf16[16,256]{1,0:T(8,128)(2,1)S(1)}, bf16[16,256]{1,0:T(8,128)(2,1)S(1)}, u32[]{:S(2)}, u32[]{:S(2)}) collective-permute-start(bf16[16,256]{1,0:T(8,128)(2,1)S(1)} %nodes.1), channel_id=1, source_target_pairs={{0,12},{4,0},{8,4},{12,8},{1,13},{5,1},{9,5},{13,9},{2,14},{6,2},{... | collective-permute-start | bytes 24584 | tf_op jit(solution)/shard_map/ppermute | solution.py:622
  57.6 0.7 collective-permute-done.15
  58.3 0.6 collective-permute-done.13
  58.9 0.1 pad_add_fusion.place
  59.0 1.1 %collective-permute-done.16 = bf16[64,256]{1,0:T(8,128)(2,1)S(1)} collective-permute-done((bf16[64,256]{1,0:T(8,128)(2,1)S(1)}, bf16[64,256]{1,0:T(8,128)(2,1)S(1)}, u32[]{:S(2)}, u32[]{:S(2)}) %collective-permute-start.16) | collective-permute-done | bytes 32800 | tf_op jit(solution)/shard_map/ppermute | solution.py:568
  60.2 2.2 %copy-done.1 = bf16[64,128,256]{2,1,0:T(8,128)(2,1)S(1)} copy-done((bf16[64,128,256]{2,1,0:T(8,128)(2,1)S(1)}, bf16[64,128,256]{2,1,0:T(8,128)(2,1)}, u32[]{:S(2)}) %copy-start.1) | copy-done | bytes 4194328
  62.4 16.1 %edges.1 = (bf16[64,128,256]{2,1,0:T(8,128)(2,1)}, bf16[128,256]{1,0:T(8,128)(2,1)}) custom-call(s32[2]{0:T(128)S(1)} %pad_add_fusion.place, bf16[64,128,256]{2,1,0:T(8,128)(2,1)S(1)} %copy-done.1, bf16[64,128,256]{2,1,0:T(8,128)(2,1)} %collective-permute-done.other_pairs, bf16[2,4,16,256]{3,2,1,0:T(8,128)(2,1)S(1)} %pad_maximum_fusion.nodes, ...), custom_call_target="tpu_custom_call" | custom-call | tf_op jit(solution)/shard_map/edges/pallas_call | solution.py:505
  (45 shorter events, 0.1 us)
Async XLA Ops:
  0.6 26.8 %collective-permute-start = (bf16[64,128,256]{2,1,0:T(8,128)(2,1)}, bf16[64,128,256]{2,1,0:T(8,128)(2,1)}, u32[]{:S(2)}, u32[]{:S(2)}) collective-permute-start(bf16[64,128,256]{2,1,0:T(8,128)(2,1)} %own_pairs.3), channel_id=1, source_target_pairs={{0,1},{1,0},{2,3},{3,2},{4,5},{5,4},{6,7},{7,6},{8,9},{9,8},{10,11... | collective-permute-start | bytes 12582920 | tf_op jit(solution)/shard_map/ppermute | solution.py:568
  1.1 43.3 %collective-permute-start.1 = (bf16[1056,256]{1,0:T(8,128)(2,1)}, bf16[1056,256]{1,0:T(8,128)(2,1)S(1)}, u32[]{:S(2)}, u32[]{:S(2)}) collective-permute-start(bf16[1056,256]{1,0:T(8,128)(2,1)} %out_own.1), channel_id=1, source_target_pairs={{0,1},{1,0},{2,3},{3,2},{4,5},{5,4},{6,7},{7,6},{8,9},{9,8},{10,11... | collective-permute-start | bytes 1622024 | tf_op jit(solution)/shard_map/ppermute | solution.py:568
  2.3 15.1 %collective-permute-start.5 = (bf16[256,408]{1,0:T(8,128)(2,1)S(1)}, bf16[256,408]{1,0:T(8,128)(2,1)S(1)}, u32[]{:S(2)}, u32[]{:S(2)}) collective-permute-start(bf16[256,408]{1,0:T(8,128)(2,1)S(1)} %copy.31.key_weight_own), channel_id=1, source_target_pairs={{0,1},{1,0},{2,3},{3,2},{4,5},{5,4},{6,7},{7,6},{8,9},{9,8},{10,11... | collective-permute-start | bytes 626696 | tf_op jit(solution)/shard_map/ppermute | solution.py:568
  3.6 8.9 %collective-permute-start.6 = (bf16[128,6]{1,0:T(8,128)(2,1)S(1)}, bf16[128,6]{1,0:T(8,128)(2,1)S(1)}, u32[]{:S(2)}, u32[]{:S(2)}) collective-permute-start(bf16[128,6]{1,0:T(8,128)(2,1)S(1)} %copy.32.bias_own), channel_id=1, source_target_pairs={{0,1},{1,0},{2,3},{3,2},{4,5},{5,4},{6,7},{7,6},{8,9},{9,8},{10,11... | collective-permute-start | bytes 4616 | tf_op jit(solution)/shard_map/ppermute | solution.py:568
  3.7 4.4 %collective-permute-start.2 = (f32[6]{0:T(128)}, f32[6]{0:T(128)S(1)}, u32[]{:S(2)}, u32[]{:S(2)}) collective-permute-start(f32[6]{0:T(128)} %point_own.1), channel_id=1, source_target_pairs={{0,1},{1,0},{2,3},{3,2},{4,5},{5,4},{6,7},{7,6},{8,9},{9,8},{10,11... | collective-permute-start | bytes 80 | tf_op jit(solution)/shard_map/ppermute | solution.py:568
  8.1 1.3 %collective-permute-start.3 = (f32[6]{0:T(128)}, f32[6]{0:T(128)S(1)}, u32[]{:S(2)}, u32[]{:S(2)}) collective-permute-start(f32[6]{0:T(128)} %chain_own.1), channel_id=1, source_target_pairs={{0,1},{1,0},{2,3},{3,2},{4,5},{5,4},{6,7},{7,6},{8,9},{9,8},{10,11... | collective-permute-start | bytes 80 | tf_op jit(solution)/shard_map/ppermute | solution.py:568
  9.4 5.2 %collective-permute-start.8 = (bf16[64,256]{1,0:T(8,128)(2,1)}, bf16[64,256]{1,0:T(8,128)(2,1)S(1)}, u32[]{:S(2)}, u32[]{:S(2)}) collective-permute-start(bf16[64,256]{1,0:T(8,128)(2,1)} %rest_0_.1), channel_id=1, source_target_pairs={{0,2},{1,3},{2,0},{3,1},{4,6},{5,7},{6,4},{7,5},{8,10},{9,11},{10,... | collective-permute-start | bytes 98312 | tf_op jit(solution)/shard_map/ppermute | solution.py:573
  12.5 3.6 %collective-permute-start.7 = (bf16[64,256]{1,0:T(8,128)(2,1)}, bf16[64,256]{1,0:T(8,128)(2,1)S(1)}, u32[]{:S(2)}, u32[]{:S(2)}) collective-permute-start(bf16[64,256]{1,0:T(8,128)(2,1)} %rest_0_.1), channel_id=1, source_target_pairs={{0,1},{1,2},{2,3},{3,0},{4,5},{5,6},{6,7},{7,4},{8,9},{9,10},{10,1... | collective-permute-start | bytes 98312 | tf_op jit(solution)/shard_map/ppermute | solution.py:573
  14.6 2.7 %collective-permute-start.9 = (bf16[64,256]{1,0:T(8,128)(2,1)}, bf16[64,256]{1,0:T(8,128)(2,1)S(1)}, u32[]{:S(2)}, u32[]{:S(2)}) collective-permute-start(bf16[64,256]{1,0:T(8,128)(2,1)} %rest_0_.1), channel_id=1, source_target_pairs={{0,3},{1,0},{2,1},{3,2},{4,7},{5,4},{6,5},{7,6},{8,11},{9,8},{10,9... | collective-permute-start | bytes 98312 | tf_op jit(solution)/shard_map/ppermute | solution.py:573
  16.1 1.3 %collective-permute-start.4 = (bf16[256,168]{1,0:T(8,128)(2,1)S(1)}, bf16[256,168]{1,0:T(8,128)(2,1)S(1)}, u32[]{:S(2)}, u32[]{:S(2)}) collective-permute-start(bf16[256,168]{1,0:T(8,128)(2,1)S(1)} %copy.30.query_weight_own), channel_id=1, source_target_pairs={{0,1},{1,0},{2,3},{3,2},{4,5},{5,4},{6,7},{7,6},{8,9},{9,8},{10,11... | collective-permute-start | bytes 258056 | tf_op jit(solution)/shard_map/ppermute | solution.py:568
  17.4 0.9 %copy-start.8 = (bf16[256,256]{1,0:T(8,128)(2,1)S(1)}, bf16[256,256]{1,0:T(8,128)(2,1)}, u32[]{:S(2)}) copy-start(bf16[256,256]{1,0:T(8,128)(2,1)} %edge_key_weight.1) | copy-start | bytes 393220
  18.3 0.8 %copy-start.9 = (bf16[128,256]{1,0:T(8,128)(2,1)S(1)}, bf16[128,256]{1,0:T(8,128)(2,1)}, u32[]{:S(2)}) copy-start(bf16[128,256]{1,0:T(8,128)(2,1)} %query_nodes.1) | copy-start | bytes 196612
  19.2 0.8 copy-start.12
  19.9 0.7 copy-start.13
  20.6 0.7 copy-start.14
  21.3 0.7 copy-start.15
  22.0 0.7 copy-start.16
  22.7 0.7 copy-start.19
  23.4 0.7 copy-start.20
  24.0 0.7 copy-start.21
  24.7 0.7 copy-start.22
  27.4 2.2 %copy-start = (bf16[64,128,256]{2,1,0:T(8,128)(2,1)S(1)}, bf16[64,128,256]{2,1,0:T(8,128)(2,1)}, u32[]{:S(2)}) copy-start(bf16[64,128,256]{2,1,0:T(8,128)(2,1)} %own_pairs.3) | copy-start | bytes 12582916
  29.6 0.9 %copy-start.6 = (s32[128,256]{1,0:T(8,128)S(1)}, s32[128,256]{1,0:T(8,128)}, u32[]{:S(2)}) copy-start(s32[128,256]{1,0:T(8,128)} %mask.1) | copy-start | bytes 393220
  30.5 20.5 %copy-start.2 = (bf16[1056,256]{1,0:T(8,128)(2,1)S(1)}, bf16[1056,256]{1,0:T(8,128)(2,1)}, u32[]{:S(2)}) copy-start(bf16[1056,256]{1,0:T(8,128)(2,1)} %out_own.1) | copy-start | bytes 1622020
  30.5 20.5 %copy-start.3 = (bf16[256,1024]{1,0:T(8,128)(2,1)S(1)}, bf16[256,1024]{1,0:T(8,128)(2,1)}, u32[]{:S(2)}) copy-start(bf16[256,1024]{1,0:T(8,128)(2,1)} %gate_weight.1) | copy-start | bytes 1572868
  30.5 20.5 %copy-start.4 = (bf16[256,1024]{1,0:T(8,128)(2,1)S(1)}, bf16[256,1024]{1,0:T(8,128)(2,1)}, u32[]{:S(2)}) copy-start(bf16[256,1024]{1,0:T(8,128)(2,1)} %up_weight.1) | copy-start | bytes 1572868
  30.5 20.5 %copy-start.5 = (bf16[1024,256]{1,0:T(8,128)(2,1)S(1)}, bf16[1024,256]{1,0:T(8,128)(2,1)}, u32[]{:S(2)}) copy-start(bf16[1024,256]{1,0:T(8,128)(2,1)} %down_weight.1) | copy-start | bytes 1572868
  30.5 20.5 %copy-start.17 = (f32[256]{0:T(256)S(1)}, f32[256]{0:T(256)}, u32[]{:S(2)}) copy-start(f32[256]{0:T(256)} %param.41) | copy-start | bytes 3076
  30.5 20.5 %copy-start.18 = (f32[256]{0:T(256)S(1)}, f32[256]{0:T(256)}, u32[]{:S(2)}) copy-start(f32[256]{0:T(256)} %param.42) | copy-start | bytes 3076
  30.5 29.6 %copy-start.7 = (bf16[256,256]{1,0:T(8,128)(2,1)S(1)}, bf16[256,256]{1,0:T(8,128)(2,1)}, u32[]{:S(2)}) copy-start(bf16[256,256]{1,0:T(8,128)(2,1)} %query_weight.1) | copy-start | bytes 393220
  30.6 29.6 %copy-start.10 = (bf16[128,256]{1,0:T(8,128)(2,1)S(1)}, bf16[128,256]{1,0:T(8,128)(2,1)}, u32[]{:S(2)}) copy-start(bf16[128,256]{1,0:T(8,128)(2,1)} %in_weight.1) | copy-start | bytes 196612
  30.6 29.6 %copy-start.11 = (bf16[256,128]{1,0:T(8,128)(2,1)S(1)}, bf16[256,128]{1,0:T(8,128)(2,1)}, u32[]{:S(2)}) copy-start(bf16[256,128]{1,0:T(8,128)(2,1)} %out_weight.1) | copy-start | bytes 196612
  39.0 5.9 %collective-permute-start.12 = (bf16[18,16,128]{2,1,0:T(8,128)(2,1)S(1)}, bf16[18,16,128]{2,1,0:T(8,128)(2,1)S(1)}, u32[]{:S(2)}, u32[]{:S(2)}) collective-permute-start(bf16[18,16,128]{2,1,0:T(8,128)(2,1)S(1)} %get-tuple-element.16), channel_id=1, source_target_pairs={{0,12},{4,0},{8,4},{12,8},{1,13},{5,1},{9,5},{13,9},{2,14},{6,2},{... | collective-permute-start | bytes 221192 | tf_op jit(solution)/shard_map/ppermute | solution.py:603
  42.7 8.3 %collective-permute-start.11 = (bf16[18,16,128]{2,1,0:T(8,128)(2,1)S(1)}, bf16[18,16,128]{2,1,0:T(8,128)(2,1)S(1)}, u32[]{:S(2)}, u32[]{:S(2)}) collective-permute-start(bf16[18,16,128]{2,1,0:T(8,128)(2,1)S(1)} %get-tuple-element.17), channel_id=1, source_target_pairs={{0,8},{4,12},{8,0},{12,4},{1,9},{5,13},{9,1},{13,5},{2,10},{6,14},... | collective-permute-start | bytes 221192 | tf_op jit(solution)/shard_map/ppermute | solution.py:603
  42.7 8.3 %collective-permute-start.10 = (bf16[18,16,128]{2,1,0:T(8,128)(2,1)S(1)}, bf16[18,16,128]{2,1,0:T(8,128)(2,1)S(1)}, u32[]{:S(2)}, u32[]{:S(2)}) collective-permute-start(bf16[18,16,128]{2,1,0:T(8,128)(2,1)S(1)} %get-tuple-element.18), channel_id=1, source_target_pairs={{0,4},{4,8},{8,12},{12,0},{1,5},{5,9},{9,13},{13,1},{2,6},{6,10},{... | collective-permute-start | bytes 221192 | tf_op jit(solution)/shard_map/ppermute | solution.py:603
  52.8 5.5 %collective-permute-start.15 = (bf16[16,256]{1,0:T(8,128)(2,1)S(1)}, bf16[16,256]{1,0:T(8,128)(2,1)S(1)}, u32[]{:S(2)}, u32[]{:S(2)}) collective-permute-start(bf16[16,256]{1,0:T(8,128)(2,1)S(1)} %nodes.1), channel_id=1, source_target_pairs={{0,4},{4,8},{8,12},{12,0},{1,5},{5,9},{9,13},{13,1},{2,6},{6,10},{... | collective-permute-start | bytes 24584 | tf_op jit(solution)/shard_map/ppermute | solution.py:622
  52.8 5.5 %collective-permute-start.14 = (bf16[16,256]{1,0:T(8,128)(2,1)S(1)}, bf16[16,256]{1,0:T(8,128)(2,1)S(1)}, u32[]{:S(2)}, u32[]{:S(2)}) collective-permute-start(bf16[16,256]{1,0:T(8,128)(2,1)S(1)} %nodes.1), channel_id=1, source_target_pairs={{0,8},{4,12},{8,0},{12,4},{1,9},{5,13},{9,1},{13,5},{2,10},{6,14},... | collective-permute-start | bytes 24584 | tf_op jit(solution)/shard_map/ppermute | solution.py:622
  54.7 4.2 %collective-permute-start.13 = (bf16[16,256]{1,0:T(8,128)(2,1)S(1)}, bf16[16,256]{1,0:T(8,128)(2,1)S(1)}, u32[]{:S(2)}, u32[]{:S(2)}) collective-permute-start(bf16[16,256]{1,0:T(8,128)(2,1)S(1)} %nodes.1), channel_id=1, source_target_pairs={{0,12},{4,0},{8,4},{12,8},{1,13},{5,1},{9,5},{13,9},{2,14},{6,2},{... | collective-permute-start | bytes 24584 | tf_op jit(solution)/shard_map/ppermute | solution.py:622
  58.9 1.2 %collective-permute-start.16 = (bf16[64,256]{1,0:T(8,128)(2,1)S(1)}, bf16[64,256]{1,0:T(8,128)(2,1)S(1)}, u32[]{:S(2)}, u32[]{:S(2)}) collective-permute-start(bf16[64,256]{1,0:T(8,128)(2,1)S(1)} %pad_maximum_fusion.1), channel_id=1, source_target_pairs={{0,1},{1,0},{2,3},{3,2},{4,5},{5,4},{6,7},{7,6},{8,9},{9,8},{10,11... | collective-permute-start | bytes 98312 | tf_op jit(solution)/shard_map/ppermute | solution.py:568
  60.2 2.2 %copy-start.1 = (bf16[64,128,256]{2,1,0:T(8,128)(2,1)S(1)}, bf16[64,128,256]{2,1,0:T(8,128)(2,1)}, u32[]{:S(2)}) copy-start(bf16[64,128,256]{2,1,0:T(8,128)(2,1)} %own_pairs.3) | copy-start | bytes 12582916

commit v2 on v1

--- a/solution.py
+++ b/solution.py
@@ -16,6 +16,8 @@
 FEATURES = CH + 4 * PV
 SLOT = 64
 ROWS = 16
+VMEM_MIB = 60
+CHUNKS = 4
 
 linear_scale = math.sqrt(1.0 / 3.0)
 masked_score = -1000000000.0
@@ -28,6 +30,10 @@
 
 def params(mib):
     return pltpu.CompilerParams(vmem_limit_bytes=mib * 2**20)
+
+
+def cost(microseconds):
+    return pl.CostEstimate(flops=0, bytes_accessed=3_000_000 * microseconds, transcendentals=0)
 
 
 def dot(left, right):
@@ -72,13 +78,89 @@
 SMEM = pl.BlockSpec(memory_space=pltpu.SMEM)
 
 
+def up16(count):
+    return -(-count // 16) * 16
+
+
+def through(moves, buffer, arrivals, departures):
+    starts, at = [], 0
+    for step, (source, target) in enumerate(moves):
+        end = at + source.shape[0]
+        load = pltpu.make_async_copy(source, buffer.at[at:end], arrivals.at[step])
+        load.start()
+        starts.append((load, pltpu.make_async_copy(buffer.at[at:end], target, departures.at[step])))
+        at = end
+    return starts
+
+
+def pass_on(starts):
+    for load, store in starts:
+        load.wait()
+        store.start()
+    for _, store in starts:
+        store.wait()
+
+
+def prepare_kernel(
+    point_gain, chain_gain, key_weight, query_weight, bias_weight, pairs, packed, sliced, last, buffer, arrivals, departures
+):
+    half = sliced.shape[1]
+    begin = pl.multiple_of((1 - lax.axis_index("sub")) * half, half)
+    span = sliced.shape[0] // CHUNKS
+    moves = [
+        (pairs.at[at * span : (at + 1) * span, pl.ds(begin, half), :], sliced.at[at * span : (at + 1) * span])
+        for at in range(CHUNKS)
+    ]
+    starts = through(moves, buffer, arrivals, departures)
+    heads, channels = bias_weight.shape
+    at = up16(key_weight.shape[0])
+    end = at + up16(query_weight.shape[0])
+    packed[0 : key_weight.shape[0]] = key_weight[...]
+    packed[at : at + query_weight.shape[0]] = query_weight[...]
+    row, lane = iota((16, 128), 0), iota((16, 128), 1)
+    pieces = jnp.zeros((16, 128), f32)
+    for which, gain in enumerate((point_gain, chain_gain)):
+        value = jnp.zeros((16, 128), f32)
+        for head in range(heads):
+            value = jnp.where(row == head, gain[head], value)
+        for step in range(3):
+            piece = rounded(value)
+            pieces = jnp.where(lane == 3 * which + step, piece, pieces)
+            value = value - piece
+    last[...] = jnp.zeros_like(last)
+    last[0:heads, 0:channels] = bias_weight[...].astype(f32)
+    last[:, channels : channels + 128] = pieces
+    packed[end : end + 16] = last[...].astype(bf16)
+    pass_on(starts)
+
+
+def prepare(point_gain, chain_gain, key_weight, query_weight, bias_weight, pairs, half):
+    operands = [key_weight, query_weight, bias_weight]
+    total = up16(key_weight.shape[0]) + up16(query_weight.shape[0]) + 16
+    hbm = pl.BlockSpec(memory_space=pl.ANY)
+    shape = jax.ShapeDtypeStruct((total, key_weight.shape[1]), bf16)
+    return pl.pallas_call(
+        prepare_kernel,
+        in_specs=[SMEM] * 2 + [whole(a) for a in operands] + [hbm],
+        out_shape=(shape, jax.ShapeDtypeStruct((pairs.shape[0], half, pairs.shape[2]), bf16)),
+        out_specs=(whole(shape), hbm),
+        scratch_shapes=[
+            pltpu.VMEM((16, key_weight.shape[1]), f32),
+            pltpu.VMEM((pairs.shape[0], half, pairs.shape[2]), bf16),
+            pltpu.SemaphoreType.DMA((CHUNKS,)),
+            pltpu.SemaphoreType.DMA((CHUNKS,)),
+        ],
+        compiler_params=params(VMEM_MIB),
+        cost_estimate=cost(2),
+        name="prepare",
+    )(point_gain, chain_gain, *operands, pairs)
+
+
 def project_kernel(
     blocks,
     place,
     point_own,
-    point_other,
     chain_own,
-    chain_other,
     query_nodes,
     query_angles,
     query_trans,
@@ -87,11 +169,9 @@
     key_trans,
     key_chain,
     query_weight_own,
-    query_weight_other,
     key_weight_own,
-    key_weight_other,
     bias_own,
-    bias_other,
+    packed,
     edge_key_weight,
     *rest,
 ):
@@ -99,28 +179,35 @@
     scores, values, bias_spread, query_frames, edge_keys = rest[blocks : blocks + 5]
     keys, key_proj, query_proj, key_side, query_side, query_rows = rest[blocks + 5 :]
     sub, mine = place[0], place[1]
-    local_heads = query_weight_own.shape[1] // QCOLS
+    local_heads = query_weight_own.shape[0] // QCOLS
     query_count, key_count = query_nodes.shape[0], keys.shape[0]
     half = scores.shape[1]
     share = key_blocks[0].shape[0]
+    query_at = up16(local_heads * KCOLS)
+    last_at = query_at + up16(local_heads * QCOLS)
+    last = packed[last_at : last_at + 16].astype(f32)
+    bias_other = last[0:local_heads, : bias_own.shape[1]].astype(bf16)
+    gains = last[:, bias_own.shape[1] :]
+    point_other = gains[:, 0:1] + gains[:, 1:2] + gains[:, 2:3]
+    chain_other = gains[:, 3:4] + gains[:, 4:5] + gains[:, 5:6]
     for step in range(blocks):
         source = lax.rem(mine - step + blocks, blocks)
         keys[pl.ds(pl.multiple_of(source * share, share), share), :] = key_blocks[step][...]
     nodes = keys[...]
-    key_proj[0] = dot_tt(key_weight_own[...], nodes)
-    key_proj[1] = dot_tt(key_weight_other[...], nodes)
-    query_proj[0] = dot_tt(query_weight_own[...], query_nodes[...])
-    query_proj[1] = dot_tt(query_weight_other[...], query_nodes[...])
+    key_proj[0] = dot_nt(key_weight_own[...], nodes)
+    key_proj[1] = dot_nt(packed[: local_heads * KCOLS], nodes)
+    query_proj[0] = dot_nt(query_weight_own[...], query_nodes[...])
+    query_proj[1] = dot_nt(packed[query_at : query_at + local_heads * QCOLS], query_nodes[...])
     edge_keys[...] = dot_tt(edge_key_weight[...], nodes)
 
-    channels = bias_own.shape[0] // 2
+    channels = bias_own.shape[1] // 2
     spread = channels * ROWS
     for at, offset in enumerate((sub * channels, (1 - sub) * channels)):
         select = (iota((2 * channels, spread), 0) == offset + iota((2 * channels, spread), 1) // ROWS)
         select = select.astype(f32).astype(bf16)
         diagonal = iota((1, ROWS, spread), 1) == iota((1, ROWS, spread), 2) % ROWS
-        for which, weight in enumerate((bias_own, bias_other)):
-            row = dot_tn(weight[...], select)
+        for which, weight in enumerate((bias_own[...], bias_other)):
+            row = dot(weight, select)
             block = jnp.where(diagonal, row[:, None, :], 0.0).reshape(local_heads * ROWS, spread)
             begin = which * local_heads * ROWS
             bias_spread[begin : begin + local_heads * ROWS, at * spread : (at + 1) * spread] = block.astype(bf16)
@@ -138,7 +225,7 @@
     key_squares = []
     for head in range(2 * local_heads):
         which, at = divmod(head, local_heads)
-        scale = (point_own if which == 0 else point_other)[at] * point_factor
+        scale = (point_own[at] if which == 0 else point_other[at : at + 1]) * point_factor
         begin = at * KCOLS
         key_side[head, 0:CH] = rounded(key_proj[which, begin : begin + CH])
         values[head, 0:CH] = key_proj[which, begin + CH : begin + 2 * CH].astype(bf16)
@@ -187,8 +274,8 @@
     same = (chains == key_chain[...].astype(f32)).astype(f32)
     for head in range(2 * local_heads):
         which, at = divmod(head, local_heads)
-        scale = (point_own if which == 0 else point_other)[at] * point_factor
-        chain_gain = (chain_own if which == 0 else chain_other)[at]
+        scale = (point_own[at] if which == 0 else point_other[at : at + 1]) * point_factor
+        chain_gain = chain_own[at] if which == 0 else chain_other[at : at + 1]
         left = query_rows[head, pl.ds(begin, half), :]
         score = dot(left.astype(bf16), key_side[head].astype(bf16))
         score = score + left[:, SLOT - 1 : SLOT] - scale * key_squares[head] + chain_gain * same
@@ -196,17 +283,17 @@
 
 
 def project(
-    place, gains, query_side, key_side, query_weights, key_weights, bias_weights, edge_key_weight, key_blocks, half
+    place, gains, query_side, key_side, query_weight, key_weight, bias_weight, packed, edge_key_weight, key_blocks, half
 ):
     query_count = query_side[0].shape[0]
     key_count = key_side[0].shape[1]
     local_heads = gains[0].shape[0]
     heads = 2 * local_heads
-    channels, hidden = bias_weights[0].shape[0], edge_key_weight.shape[1]
-    operands = [*query_side, *key_side, *query_weights, *key_weights, *bias_weights, edge_key_weight, *key_blocks]
+    channels, hidden = bias_weight.shape[1], edge_key_weight.shape[1]
+    operands = [*query_side, *key_side, query_weight, key_weight, bias_weight, packed, edge_key_weight, *key_blocks]
     return pl.pallas_call(
         functools.partial(project_kernel, len(key_blocks)),
-        in_specs=[SMEM] * 5 + [whole(a) for a in operands],
+        in_specs=[SMEM] * 3 + [whole(a) for a in operands],
         out_shape=(
             jax.ShapeDtypeStruct((heads, half, key_count), f32),
             jax.ShapeDtypeStruct((heads, SLOT, key_count), bf16),
@@ -222,7 +309,8 @@
             pltpu.VMEM((heads, SLOT, query_count), f32),
             pltpu.VMEM((heads, query_count, SLOT), f32),
         ],
-        compiler_params=params(32),
+        compiler_params=params(VMEM_MIB),
+        cost_estimate=cost(4),
         name="project",
     )(place, *gains, *operands)
 
@@ -336,7 +424,7 @@
             grid=(steps,),
             in_specs=[
                 pair_block,
-                pair_block,
+                pl.BlockSpec((channels, ROWS, keys), lambda g, p: (0, g, 0)),
                 pl.BlockSpec((heads, ROWS, keys), lambda g, p: (0, g, 0)),
                 pl.BlockSpec((ROWS, keys), lambda g, p: (p[0] * steps + g, 0)),
                 whole(values),
@@ -354,7 +442,8 @@
             ],
         ),
         out_shape=jax.ShapeDtypeStruct((heads + heads // 2, half, 2 * channels), bf16),
-        compiler_params=params(40),
+        compiler_params=params(VMEM_MIB),
+        cost_estimate=cost(9),
         name="attend",
     )(place, own_pairs, other_pairs, base_scores, mask, values, bias_spread, frames)
 
@@ -436,30 +525,14 @@
         functools.partial(node_kernel, len(parts)),
         in_specs=[whole(a) for a in operands],
         out_shape=jax.ShapeDtypeStruct(nodes.shape, bf16),
-        compiler_params=params(32),
+        compiler_params=params(16),
+        cost_estimate=cost(2),
         name="nodes",
     )(*operands)
 
 
-def edge_kernel(
-    place,
-    own_pairs,
-    other_pairs,
-    nodes,
-    edge_keys,
-    in_weight,
-    out_weight,
-    query_weight,
-    result,
-    new_nodes,
-    left,
-    out_left,
-    turned,
-    hidden,
-    fresh,
-):
-    channels, rows, keys = own_pairs.shape
-    both = 2 * channels
+def turn_kernel(place, own_pairs, other_pairs, in_weight, out_weight, result, left, out_left):
+    channels = own_pairs.shape[0]
     sub = place[0]
 
     @pl.when(pl.program_id(0) == 0)
@@ -467,71 +540,158 @@
         own = pl.multiple_of(sub * channels, channels)
         other = pl.multiple_of((1 - sub) * channels, channels)
         left[:, 0:channels] = in_weight[pl.ds(own, channels), :].astype(f32).T.astype(bf16)
-        left[:, channels:both] = in_weight[pl.ds(other, channels), :].astype(f32).T.astype(bf16)
+        left[:, channels:] = in_weight[pl.ds(other, channels), :].astype(f32).T.astype(bf16)
         flipped = out_weight[...].astype(f32).T
-        out_left[...] = jnp.where(sub == 0, flipped[0:channels], flipped[channels:]).astype(bf16)
-        picks = iota((rows, 2 * rows, keys), 1) % rows == iota((rows, 2 * rows, keys), 0)
-        turned[:, both:, :] = picks.astype(f32).astype(bf16)
-
-    new_nodes[...] = nodes[0, 0]
-    queries = dot_tt(query_weight[...], nodes[0, 0])
+        out_left[0:channels] = jnp.where(sub == 0, flipped[0:channels], flipped[channels:]).astype(bf16)
+        out_left[channels:] = jnp.where(sub == 0, flipped[channels:], flipped[0:channels]).astype(bf16)
+
+    result[:, 0:channels, :] = jnp.swapaxes(own_pairs[...], 0, 1)
+    result[:, channels:, :] = jnp.swapaxes(other_pairs[...], 0, 1)
+
+
+def turn_pairs(place, own_pairs, other_pairs, in_weight, out_weight):
+    channels, half, keys = other_pairs.shape
+    both, hidden = in_weight.shape
+    steps = half // ROWS
+    return pl.pallas_call(
+        turn_kernel,
+        grid_spec=pltpu.PrefetchScalarGridSpec(
+            num_scalar_prefetch=1,
+            grid=(steps,),
+            in_specs=[
+                pl.BlockSpec((channels, ROWS, keys), lambda g, p: (0, p[0] * steps + g, 0)),
+                pl.BlockSpec((channels, ROWS, keys), lambda g, p: (0, g, 0)),
+                whole(in_weight),
+                whole(out_weight),
+            ],
+            out_specs=(
+                pl.BlockSpec((ROWS, both, keys), lambda g, p: (g, 0, 0)),
+                pl.BlockSpec((hidden, both), lambda g, p: (0, 0)),
+                pl.BlockSpec((both, hidden), lambda g, p: (0, 0)),
+            ),
+        ),
+        out_shape=(
+            jax.ShapeDtypeStruct((half, both, keys), bf16),
+            jax.ShapeDtypeStruct((hidden, both), bf16),
+            jax.ShapeDtypeStruct((both, hidden), bf16),
+        ),
+        compiler_params=params(VMEM_MIB),
+        cost_estimate=cost(4),
+        name="turn_pairs",
+    )(place, own_pairs, other_pairs, in_weight, out_weight)
+
+
+def edge_kernel(
+    place, turned, nodes, edge_keys, in_left, out_left, query_weight, kept, sent, new_nodes, left, picks, hidden, fresh
+):
+    rows, both, keys = turned.shape
+    channels = both // 2
+
+    @pl.when(pl.program_id(0) == 0)
+    def _():
+        left[:, 0:both] = in_left[...]
+        chosen = iota((rows, 2 * rows, keys), 1) % rows == iota((rows, 2 * rows, keys), 0)
+        picks[...] = chosen.astype(f32).astype(bf16)
+
+    queries = dot_tt(query_weight[...], nodes[0])
     high = queries.astype(bf16)
     left[:, both : both + rows] = high
     left[:, both + rows :] = (queries - high.astype(f32)).astype(bf16)
-    turned[:, 0:channels, :] = jnp.swapaxes(own_pairs[...], 0, 1)
-    turned[:, channels:both, :] = jnp.swapaxes(other_pairs[...], 0, 1)
+    new_nodes[...] = nodes[0]
+    for at in range(sent.shape[0] - channels):
+        sent[channels + at] = nodes[0, :, at * keys : (at + 1) * keys]
     for row in range(rows):
-        hidden[row] = jnp.maximum(dot(left[...], turned[row]) + edge_keys[...], 0.0).astype(bf16)
+        right = jnp.concatenate([turned[row], picks[row]], axis=0)
+        hidden[row] = jnp.maximum(dot(left[...], right) + edge_keys[...], 0.0).astype(bf16)
     for row in range(rows):
-        out = dot(out_left[...], hidden[row])
-        for at in range(keys // 128):
-            fresh[at, pl.ds(row, channels, stride=rows), :] = out[:, at * 128 : (at + 1) * 128]
-    for at in range(keys // 128):
-        span = slice(at * 128, (at + 1) * 128)
-        old = own_pairs[:, :, span].reshape(channels * rows, 128).astype(f32)
-        result[:, :, span] = (old + fresh[at]).astype(bf16).reshape(channels, rows, 128)
-
-
-def update_pairs(place, own_pairs, other_pairs, nodes, edge_keys, in_weight, out_weight, query_weight):
-    channels, count, keys = own_pairs.shape
-    hidden = in_weight.shape[1]
-    features = nodes.shape[-1]
-    steps = nodes.shape[1]
-    pair_block = pl.BlockSpec((channels, ROWS, keys), lambda g, p: (0, g, 0))
-
-    def node_block(g, p):
-        return (lax.rem(g // steps + p[0], 2), lax.rem(lax.rem(g, steps) + p[1], steps), 0, 0)
-
+        old = turned[row].astype(f32)
+        fresh[row] = (old + dot(out_left[...], hidden[row])).astype(bf16)
+    kept[...] = jnp.swapaxes(fresh[:, 0:channels, :], 0, 1)
+    sent[0:channels] = jnp.swapaxes(fresh[:, channels:, :], 0, 1)
+
+
+def update_pairs(place, count, turned, nodes, edge_keys, in_left, out_left, query_weight):
+    half, both, keys = turned.shape
+    channels, hidden = both // 2, in_left.shape[0]
+    steps, _, features = nodes.shape
+    assert features % keys == 0
+    extra = features // keys
     return pl.pallas_call(
         edge_kernel,
         grid_spec=pltpu.PrefetchScalarGridSpec(
             num_scalar_prefetch=1,
-            grid=(count // ROWS,),
+            grid=(steps,),
             in_specs=[
-                pair_block,
-                pair_block,
-                pl.BlockSpec((1, 1, ROWS, features), node_block),
+                pl.BlockSpec((ROWS, both, keys), lambda g, p: (g, 0, 0)),
+                pl.BlockSpec((1, ROWS, features), lambda g, p: (lax.rem(g + p[1], steps), 0, 0)),
                 whole(edge_keys),
-                whole(in_weight),
-                whole(out_weight),
+                whole(in_left),
+                whole(out_left),
                 whole(query_weight),
             ],
-            out_specs=(pair_block, pl.BlockSpec((ROWS, features), lambda g, p: (g, 0))),
+            out_specs=(
+                pl.BlockSpec((channels, ROWS, keys), lambda g, p: (0, p[0] * steps + g, 0)),
+                pl.BlockSpec((channels + extra, ROWS, keys), lambda g, p: (0, g, 0)),
+                pl.BlockSpec((ROWS, features), lambda g, p: (p[0] * steps + g, 0)),
+            ),
             scratch_shapes=[
-                pltpu.VMEM((hidden, 2 * channels + 2 * ROWS), bf16),
-                pltpu.VMEM((channels, hidden), bf16),
-                pltpu.VMEM((ROWS, 2 * channels + 2 * ROWS, keys), bf16),
+                pltpu.VMEM((hidden, both + 2 * ROWS), bf16),
+                pltpu.VMEM((ROWS, 2 * ROWS, keys), bf16),
                 pltpu.VMEM((ROWS, hidden, keys), bf16),
-                pltpu.VMEM((keys // 128, channels * ROWS, 128), f32),
+                pltpu.VMEM((ROWS, both, keys), bf16),
             ],
         ),
         out_shape=(
-            jax.ShapeDtypeStruct(own_pairs.shape, bf16),
+            jax.ShapeDtypeStruct((channels, count, keys), bf16),
+            jax.ShapeDtypeStruct((channels + extra, half, keys), bf16),
             jax.ShapeDtypeStruct((count, features), bf16),
         ),
-        compiler_params=params(40),
+        compiler_params=params(VMEM_MIB),
+        cost_estimate=cost(8),
         name="edges",
-    )(place, own_pairs, other_pairs, nodes, edge_keys, in_weight, out_weight, query_weight)
+    )(place, turned, nodes, edge_keys, in_left, out_left, query_weight)
+
+
+def finish_kernel(arrived, pairs_in, nodes_in, pairs, nodes, buffer, arrivals, departures):
+    channels, half, keys = pairs.shape[0], arrived.shape[1], arrived.shape[2]
+    begin = pl.multiple_of((1 - lax.axis_index("sub")) * half, half)
+    rows = pl.ds(begin, half)
+    span = channels // CHUNKS
+    moves = [
+        (arrived.at[at * span : (at + 1) * span], pairs.at[at * span : (at + 1) * span, rows, :])
+        for at in range(CHUNKS)
+    ]
+    starts = through(moves, buffer, arrivals, departures)
+    for at in range(arrived.shape[0] - channels):
+        source = arrived.at[channels + at]
+        load = pltpu.make_async_copy(source, buffer.at[channels + at], arrivals.at[CHUNKS + at])
+        target = nodes.at[rows, at * keys : (at + 1) * keys]
+        load.start()
+        starts.append((load, pltpu.make_async_copy(buffer.at[channels + at], target, departures.at[CHUNKS + at])))
+    pass_on(starts)
+
+
+def finish(arrived, pairs, nodes):
+    hbm = pl.BlockSpec(memory_space=pl.ANY)
+    copies = CHUNKS + arrived.shape[0] - pairs.shape[0]
+    return pl.pallas_call(
+        finish_kernel,
+        in_specs=[hbm] * 3,
+        out_specs=(hbm, hbm),
+        out_shape=(
+            jax.ShapeDtypeStruct(pairs.shape, bf16),
+            jax.ShapeDtypeStruct(nodes.shape, bf16),
+        ),
+        scratch_shapes=[
+            pltpu.VMEM(arrived.shape, bf16),
+            pltpu.SemaphoreType.DMA((copies,)),
+            pltpu.SemaphoreType.DMA((copies,)),
+        ],
+        input_output_aliases={1: 0, 2: 1},
+        compiler_params=params(62),
+        cost_estimate=cost(1),
+        name="finish",
+    )(arrived, pairs, nodes)
 
 
 def shards(
@@ -568,45 +728,53 @@
         return lax.ppermute(values, "sub", [(i, (i + 1) % subs) for i in range(subs)])
 
     group = rows * subs
-    mine = lax.axis_index(("row", "sub"))
     key_blocks = [node_key] + [
         lax.ppermute(node_key, ("row", "sub"), [(i, (i + k) % group) for i in range(group)])
         for k in range(1, group)
     ]
-    other_query, other_key, other_bias = swap(query_weight), swap(key_weight), swap(bias_weight)
-    other_point, other_chain = swap(point_gain), swap(chain_gain)
-    other_pairs = swap(pair_features)
-    other_out = swap(out_weight)
-
-    query_count = node_query.shape[0]
-    half = query_count // subs
+    half = node_query.shape[0] // subs
+    query_weight, key_weight, bias_weight = query_weight.T, key_weight.T, bias_weight.T
+    packed, late_pairs = prepare(
+        point_gain, chain_gain, key_weight, query_weight, bias_weight, pair_features, half
+    )
+    packed = swap(packed)
+    other_pairs = swap(late_pairs)
+
     share = half // cols
-    place = jnp.stack([sub, mine]).astype(jnp.int32)
+    place = jnp.stack([sub, lax.axis_index(("row", "sub"))]).astype(jnp.int32)
     base_scores, values, bias_spread, frames, edge_keys = project(
         place,
-        [point_gain, other_point, chain_gain, other_chain],
+        [point_gain, chain_gain],
         [node_query, query_angles, query_trans, query_chain[None, :]],
         [key_angles, key_trans, key_chain[None, :]],
-        [query_weight, other_query],
-        [key_weight, other_key],
-        [bias_weight, other_bias],
+        query_weight,
+        key_weight,
+        bias_weight,
+        packed,
         edge_key_weight,
         key_blocks,
         half,
     )
     part = attend(place, pair_features, other_pairs, base_scores, pair_mask, values, bias_spread, frames)
+    other_out = swap(lax.optimization_barrier((out_weight, base_scores))[0])
 
     def piece(k):
         return lax.dynamic_slice_in_dim(part, lax.rem(col + k, cols) * share, share, 1)
 
-    parts = [piece(0)] + [
-        lax.ppermute(piece(k), "col", [(i, (i + k) % cols) for i in range(cols)]) for k in range(1, cols)
+    pieces = [piece(k) for k in range(cols)]
+    parts = [pieces[0]] + [
+        lax.ppermute(pieces[k], "col", [(i, (i + k) % cols) for i in range(cols)]) for k in range(1, cols)
     ]
     spare = -share % ROWS
     own_nodes = lax.dynamic_slice_in_dim(node_query, sub * half + col * share, share, 0)
     if spare:
         parts = [jnp.pad(p, ((0, 0), (0, spare), (0, 0))) for p in parts]
         own_nodes = jnp.pad(own_nodes, ((0, spare), (0, 0)))
+    turn_place, _ = lax.optimization_barrier((place, pieces))
+    turned, in_left, out_left = turn_pairs(
+        turn_place, pair_features, other_pairs, edge_in_weight, edge_out_weight
+    )
+    own_nodes, turned = lax.optimization_barrier((own_nodes, turned))
     fresh_nodes = update_nodes(
         parts,
         own_nodes,
@@ -621,24 +789,18 @@
     ring = [fresh_nodes] + [
         lax.ppermute(fresh_nodes, "col", [(i, (i - k) % cols) for i in range(cols)]) for k in range(1, cols)
     ]
-    half_nodes = jnp.concatenate(ring, axis=0)
+    near_nodes = jnp.concatenate(ring, axis=0)
     if spare:
-        half_nodes = jnp.roll(half_nodes, col * share, axis=0)
+        near_nodes = jnp.roll(near_nodes, col * share, axis=0)
         turn = 0 * col
     else:
         turn = lax.rem(cols - col, cols) * (share // ROWS)
-    both_nodes = jnp.stack([half_nodes, swap(half_nodes)])
-    both_nodes = both_nodes.reshape(subs, half // ROWS, ROWS, node_query.shape[1])
-    updated_pairs, updated_nodes = update_pairs(
-        jnp.stack([sub, turn]).astype(jnp.int32),
-        pair_features,
-        other_pairs,
-        both_nodes,
-        edge_keys,
-        edge_in_weight,
-        edge_out_weight,
-        edge_query_weight,
+    near_nodes = near_nodes.reshape(half // ROWS, ROWS, near_nodes.shape[1])
+    edge_place = jnp.stack([sub, turn]).astype(jnp.int32)
+    kept, sent, new_nodes = update_pairs(
+        edge_place, pair_features.shape[1], turned, near_nodes, edge_keys, in_left, out_left, edge_query_weight
     )
+    updated_pairs, updated_nodes = finish(swap(sent), kept, new_nodes)
     return (updated_nodes, updated_pairs)
 
 

time: 79.1 us -> 66.8 us (0.84)
  local copies, waits for them, and re-layouts: 16.8 us -> 3.91 us
  waiting for transfers between devices: 17.2 us -> 7.23 us
  Pallas kernels: 28.3 us -> 37.1 us
  other arithmetic: 0.16 us -> 1.75 us
    unnamed x49 -> x24, local copies, waits for them, and re-layouts: 16.1 us -> 2.07 us
    pallas_call x0 -> x3, Pallas kernels: none -> 12.6 us  [the longest x1 5.97 us: turn_pairs(): pl.pallas_call(turn_kernel, grid_spec=pltpu.PrefetchScalarGridSpec(num_sc...]
    pallas_call x1, Pallas kernels: 16.1 us -> 9.06 us  [update_pairs(): pl.pallas_call(edge_kernel, grid_spec=pltpu.PrefetchScalarGridSpec(num_sc...]
    ppermute x3, waiting for transfers between devices: 6.58 us -> 0.01 us  [shards(): lax.ppermute(pieces[k], 'col', [(i, (i + k) % cols) for i in range(cols)])]
    pallas_call x1, Pallas kernels: 2.06 us -> 3.91 us  [project(): pl.pallas_call(functools.partial(project_kernel, len(key_blocks)), in_spe...]
    ppermute x3, waiting for transfers between devices: 2.91 us -> 1.06 us  [shards(): lax.ppermute(node_key, ('row', 'sub'), [(i, (i + k) % group) for i in ran...]
    ppermute x8 -> x4, waiting for transfers between devices: 6.33 us -> 4.55 us  [swap(): lax.ppermute(values, 'sub', [(i, (i + 1) % subs) for i in range(subs)])]
    pallas_call x1, Pallas kernels: 8.38 us -> 9.7 us  [attend(): pl.pallas_call(attend_kernel, grid_spec=pltpu.PrefetchScalarGridSpec(num_...]
  transfers between devices with their start and end apart: 17 -> 13, of which waited for: 11 -> 4; matrix products, arithmetic and copies ran while one was open for 5% -> 5% of each run, Pallas kernels for 13% -> 30%
where the time goes in v2:
time: 66.8 us; the launch traced here: 66.3 us
  Pallas kernels  37.1 us (56%)
  starting transfers between devices  15.5 us (23%)
  waiting for transfers between devices  7.23 us (11%)
  local copies, waits for them, and re-layouts  3.91 us (6%)
  other arithmetic  1.75 us (3%)
  between operations  0.8 us (1%)
    pallas_call x1, Pallas kernels, attend(): pl.pallas_call(attend_kernel, grid_spec=pltpu.PrefetchScalarGridSpec(num_...  9.7 us
    pallas_call x1, Pallas kernels, update_pairs(): pl.pallas_call(edge_kernel, grid_spec=pltpu.PrefetchScalarGridSpec(num_sc...  9.06 us
    pallas_call x1, Pallas kernels, turn_pairs(): pl.pallas_call(turn_kernel, grid_spec=pltpu.PrefetchScalarGridSpec(num_sc...  5.97 us
    ppermute x3, starting transfers between devices, shards(): lax.ppermute(pieces[k], 'col', [(i, (i + k) % cols) for i in range(cols)])  5.14 us
    ppermute x3, starting transfers between devices, shards(): lax.ppermute(fresh_nodes, 'col', [(i, (i - k) % cols) for i in range(cols)])  4.92 us
    ppermute x3, starting transfers between devices, shards(): lax.ppermute(node_key, ('row', 'sub'), [(i, (i + k) % group) for i in ran...  4.66 us
    ppermute x4, waiting for transfers between devices, swap(): lax.ppermute(values, 'sub', [(i, (i + 1) % subs) for i in range(subs)])  4.55 us
    pallas_call x1, Pallas kernels, prepare(): pl.pallas_call(prepare_kernel, in_specs=[SMEM] * 2 + [whole(a) for a in o...  4.18 us
  transfers between devices with their start and end apart: 13, of which 4 were waited for; matrix products, arithmetic and copies ran while one was open for 5% of the time, Pallas kernels for 30%

profile of v2, /device:TPU:0, one launch (start us, length us, event | category | flops | bytes accessed | tf_op | source)
XLA Modules:
  0.0 66.3 jit_solution(11347138736997632261)
XLA Ops:
  0.6 0.0 copy-start.8
  0.6 0.0 copy-start
  0.7 4.2 %prepare.1 = (bf16[608,256]{1,0:T(8,128)(2,1)}, bf16[64,64,256]{2,1,0:T(8,128)(2,1)}) custom-call(f32[6]{0:T(128)} %point_own.1, f32[6]{0:T(128)} %chain_own.1, bf16[408,256]{1,0:T(8,128)(2,1)} %bitcast.13, bf16[168,256]{1,0:T(8,128)(2,1)} %bitcast.15, bf16[6,128]{1,0:T(8,128)(2,1)} %bitcast.18, bf16[64,128,256]{2,1,0:T(8,128)(2,1)} %own_pairs.3), custom_call_target="tpu_custom_call" | custom-call | bytes 6000000 | tf_op jit(solution)/shard_map/prepare/pallas_call | solution.py:142
  4.8 0.5 collective-permute-start
  5.4 0.1 collective-permute-start.1
  5.4 2.9 %collective-permute-start.3 = (bf16[64,256]{1,0:T(8,128)(2,1)S(1)}, bf16[64,256]{1,0:T(8,128)(2,1)S(1)}, u32[]{:S(2)}, u32[]{:S(2)}) collective-permute-start(bf16[64,256]{1,0:T(8,128)(2,1)S(1)} %copy-done.8), channel_id=1, source_target_pairs={{0,2},{1,3},{2,0},{3,1},{4,6},{5,7},{6,4},{7,5},{8,10},{9,11},{10,... | collective-permute-start | bytes 98312 | tf_op jit(solution)/shard_map/ppermute | solution.py:732
  8.4 0.0 collective-permute-start.2
  8.4 1.7 %collective-permute-start.4 = (bf16[64,256]{1,0:T(8,128)(2,1)S(1)}, bf16[64,256]{1,0:T(8,128)(2,1)S(1)}, u32[]{:S(2)}, u32[]{:S(2)}) collective-permute-start(bf16[64,256]{1,0:T(8,128)(2,1)S(1)} %copy-done.8), channel_id=1, source_target_pairs={{0,3},{1,0},{2,1},{3,2},{4,7},{5,4},{6,5},{7,6},{8,11},{9,8},{10,9... | collective-permute-start | bytes 98312 | tf_op jit(solution)/shard_map/ppermute | solution.py:732
  10.1 0.6 pad_add_fusion.1.place
  10.7 0.0 collective-permute-done.3.rest_2_
  10.7 1.1 %collective-permute-done.2.rest_1_ = bf16[64,256]{1,0:T(8,128)(2,1)S(1)} collective-permute-done((bf16[64,256]{1,0:T(8,128)(2,1)S(1)}, bf16[64,256]{1,0:T(8,128)(2,1)S(1)}, u32[]{:S(2)}, u32[]{:S(2)}) %collective-permute-start.2) | collective-permute-done | bytes 32800 | tf_op jit(solution)/shard_map/ppermute | solution.py:732
  11.7 0.0 collective-permute-done.4.rest_3_
  11.7 0.0 collective-permute-done.1.packed
  11.8 0.6 copy-done.10
  12.3 0.0 copy-done.11
  12.3 0.1 copy-done.7
  12.5 3.9 %project.1 = (f32[12,64,256]{2,1,0:T(8,128)}, bf16[12,64,256]{2,1,0:T(8,128)(2,1)}, bf16[192,2048]{1,0:T(8,128)(2,1)}, f32[128,16]{1,0:T(8,128)}, f32[256,256]{1,0:T(8,128)}) custom-call(s32[2]{0:T(128)} %pad_add_fusion.1.place, f32[6]{0:T(128)} %point_own.1, f32[6]{0:T(128)} %chain_own.1, bf16[128,256]{1,0:T(8,128)(2,1)} %query_nodes.1, ...), custom_call_target="tpu_custom_call" | custom-call | bytes 12000000 | tf_op jit(solution)/shard_map/project/pallas_call | solution.py:294
  16.4 0.0 copy-done
  16.4 0.2 collective-permute-start.5
  16.6 0.0 collective-permute-done.other_pairs
  16.6 1.3 %copy-done.6 = bf16[64,64,256]{2,1,0:T(8,128)(2,1)} copy-done((bf16[64,64,256]{2,1,0:T(8,128)(2,1)}, bf16[64,64,256]{2,1,0:T(8,128)(2,1)S(1)}, u32[]{:S(2)}) %copy-start.6) | copy-done | bytes 2097176
  17.9 9.7 %attend.1 = bf16[18,64,128]{2,1,0:T(8,128)(2,1)} custom-call(s32[2]{0:T(128)} %pad_add_fusion.1.place, bf16[64,128,256]{2,1,0:T(8,128)(2,1)} %own_pairs.3, bf16[64,64,256]{2,1,0:T(8,128)(2,1)} %copy-done.6, f32[12,64,256]{2,1,0:T(8,128)} %get-tuple-element.23.base_scores, s32[128,256]{1,0:T(8,128)} %mask.1, bf16[12,64,256]{2,1,0:T(8,128)(2,1)} %get-tuple-element.24.values, ...), custom_call_target="tpu_custom_call" | custom-call | bytes 27000000 | tf_op jit(solution)/shard_map/attend/pallas_call | solution.py:420
  27.6 0.0 copy-start.3
  27.6 0.0 copy-start.4
  27.6 0.0 copy-start.5
  27.7 1.1 %constant_dynamic-slice_fusion = (bf16[18,16,128]{2,1,0:T(8,128)(2,1)S(1)}, bf16[18,16,128]{2,1,0:T(8,128)(2,1)S(1)}, bf16[18,16,128]{2,1,0:T(8,128)(2,1)S(1)}, bf16[18,16,128]{2,1,0:T(8,128)(2,1)S(1)}) fusion(bf16[18,64,128]{2,1,0:T(8,128)(2,1)} %attend.1, s32[]{:T(128)S(6)} %select_n.19, s32[]{:T(128)S(6)} %select_n.18, s32[]{:T(128)S(6)} %select_n.17, ...), kind=kLoop, calls=%fused_computation.1 | loop fusion | bytes 589840 | tf_op jit(solution)/shard_map/dynamic_slice | solution.py:762
  28.8 4.1 %collective-permute-start.8 = (bf16[18,16,128]{2,1,0:T(8,128)(2,1)S(1)}, bf16[18,16,128]{2,1,0:T(8,128)(2,1)S(1)}, u32[]{:S(2)}, u32[]{:S(2)}) collective-permute-start(bf16[18,16,128]{2,1,0:T(8,128)(2,1)S(1)} %get-tuple-element.40), channel_id=1, source_target_pairs={{0,12},{4,0},{8,4},{12,8},{1,13},{5,1},{9,5},{13,9},{2,14},{6,2},{... | collective-permute-start | bytes 221192 | tf_op jit(solution)/shard_map/ppermute | solution.py:766
  32.9 0.0 collective-permute-start.7
  32.9 1.0 %collective-permute-start.6 = (bf16[18,16,128]{2,1,0:T(8,128)(2,1)S(1)}, bf16[18,16,128]{2,1,0:T(8,128)(2,1)S(1)}, u32[]{:S(2)}, u32[]{:S(2)}) collective-permute-start(bf16[18,16,128]{2,1,0:T(8,128)(2,1)S(1)} %get-tuple-element.42), channel_id=1, source_target_pairs={{0,4},{4,8},{8,12},{12,0},{1,5},{5,9},{9,13},{13,1},{2,6},{6,10},{... | collective-permute-start | bytes 221192 | tf_op jit(solution)/shard_map/ppermute | solution.py:766
  33.9 0.7 %constant_dynamic-slice_fusion.4.nodes = bf16[16,256]{1,0:T(8,128)(2,1)S(1)} fusion(bf16[128,256]{1,0:T(8,128)(2,1)} %query_nodes.1, s32[]{:T(128)S(6)} %select_n.15), kind=kLoop, calls=%fused_computation.5 | loop fusion | bytes 16388 | tf_op jit(solution)/shard_map/dynamic_slice | solution.py:769
  34.6 6.0 %turn_pairs.1 = (bf16[64,128,256]{2,1,0:T(8,128)(2,1)}, bf16[256,128]{1,0:T(8,128)(2,1)}, bf16[128,256]{1,0:T(8,128)(2,1)}) custom-call(s32[2]{0:T(128)} %pad_add_fusion.1.place, bf16[64,128,256]{2,1,0:T(8,128)(2,1)} %own_pairs.3, bf16[64,64,256]{2,1,0:T(8,128)(2,1)} %copy-done.6, bf16[128,256]{1,0:T(8,128)(2,1)} %in_weight.1, bf16[256,128]{1,0:T(8,128)(2,1)} %out_weight.1), custom_call_target="tpu_custom_call" | custom-call | bytes 12000000 | tf_op jit(solution)/shard_map/turn_pairs/pallas_call | solution.py:556
  40.6 0.0 collective-permute-done.5.out_other
  40.6 0.0 collective-permute-done.8.rest_3_
  40.6 0.0 collective-permute-done.7.rest_2_
  40.6 0.0 collective-permute-done.6.rest_1_
  40.7 1.8 %nodes.1 = bf16[16,256]{1,0:T(8,128)(2,1)S(1)} custom-call(bf16[16,256]{1,0:T(8,128)(2,1)S(1)} %constant_dynamic-slice_fusion.4.nodes, bf16[1056,256]{1,0:T(8,128)(2,1)S(1)} %copy-done, bf16[1056,256]{1,0:T(8,128)(2,1)S(1)} %collective-permute-done.5.out_other, f32[1,256]{1,0:T(1,128)S(1)} %bitcast.11, f32[1,256]{1,0:T(1,128)S(1)} %bitcast.12, ...), custom_call_target="tpu_custom_call" | custom-call | bytes 6000000 | tf_op jit(solution)/shard_map/nodes/pallas_call | solution.py:524
  42.5 2.5 %collective-permute-start.11 = (bf16[16,256]{1,0:T(8,128)(2,1)S(1)}, bf16[16,256]{1,0:T(8,128)(2,1)S(1)}, u32[]{:S(2)}, u32[]{:S(2)}) collective-permute-start(bf16[16,256]{1,0:T(8,128)(2,1)S(1)} %nodes.1), channel_id=1, source_target_pairs={{0,4},{4,8},{8,12},{12,0},{1,5},{5,9},{9,13},{13,1},{2,6},{6,10},{... | collective-permute-start | bytes 24584 | tf_op jit(solution)/shard_map/ppermute | solution.py:790
  45.0 0.9 %collective-permute-start.10 = (bf16[16,256]{1,0:T(8,128)(2,1)S(1)}, bf16[16,256]{1,0:T(8,128)(2,1)S(1)}, u32[]{:S(2)}, u32[]{:S(2)}) collective-permute-start(bf16[16,256]{1,0:T(8,128)(2,1)S(1)} %nodes.1), channel_id=1, source_target_pairs={{0,8},{4,12},{8,0},{12,4},{1,9},{5,13},{9,1},{13,5},{2,10},{6,14},... | collective-permute-start | bytes 24584 | tf_op jit(solution)/shard_map/ppermute | solution.py:790
  45.9 1.5 %collective-permute-start.9 = (bf16[16,256]{1,0:T(8,128)(2,1)S(1)}, bf16[16,256]{1,0:T(8,128)(2,1)S(1)}, u32[]{:S(2)}, u32[]{:S(2)}) collective-permute-start(bf16[16,256]{1,0:T(8,128)(2,1)S(1)} %nodes.1), channel_id=1, source_target_pairs={{0,12},{4,0},{8,4},{12,8},{1,13},{5,1},{9,5},{13,9},{2,14},{6,2},{... | collective-permute-start | bytes 24584 | tf_op jit(solution)/shard_map/ppermute | solution.py:790
  47.4 0.6 pad_add_fusion.place
  48.0 0.0 collective-permute-done.11
  48.0 1.5 %collective-permute-done.10 = bf16[16,256]{1,0:T(8,128)(2,1)S(1)} collective-permute-done((bf16[16,256]{1,0:T(8,128)(2,1)S(1)}, bf16[16,256]{1,0:T(8,128)(2,1)S(1)}, u32[]{:S(2)}, u32[]{:S(2)}) %collective-permute-start.10) | collective-permute-done | bytes 8224 | tf_op jit(solution)/shard_map/ppermute | solution.py:790
  49.5 0.1 collective-permute-done.9
  49.6 0.6 pad_maximum_fusion
  50.2 9.1 %edges.1 = (bf16[64,128,256]{2,1,0:T(8,128)(2,1)}, bf16[65,64,256]{2,1,0:T(8,128)(2,1)}, bf16[128,256]{1,0:T(8,128)(2,1)}) custom-call(s32[2]{0:T(128)} %pad_add_fusion.place, bf16[64,128,256]{2,1,0:T(8,128)(2,1)} %get-tuple-element.29.turned, bf16[4,16,256]{2,1,0:T(8,128)(2,1)} %bitcast.17, f32[256,256]{1,0:T(8,128)} %get-tuple-element.32.edge_keys, ...), custom_call_target="tpu_custom_call" | custom-call | bytes 24000000 | tf_op jit(solution)/shard_map/edges/pallas_call | solution.py:619
  59.3 0.0 collective-permute-start.12
  59.3 4.5 %collective-permute-done.12.arrived = bf16[65,64,256]{2,1,0:T(8,128)(2,1)} collective-permute-done((bf16[65,64,256]{2,1,0:T(8,128)(2,1)}, bf16[65,64,256]{2,1,0:T(8,128)(2,1)}, u32[]{:S(2)}, u32[]{:S(2)}) %collective-permute-start.12) | collective-permute-done | bytes 2129952 | tf_op jit(solution)/shard_map/ppermute | solution.py:728
  63.8 2.4 %finish.1 = (bf16[64,128,256]{2,1,0:T(8,128)(2,1)}, bf16[128,256]{1,0:T(8,128)(2,1)}) custom-call(bf16[65,64,256]{2,1,0:T(8,128)(2,1)} %collective-permute-done.12.arrived, bf16[64,128,256]{2,1,0:T(8,128)(2,1)} %get-tuple-element.36.pairs_in, bf16[128,256]{1,0:T(8,128)(2,1)} %get-tuple-element.37.nodes_in), custom_call_target="tpu_custom_call", output_to_operand_aliasing={{0}: (1, {}), {1}: (2, {})} | custom-call | bytes 3000000 | tf_op jit(solution)/shard_map/finish/pallas_call | solution.py:677
  (14 shorter events, 0.0 us)
Async XLA Ops:
  0.6 4.8 %copy-start.8 = (bf16[64,256]{1,0:T(8,128)(2,1)S(1)}, bf16[64,256]{1,0:T(8,128)(2,1)}, u32[]{:S(2)}) copy-start(bf16[64,256]{1,0:T(8,128)(2,1)} %rest_0_.1) | copy-start | bytes 98308
  0.6 15.7 %copy-start = (bf16[1056,256]{1,0:T(8,128)(2,1)S(1)}, bf16[1056,256]{1,0:T(8,128)(2,1)}, u32[]{:S(2)}) copy-start(bf16[1056,256]{1,0:T(8,128)(2,1)} %out_own.1) | copy-start | bytes 1622020
  4.8 11.8 %collective-permute-start = (bf16[64,64,256]{2,1,0:T(8,128)(2,1)}, bf16[64,64,256]{2,1,0:T(8,128)(2,1)S(1)}, u32[]{:S(2)}, u32[]{:S(2)}) collective-permute-start(bf16[64,64,256]{2,1,0:T(8,128)(2,1)} %get-tuple-element.21), channel_id=1, source_target_pairs={{0,1},{1,0},{2,3},{3,2},{4,5},{5,4},{6,7},{7,6},{8,9},{9,8},{10,11... | collective-permute-start | bytes 6291464 | tf_op jit(solution)/shard_map/ppermute | solution.py:728
  5.4 6.4 %collective-permute-start.1 = (bf16[608,256]{1,0:T(8,128)(2,1)}, bf16[608,256]{1,0:T(8,128)(2,1)S(1)}, u32[]{:S(2)}, u32[]{:S(2)}) collective-permute-start(bf16[608,256]{1,0:T(8,128)(2,1)} %get-tuple-element.22), channel_id=1, source_target_pairs={{0,1},{1,0},{2,3},{3,2},{4,5},{5,4},{6,7},{7,6},{8,9},{9,8},{10,11... | collective-permute-start | bytes 933896 | tf_op jit(solution)/shard_map/ppermute | solution.py:728
  5.4 5.2 %collective-permute-start.3 = (bf16[64,256]{1,0:T(8,128)(2,1)S(1)}, bf16[64,256]{1,0:T(8,128)(2,1)S(1)}, u32[]{:S(2)}, u32[]{:S(2)}) collective-permute-start(bf16[64,256]{1,0:T(8,128)(2,1)S(1)} %copy-done.8), channel_id=1, source_target_pairs={{0,2},{1,3},{2,0},{3,1},{4,6},{5,7},{6,4},{7,5},{8,10},{9,11},{10,... | collective-permute-start | bytes 98312 | tf_op jit(solution)/shard_map/ppermute | solution.py:732
  8.4 3.4 %collective-permute-start.2 = (bf16[64,256]{1,0:T(8,128)(2,1)S(1)}, bf16[64,256]{1,0:T(8,128)(2,1)S(1)}, u32[]{:S(2)}, u32[]{:S(2)}) collective-permute-start(bf16[64,256]{1,0:T(8,128)(2,1)S(1)} %copy-done.8), channel_id=1, source_target_pairs={{0,1},{1,2},{2,3},{3,0},{4,5},{5,6},{6,7},{7,4},{8,9},{9,10},{10,1... | collective-permute-start | bytes 98312 | tf_op jit(solution)/shard_map/ppermute | solution.py:732
  8.4 3.4 %collective-permute-start.4 = (bf16[64,256]{1,0:T(8,128)(2,1)S(1)}, bf16[64,256]{1,0:T(8,128)(2,1)S(1)}, u32[]{:S(2)}, u32[]{:S(2)}) collective-permute-start(bf16[64,256]{1,0:T(8,128)(2,1)S(1)} %copy-done.8), channel_id=1, source_target_pairs={{0,3},{1,0},{2,1},{3,2},{4,7},{5,4},{6,5},{7,6},{8,11},{9,8},{10,9... | collective-permute-start | bytes 98312 | tf_op jit(solution)/shard_map/ppermute | solution.py:732
  10.7 1.1 %copy-start.9 = (bf16[64,256]{1,0:T(8,128)(2,1)}, bf16[64,256]{1,0:T(8,128)(2,1)S(1)}, u32[]{:S(2)}) copy-start(bf16[64,256]{1,0:T(8,128)(2,1)S(1)} %collective-permute-done.3.rest_2_) | copy-start | bytes 98308
  11.7 0.6 copy-start.10
  11.7 0.6 copy-start.11
  11.7 0.7 %copy-start.7 = (bf16[608,256]{1,0:T(8,128)(2,1)}, bf16[608,256]{1,0:T(8,128)(2,1)S(1)}, u32[]{:S(2)}) copy-start(bf16[608,256]{1,0:T(8,128)(2,1)S(1)} %collective-permute-done.1.packed) | copy-start | bytes 933892
  16.4 24.2 %collective-permute-start.5 = (bf16[1056,256]{1,0:T(8,128)(2,1)S(1)}, bf16[1056,256]{1,0:T(8,128)(2,1)S(1)}, u32[]{:S(2)}, u32[]{:S(2)}) collective-permute-start(bf16[1056,256]{1,0:T(8,128)(2,1)S(1)} %copy-done), channel_id=1, source_target_pairs={{0,1},{1,0},{2,3},{3,2},{4,5},{5,4},{6,7},{7,6},{8,9},{9,8},{10,11... | collective-permute-start | bytes 1622024 | tf_op jit(solution)/shard_map/ppermute | solution.py:728
  16.6 1.3 %copy-start.6 = (bf16[64,64,256]{2,1,0:T(8,128)(2,1)}, bf16[64,64,256]{2,1,0:T(8,128)(2,1)S(1)}, u32[]{:S(2)}) copy-start(bf16[64,64,256]{2,1,0:T(8,128)(2,1)S(1)} %collective-permute-done.other_pairs) | copy-start | bytes 6291460
  27.6 13.0 %copy-start.1 = (bf16[256,1024]{1,0:T(8,128)(2,1)S(1)}, bf16[256,1024]{1,0:T(8,128)(2,1)}, u32[]{:S(2)}) copy-start(bf16[256,1024]{1,0:T(8,128)(2,1)} %gate_weight.1) | copy-start | bytes 1572868
  27.6 13.0 %copy-start.2 = (bf16[256,1024]{1,0:T(8,128)(2,1)S(1)}, bf16[256,1024]{1,0:T(8,128)(2,1)}, u32[]{:S(2)}) copy-start(bf16[256,1024]{1,0:T(8,128)(2,1)} %up_weight.1) | copy-start | bytes 1572868
  27.6 13.0 %copy-start.3 = (bf16[1024,256]{1,0:T(8,128)(2,1)S(1)}, bf16[1024,256]{1,0:T(8,128)(2,1)}, u32[]{:S(2)}) copy-start(bf16[1024,256]{1,0:T(8,128)(2,1)} %down_weight.1) | copy-start | bytes 1572868
  27.6 13.0 %copy-start.4 = (f32[256]{0:T(256)S(1)}, f32[256]{0:T(256)}, u32[]{:S(2)}) copy-start(f32[256]{0:T(256)} %param.41) | copy-start | bytes 3076
  27.6 13.0 %copy-start.5 = (f32[256]{0:T(256)S(1)}, f32[256]{0:T(256)}, u32[]{:S(2)}) copy-start(f32[256]{0:T(256)} %param.42) | copy-start | bytes 3076
  28.8 11.8 %collective-permute-start.8 = (bf16[18,16,128]{2,1,0:T(8,128)(2,1)S(1)}, bf16[18,16,128]{2,1,0:T(8,128)(2,1)S(1)}, u32[]{:S(2)}, u32[]{:S(2)}) collective-permute-start(bf16[18,16,128]{2,1,0:T(8,128)(2,1)S(1)} %get-tuple-element.40), channel_id=1, source_target_pairs={{0,12},{4,0},{8,4},{12,8},{1,13},{5,1},{9,5},{13,9},{2,14},{6,2},{... | collective-permute-start | bytes 221192 | tf_op jit(solution)/shard_map/ppermute | solution.py:766
  32.9 7.7 %collective-permute-start.7 = (bf16[18,16,128]{2,1,0:T(8,128)(2,1)S(1)}, bf16[18,16,128]{2,1,0:T(8,128)(2,1)S(1)}, u32[]{:S(2)}, u32[]{:S(2)}) collective-permute-start(bf16[18,16,128]{2,1,0:T(8,128)(2,1)S(1)} %get-tuple-element.41), channel_id=1, source_target_pairs={{0,8},{4,12},{8,0},{12,4},{1,9},{5,13},{9,1},{13,5},{2,10},{6,14},... | collective-permute-start | bytes 221192 | tf_op jit(solution)/shard_map/ppermute | solution.py:766
  32.9 7.7 %collective-permute-start.6 = (bf16[18,16,128]{2,1,0:T(8,128)(2,1)S(1)}, bf16[18,16,128]{2,1,0:T(8,128)(2,1)S(1)}, u32[]{:S(2)}, u32[]{:S(2)}) collective-permute-start(bf16[18,16,128]{2,1,0:T(8,128)(2,1)S(1)} %get-tuple-element.42), channel_id=1, source_target_pairs={{0,4},{4,8},{8,12},{12,0},{1,5},{5,9},{9,13},{13,1},{2,6},{6,10},{... | collective-permute-start | bytes 221192 | tf_op jit(solution)/shard_map/ppermute | solution.py:766
  42.5 5.5 %collective-permute-start.11 = (bf16[16,256]{1,0:T(8,128)(2,1)S(1)}, bf16[16,256]{1,0:T(8,128)(2,1)S(1)}, u32[]{:S(2)}, u32[]{:S(2)}) collective-permute-start(bf16[16,256]{1,0:T(8,128)(2,1)S(1)} %nodes.1), channel_id=1, source_target_pairs={{0,4},{4,8},{8,12},{12,0},{1,5},{5,9},{9,13},{13,1},{2,6},{6,10},{... | collective-permute-start | bytes 24584 | tf_op jit(solution)/shard_map/ppermute | solution.py:790
  45.0 4.6 %collective-permute-start.10 = (bf16[16,256]{1,0:T(8,128)(2,1)S(1)}, bf16[16,256]{1,0:T(8,128)(2,1)S(1)}, u32[]{:S(2)}, u32[]{:S(2)}) collective-permute-start(bf16[16,256]{1,0:T(8,128)(2,1)S(1)} %nodes.1), channel_id=1, source_target_pairs={{0,8},{4,12},{8,0},{12,4},{1,9},{5,13},{9,1},{13,5},{2,10},{6,14},... | collective-permute-start | bytes 24584 | tf_op jit(solution)/shard_map/ppermute | solution.py:790
  45.9 3.7 %collective-permute-start.9 = (bf16[16,256]{1,0:T(8,128)(2,1)S(1)}, bf16[16,256]{1,0:T(8,128)(2,1)S(1)}, u32[]{:S(2)}, u32[]{:S(2)}) collective-permute-start(bf16[16,256]{1,0:T(8,128)(2,1)S(1)} %nodes.1), channel_id=1, source_target_pairs={{0,12},{4,0},{8,4},{12,8},{1,13},{5,1},{9,5},{13,9},{2,14},{6,2},{... | collective-permute-start | bytes 24584 | tf_op jit(solution)/shard_map/ppermute | solution.py:790
  59.3 4.5 %collective-permute-start.12 = (bf16[65,64,256]{2,1,0:T(8,128)(2,1)}, bf16[65,64,256]{2,1,0:T(8,128)(2,1)}, u32[]{:S(2)}, u32[]{:S(2)}) collective-permute-start(bf16[65,64,256]{2,1,0:T(8,128)(2,1)} %get-tuple-element.35), channel_id=1, source_target_pairs={{0,1},{1,0},{2,3},{3,2},{4,5},{5,4},{6,7},{7,6},{8,9},{9,8},{10,11... | collective-permute-start | bytes 6389768 | tf_op jit(solution)/shard_map/ppermute | solution.py:728

commit v3 on v2

--- a/solution.py
+++ b/solution.py
@@ -18,6 +18,9 @@
 ROWS = 16
 VMEM_MIB = 60
 CHUNKS = 4
+ATTEND_ROWS = 32
+TURN_ROWS = 32
+EDGE_ROWS = 16
 
 linear_scale = math.sqrt(1.0 / 3.0)
 masked_score = -1000000000.0
@@ -82,36 +85,7 @@
     return -(-count // 16) * 16
 
 
-def through(moves, buffer, arrivals, departures):
-    starts, at = [], 0
-    for step, (source, target) in enumerate(moves):
-        end = at + source.shape[0]
-        load = pltpu.make_async_copy(source, buffer.at[at:end], arrivals.at[step])
-        load.start()
-        starts.append((load, pltpu.make_async_copy(buffer.at[at:end], target, departures.at[step])))
-        at = end
-    return starts
-
-
-def pass_on(starts):
-    for load, store in starts:
-        load.wait()
-        store.start()
-    for _, store in starts:
-        store.wait()
-
-
-def prepare_kernel(
-    point_gain, chain_gain, key_weight, query_weight, bias_weight, pairs, packed, sliced, last, buffer, arrivals, departures
-):
-    half = sliced.shape[1]
-    begin = pl.multiple_of((1 - lax.axis_index("sub")) * half, half)
-    span = sliced.shape[0] // CHUNKS
-    moves = [
-        (pairs.at[at * span : (at + 1) * span, pl.ds(begin, half), :], sliced.at[at * span : (at + 1) * span])
-        for at in range(CHUNKS)
-    ]
-    starts = through(moves, buffer, arrivals, departures)
+def pack_kernel(point_gain, chain_gain, key_weight, query_weight, bias_weight, nodes, packed, last):
     heads, channels = bias_weight.shape
     at = up16(key_weight.shape[0])
     end = at + up16(query_weight.shape[0])
@@ -131,29 +105,57 @@
     last[0:heads, 0:channels] = bias_weight[...].astype(f32)
     last[:, channels : channels + 128] = pieces
     packed[end : end + 16] = last[...].astype(bf16)
-    pass_on(starts)
-
-
-def prepare(point_gain, chain_gain, key_weight, query_weight, bias_weight, pairs, half):
-    operands = [key_weight, query_weight, bias_weight]
-    total = up16(key_weight.shape[0]) + up16(query_weight.shape[0]) + 16
+    packed[end + 16 :] = nodes[...]
+
+
+def pack(point_gain, chain_gain, key_weight, query_weight, bias_weight, nodes):
+    operands = [key_weight, query_weight, bias_weight, nodes]
+    total = up16(key_weight.shape[0]) + up16(query_weight.shape[0]) + 16 + nodes.shape[0]
+    return pl.pallas_call(
+        pack_kernel,
+        in_specs=[SMEM] * 2 + [whole(a) for a in operands],
+        out_shape=jax.ShapeDtypeStruct((total, key_weight.shape[1]), bf16),
+        scratch_shapes=[pltpu.VMEM((16, key_weight.shape[1]), f32)],
+        compiler_params=params(63),
+        cost_estimate=cost(2),
+        name="pack",
+    )(point_gain, chain_gain, *operands)
+
+
+def slice_kernel(pairs, sliced, buffer, arrivals, departures):
+    half = sliced.shape[1]
+    begin = pl.multiple_of((1 - lax.axis_index("sub")) * half, half)
+    span = sliced.shape[0] // CHUNKS
+    copies = []
+    for chunk in range(CHUNKS):
+        at = slice(chunk * span, (chunk + 1) * span)
+        load = pltpu.make_async_copy(pairs.at[at, pl.ds(begin, half), :], buffer.at[at], arrivals.at[chunk])
+        load.start()
+        copies.append((load, pltpu.make_async_copy(buffer.at[at], sliced.at[at], departures.at[chunk])))
+    for load, store in copies:
+        load.wait()
+        store.start()
+    for _, store in copies:
+        store.wait()
+
+
+def slice_pairs(pairs, half):
+    shape = (pairs.shape[0], half, pairs.shape[2])
     hbm = pl.BlockSpec(memory_space=pl.ANY)
-    shape = jax.ShapeDtypeStruct((total, key_weight.shape[1]), bf16)
     return pl.pallas_call(
-        prepare_kernel,
-        in_specs=[SMEM] * 2 + [whole(a) for a in operands] + [hbm],
-        out_shape=(shape, jax.ShapeDtypeStruct((pairs.shape[0], half, pairs.shape[2]), bf16)),
-        out_specs=(whole(shape), hbm),
+        slice_kernel,
+        in_specs=[hbm],
+        out_specs=hbm,
+        out_shape=jax.ShapeDtypeStruct(shape, bf16),
         scratch_shapes=[
-            pltpu.VMEM((16, key_weight.shape[1]), f32),
-            pltpu.VMEM((pairs.shape[0], half, pairs.shape[2]), bf16),
+            pltpu.VMEM(shape, bf16),
             pltpu.SemaphoreType.DMA((CHUNKS,)),
             pltpu.SemaphoreType.DMA((CHUNKS,)),
         ],
-        compiler_params=params(VMEM_MIB),
-        cost_estimate=cost(2),
-        name="prepare",
-    )(point_gain, chain_gain, *operands, pairs)
+        compiler_params=params(63),
+        cost_estimate=cost(3),
+        name="slice_pairs",
+    )(pairs)
 
 
 def project_kernel(
@@ -190,9 +192,11 @@
     gains = last[:, bias_own.shape[1] :]
     point_other = gains[:, 0:1] + gains[:, 1:2] + gains[:, 2:3]
     chain_other = gains[:, 3:4] + gains[:, 4:5] + gains[:, 5:6]
-    for step in range(blocks):
-        source = lax.rem(mine - step + blocks, blocks)
-        keys[pl.ds(pl.multiple_of(source * share, share), share), :] = key_blocks[step][...]
+    rows = (blocks + 1) // 2
+    arrived = [key_blocks[0][...], packed[last_at + 16 :], *(block[...] for block in key_blocks[1:])]
+    for step, block in enumerate(arrived):
+        source = 2 * lax.rem(mine - step // 2 + rows, rows) + (1 - sub if step % 2 else sub)
+        keys[pl.ds(pl.multiple_of(source * share, share), share), :] = block
     nodes = keys[...]
     key_proj[0] = dot_nt(key_weight_own[...], nodes)
     key_proj[1] = dot_nt(packed[: local_heads * KCOLS], nodes)
@@ -309,29 +313,26 @@
             pltpu.VMEM((heads, SLOT, query_count), f32),
             pltpu.VMEM((heads, query_count, SLOT), f32),
         ],
-        compiler_params=params(VMEM_MIB),
-        cost_estimate=cost(4),
+        compiler_params=params(63),
+        cost_estimate=cost(12),
         name="project",
     )(place, *gains, *operands)
 
 
 def attend_kernel(
+    targets,
     place,
-    own_pairs,
-    other_pairs,
     base_scores,
-    mask,
     values,
     bias_spread,
     frames,
-    part,
-    weight_high,
-    weight_low,
-    peaks,
-    sums,
-    gather_own,
-    gather_other,
+    mask,
+    own_pairs,
+    other_pairs,
+    *rest,
 ):
+    results = rest[:targets]
+    part, weight_high, weight_low, peaks, sums, gather_own, gather_other = rest[targets:]
     step = pl.program_id(0)
     sub = place[0]
     heads, _, keys = base_scores.shape
@@ -346,27 +347,31 @@
         gather_own[...] = (target == source + sub * channels).astype(f32).astype(bf16)
         gather_other[...] = (target == source + (1 - sub) * channels).astype(f32).astype(bf16)
 
-    own = own_pairs[...].reshape(spread, keys)
-    other = other_pairs[...].reshape(spread, keys)
-    bias = dot(bias_spread[:, :spread], own) + dot(bias_spread[:, spread:], other)
-    score = base_scores[...] + linear_scale * bias.reshape(heads, ROWS, keys)
-    score = jnp.where(mask[...][None] == 1, score, masked_score)
-    peak = jnp.max(score, axis=2, keepdims=True)
-    weight = jnp.exp(score - peak)
-    total = jnp.sum(weight, axis=2, keepdims=True)
-    high = weight.astype(bf16)
-    begin = pl.multiple_of(step * ROWS, ROWS)
-    weight_high[:, pl.ds(begin, ROWS), :] = high
-    weight_low[:, pl.ds(begin, ROWS), :] = (weight - high.astype(f32)).astype(bf16)
-    peaks[:, pl.ds(begin, ROWS), :] = jnp.broadcast_to(peak, (heads, ROWS, lanes))
-    sums[:, pl.ds(begin, ROWS), :] = jnp.broadcast_to(total, (heads, ROWS, lanes))
-    flat = high.reshape(heads * ROWS, keys)
-    scale = (1.0 / total).reshape(heads * ROWS, 1)
+    rows = own_pairs.shape[1]
     diagonal = iota((heads * ROWS, spread), 0) % ROWS == iota((heads * ROWS, spread), 1) % ROWS
-    own_part = jnp.where(diagonal, dot_nt(flat, own) * scale, 0.0).astype(bf16)
-    other_part = jnp.where(diagonal, dot_nt(flat, other) * scale, 0.0).astype(bf16)
-    pairs = dot(own_part, gather_own[...]) + dot(other_part, gather_other[...])
-    part[0:heads, pl.ds(begin, ROWS), :] = pairs.reshape(heads, ROWS, lanes).astype(bf16)
+    blocks = []
+    for begin in range(0, rows, ROWS):
+        span = slice(begin, begin + ROWS)
+        own = own_pairs[:, span, :].reshape(spread, keys)
+        other = other_pairs[:, span, :].reshape(spread, keys)
+        bias = dot(bias_spread[:, :spread], own) + dot(bias_spread[:, spread:], other)
+        score = base_scores[:, span, :] + linear_scale * bias.reshape(heads, ROWS, keys)
+        score = jnp.where(mask[span, :][None] == 1, score, masked_score)
+        peak = jnp.max(score, axis=2, keepdims=True)
+        weight = jnp.exp(score - peak)
+        total = jnp.sum(weight, axis=2, keepdims=True)
+        high = weight.astype(bf16)
+        at = pl.ds(pl.multiple_of(step * rows + begin, ROWS), ROWS)
+        weight_high[:, at, :] = high
+        weight_low[:, at, :] = (weight - high.astype(f32)).astype(bf16)
+        peaks[:, at, :] = jnp.broadcast_to(peak, (heads, ROWS, lanes))
+        sums[:, at, :] = jnp.broadcast_to(total, (heads, ROWS, lanes))
+        blocks.append((at, own, other, high.reshape(heads * ROWS, keys), (1.0 / total).reshape(heads * ROWS, 1)))
+    for at, own, other, flat, scale in blocks:
+        own_part = jnp.where(diagonal, dot_nt(flat, own) * scale, 0.0).astype(bf16)
+        other_part = jnp.where(diagonal, dot_nt(flat, other) * scale, 0.0).astype(bf16)
+        pairs = dot(own_part, gather_own[...]) + dot(other_part, gather_other[...])
+        part[0:heads, at, :] = pairs.reshape(heads, ROWS, lanes).astype(bf16)
 
     @pl.when(step == pl.num_programs(0) - 1)
     def _():
@@ -410,29 +415,36 @@
                     value = value - piece
                     at += 1
             part[heads + pair] = jnp.where(slot < at, result, 0.0).astype(bf16)
-
-
-def attend(place, own_pairs, other_pairs, base_scores, mask, values, bias_spread, frames):
+        share = half // targets
+        for target in range(targets):
+            at = jnp.bitwise_xor(place[2], target) * share if targets > 1 else 0
+            results[target][...] = part[:, pl.ds(pl.multiple_of(at, share) if targets > 1 else 0, share), :]
+
+
+def attend(place, own_pairs, other_pairs, base_scores, mask, values, bias_spread, frames, targets):
     heads, half, keys = base_scores.shape
     channels = own_pairs.shape[0]
-    steps = half // ROWS
-    pair_block = pl.BlockSpec((channels, ROWS, keys), lambda g, p: (0, p[0] * steps + g, 0))
+    rows = math.gcd(half, ATTEND_ROWS)
+    steps = half // rows
+    pair_block = pl.BlockSpec((channels, rows, keys), lambda g, p: (0, p[0] * steps + g, 0))
+    slots = heads + heads // 2
     return pl.pallas_call(
-        attend_kernel,
+        functools.partial(attend_kernel, targets),
         grid_spec=pltpu.PrefetchScalarGridSpec(
             num_scalar_prefetch=1,
             grid=(steps,),
             in_specs=[
-                pair_block,
-                pl.BlockSpec((channels, ROWS, keys), lambda g, p: (0, g, 0)),
-                pl.BlockSpec((heads, ROWS, keys), lambda g, p: (0, g, 0)),
-                pl.BlockSpec((ROWS, keys), lambda g, p: (p[0] * steps + g, 0)),
+                pl.BlockSpec((heads, rows, keys), lambda g, p: (0, g, 0)),
                 whole(values),
                 whole(bias_spread),
                 pl.BlockSpec((half, frames.shape[1]), lambda g, p: (p[0], 0)),
+                pl.BlockSpec((rows, keys), lambda g, p: (p[0] * steps + g, 0)),
+                pair_block,
+                pl.BlockSpec((channels, rows, keys), lambda g, p: (0, g, 0)),
             ],
-            out_specs=pl.BlockSpec((heads + heads // 2, half, 2 * channels), lambda g, p: (0, 0, 0)),
+            out_specs=[pl.BlockSpec((slots, half // targets, 2 * channels), lambda g, p: (0, 0, 0))] * targets,
             scratch_shapes=[
+                pltpu.VMEM((slots, half, 2 * channels), bf16),
                 pltpu.VMEM((heads, half, keys), bf16),
                 pltpu.VMEM((heads, half, keys), bf16),
                 pltpu.VMEM((heads, half, 2 * channels), f32),
@@ -441,11 +453,11 @@
                 pltpu.VMEM((channels * ROWS, 2 * channels), bf16),
             ],
         ),
-        out_shape=jax.ShapeDtypeStruct((heads + heads // 2, half, 2 * channels), bf16),
-        compiler_params=params(VMEM_MIB),
+        out_shape=[jax.ShapeDtypeStruct((slots, half // targets, 2 * channels), bf16)] * targets,
+        compiler_params=params(63),
         cost_estimate=cost(9),
         name="attend",
-    )(place, own_pairs, other_pairs, base_scores, mask, values, bias_spread, frames)
+    )(place, base_scores, values, bias_spread, frames, mask, own_pairs, other_pairs)
 
 
 def norm(values, gain):
@@ -456,6 +468,7 @@
 
 def node_kernel(
     count,
+    place,
     nodes,
     out_own,
     out_other,
@@ -512,23 +525,24 @@
             mixed = mixed + factor * part[head].astype(f32)
         projected = projected + dot(mixed.astype(bf16), weight[begin + FEATURES : begin + FEATURES + lanes])
         projected = projected + dot(merged[span, lane : lane + FEATURES], weight[begin : begin + FEATURES])
-    first_nodes = norm(nodes[...].astype(f32) + projected, first_gain[...])
+    own = nodes[pl.ds(pl.multiple_of(place[0], ROWS), rows), :]
+    first_nodes = norm(own.astype(f32) + projected, first_gain[...])
     first_rounded = first_nodes.astype(bf16)
     gate = dot(first_rounded, gate_weight[...])
     hidden = (gate / (1.0 + jnp.exp(-gate)) * dot(first_rounded, up_weight[...])).astype(bf16)
     result[...] = norm(first_nodes + dot(hidden, down_weight[...]), second_gain[...]).astype(bf16)
 
 
-def update_nodes(parts, nodes, out_own, out_other, first_gain, second_gain, gate_weight, up_weight, down_weight):
+def update_nodes(place, parts, nodes, out_own, out_other, first_gain, second_gain, gate_weight, up_weight, down_weight):
     operands = [nodes, out_own, out_other, first_gain, second_gain, gate_weight, up_weight, down_weight, *parts]
     return pl.pallas_call(
         functools.partial(node_kernel, len(parts)),
-        in_specs=[whole(a) for a in operands],
-        out_shape=jax.ShapeDtypeStruct(nodes.shape, bf16),
+        in_specs=[SMEM] + [whole(a) for a in operands],
+        out_shape=jax.ShapeDtypeStruct((parts[0].shape[1], nodes.shape[1]), bf16),
         compiler_params=params(16),
         cost_estimate=cost(2),
         name="nodes",
-    )(*operands)
+    )(place, *operands)
 
 
 def turn_kernel(place, own_pairs, other_pairs, in_weight, out_weight, result, left, out_left):
@@ -549,23 +563,24 @@
     result[:, channels:, :] = jnp.swapaxes(other_pairs[...], 0, 1)
 
 
-def turn_pairs(place, own_pairs, other_pairs, in_weight, out_weight):
-    channels, half, keys = other_pairs.shape
+def turn_pairs(place, own_pairs, other_pairs, in_weight, out_weight, half):
+    channels, _, keys = other_pairs.shape
     both, hidden = in_weight.shape
-    steps = half // ROWS
+    rows = math.gcd(half, TURN_ROWS)
+    steps = half // rows
     return pl.pallas_call(
         turn_kernel,
         grid_spec=pltpu.PrefetchScalarGridSpec(
             num_scalar_prefetch=1,
             grid=(steps,),
             in_specs=[
-                pl.BlockSpec((channels, ROWS, keys), lambda g, p: (0, p[0] * steps + g, 0)),
-                pl.BlockSpec((channels, ROWS, keys), lambda g, p: (0, g, 0)),
+                pl.BlockSpec((channels, rows, keys), lambda g, p: (0, p[0] * steps + g, 0)),
+                pl.BlockSpec((channels, rows, keys), lambda g, p: (0, g, 0)),
                 whole(in_weight),
                 whole(out_weight),
             ],
             out_specs=(
-                pl.BlockSpec((ROWS, both, keys), lambda g, p: (g, 0, 0)),
+                pl.BlockSpec((rows, both, keys), lambda g, p: (g, 0, 0)),
                 pl.BlockSpec((hidden, both), lambda g, p: (0, 0)),
                 pl.BlockSpec((both, hidden), lambda g, p: (0, 0)),
             ),
@@ -575,70 +590,83 @@
             jax.ShapeDtypeStruct((hidden, both), bf16),
             jax.ShapeDtypeStruct((both, hidden), bf16),
         ),
-        compiler_params=params(VMEM_MIB),
+        compiler_params=params(16),
         cost_estimate=cost(4),
         name="turn_pairs",
     )(place, own_pairs, other_pairs, in_weight, out_weight)
 
 
-def edge_kernel(
-    place, turned, nodes, edge_keys, in_left, out_left, query_weight, kept, sent, new_nodes, left, picks, hidden, fresh
-):
-    rows, both, keys = turned.shape
+def edge_kernel(count, place, turned, *rest):
+    ring = rest[:count]
+    edge_keys, in_left, out_left, query_weight, kept, sent, new_nodes, nodes, left, picks, hidden, fresh = rest[count:]
+    step, rows = pl.program_id(0), ROWS
+    _, both, keys = turned.shape
     channels = both // 2
 
     @pl.when(pl.program_id(0) == 0)
     def _():
-        left[:, 0:both] = in_left[...]
+        at = 0
+        for source in ring:
+            for begin in range(0, source.shape[0], rows):
+                nodes[at] = source[begin : begin + rows]
+                at += 1
+        for span in range(left.shape[0]):
+            left[span, :, 0:both] = in_left[...]
         chosen = iota((rows, 2 * rows, keys), 1) % rows == iota((rows, 2 * rows, keys), 0)
         picks[...] = chosen.astype(f32).astype(bf16)
 
-    queries = dot_tt(query_weight[...], nodes[0])
-    high = queries.astype(bf16)
-    left[:, both : both + rows] = high
-    left[:, both + rows :] = (queries - high.astype(f32)).astype(bf16)
-    new_nodes[...] = nodes[0]
-    for at in range(sent.shape[0] - channels):
-        sent[channels + at] = nodes[0, :, at * keys : (at + 1) * keys]
-    for row in range(rows):
-        right = jnp.concatenate([turned[row], picks[row]], axis=0)
-        hidden[row] = jnp.maximum(dot(left[...], right) + edge_keys[...], 0.0).astype(bf16)
-    for row in range(rows):
+    spans = turned.shape[0] // rows
+    for span in range(spans):
+        begin = span * rows
+        own = nodes[jnp.bitwise_xor(step * spans + span, place[1])]
+        queries = dot_tt(query_weight[...], own)
+        high = queries.astype(bf16)
+        left[span, :, both : both + rows] = high
+        left[span, :, both + rows :] = (queries - high.astype(f32)).astype(bf16)
+        new_nodes[begin : begin + rows] = own
+        for at in range(sent.shape[0] - channels):
+            sent[channels + at, begin : begin + rows] = own[:, at * keys : (at + 1) * keys]
+    for row in range(spans * rows):
+        right = jnp.concatenate([turned[row], picks[row % rows]], axis=0)
+        hidden[row] = jnp.maximum(dot(left[row // rows], right) + edge_keys[...], 0.0).astype(bf16)
+    for row in range(spans * rows):
         old = turned[row].astype(f32)
         fresh[row] = (old + dot(out_left[...], hidden[row])).astype(bf16)
     kept[...] = jnp.swapaxes(fresh[:, 0:channels, :], 0, 1)
     sent[0:channels] = jnp.swapaxes(fresh[:, channels:, :], 0, 1)
 
 
-def update_pairs(place, count, turned, nodes, edge_keys, in_left, out_left, query_weight):
+def update_pairs(place, count, turned, ring, edge_keys, in_left, out_left, query_weight):
     half, both, keys = turned.shape
     channels, hidden = both // 2, in_left.shape[0]
-    steps, _, features = nodes.shape
+    rows, features = math.gcd(half, EDGE_ROWS), ring[0].shape[1]
+    steps = half // rows
     assert features % keys == 0
     extra = features // keys
     return pl.pallas_call(
-        edge_kernel,
+        functools.partial(edge_kernel, len(ring)),
         grid_spec=pltpu.PrefetchScalarGridSpec(
             num_scalar_prefetch=1,
             grid=(steps,),
             in_specs=[
-                pl.BlockSpec((ROWS, both, keys), lambda g, p: (g, 0, 0)),
-                pl.BlockSpec((1, ROWS, features), lambda g, p: (lax.rem(g + p[1], steps), 0, 0)),
+                pl.BlockSpec((rows, both, keys), lambda g, p: (g, 0, 0)),
+                *[whole(a) for a in ring],
                 whole(edge_keys),
                 whole(in_left),
                 whole(out_left),
                 whole(query_weight),
             ],
             out_specs=(
-                pl.BlockSpec((channels, ROWS, keys), lambda g, p: (0, p[0] * steps + g, 0)),
-                pl.BlockSpec((channels + extra, ROWS, keys), lambda g, p: (0, g, 0)),
-                pl.BlockSpec((ROWS, features), lambda g, p: (p[0] * steps + g, 0)),
+                pl.BlockSpec((channels, rows, keys), lambda g, p: (0, p[0] * steps + g, 0)),
+                pl.BlockSpec((channels + extra, rows, keys), lambda g, p: (0, g, 0)),
+                pl.BlockSpec((rows, features), lambda g, p: (p[0] * steps + g, 0)),
             ),
             scratch_shapes=[
-                pltpu.VMEM((hidden, both + 2 * ROWS), bf16),
+                pltpu.VMEM((half // ROWS, ROWS, features), bf16),
+                pltpu.VMEM((rows // ROWS, hidden, both + 2 * ROWS), bf16),
                 pltpu.VMEM((ROWS, 2 * ROWS, keys), bf16),
-                pltpu.VMEM((ROWS, hidden, keys), bf16),
-                pltpu.VMEM((ROWS, both, keys), bf16),
+                pltpu.VMEM((rows, hidden, keys), bf16),
+                pltpu.VMEM((rows, both, keys), bf16),
             ],
         ),
         out_shape=(
@@ -646,49 +674,39 @@
             jax.ShapeDtypeStruct((channels + extra, half, keys), bf16),
             jax.ShapeDtypeStruct((count, features), bf16),
         ),
-        compiler_params=params(VMEM_MIB),
+        compiler_params=params(20),
         cost_estimate=cost(8),
         name="edges",
-    )(place, turned, nodes, edge_keys, in_left, out_left, query_weight)
-
-
-def finish_kernel(arrived, pairs_in, nodes_in, pairs, nodes, buffer, arrivals, departures):
+    )(place, turned, *ring, edge_keys, in_left, out_left, query_weight)
+
+
+def finish_kernel(arrived, pairs_in, nodes_in, pairs, nodes, sems):
     channels, half, keys = pairs.shape[0], arrived.shape[1], arrived.shape[2]
     begin = pl.multiple_of((1 - lax.axis_index("sub")) * half, half)
     rows = pl.ds(begin, half)
-    span = channels // CHUNKS
-    moves = [
-        (arrived.at[at * span : (at + 1) * span], pairs.at[at * span : (at + 1) * span, rows, :])
-        for at in range(CHUNKS)
-    ]
-    starts = through(moves, buffer, arrivals, departures)
+    copies = [pltpu.make_async_copy(arrived.at[0:channels], pairs.at[:, rows, :], sems.at[0])]
     for at in range(arrived.shape[0] - channels):
-        source = arrived.at[channels + at]
-        load = pltpu.make_async_copy(source, buffer.at[channels + at], arrivals.at[CHUNKS + at])
         target = nodes.at[rows, at * keys : (at + 1) * keys]
-        load.start()
-        starts.append((load, pltpu.make_async_copy(buffer.at[channels + at], target, departures.at[CHUNKS + at])))
-    pass_on(starts)
+        copies.append(pltpu.make_async_copy(arrived.at[channels + at], target, sems.at[1 + at]))
+    for copy in copies:
+        copy.start()
+    for copy in copies:
+        copy.wait()
 
 
 def finish(arrived, pairs, nodes):
     hbm = pl.BlockSpec(memory_space=pl.ANY)
-    copies = CHUNKS + arrived.shape[0] - pairs.shape[0]
     return pl.pallas_call(
         finish_kernel,
-        in_specs=[hbm] * 3,
+        in_specs=[whole(arrived), hbm, hbm],
         out_specs=(hbm, hbm),
         out_shape=(
             jax.ShapeDtypeStruct(pairs.shape, bf16),
             jax.ShapeDtypeStruct(nodes.shape, bf16),
         ),
-        scratch_shapes=[
-            pltpu.VMEM(arrived.shape, bf16),
-            pltpu.SemaphoreType.DMA((copies,)),
-            pltpu.SemaphoreType.DMA((copies,)),
-        ],
+        scratch_shapes=[pltpu.SemaphoreType.DMA((1 + arrived.shape[0] - pairs.shape[0],))],
         input_output_aliases={1: 0, 2: 1},
-        compiler_params=params(62),
+        compiler_params=params(8),
         cost_estimate=cost(1),
         name="finish",
     )(arrived, pairs, nodes)
@@ -727,21 +745,25 @@
     def swap(values):
         return lax.ppermute(values, "sub", [(i, (i + 1) % subs) for i in range(subs)])
 
-    group = rows * subs
+    def step(by_row, by_sub):
+        return [
+            (r * subs + c, (r + by_row) % rows * subs + (c + by_sub) % subs) for r in range(rows) for c in range(subs)
+        ]
+
     key_blocks = [node_key] + [
-        lax.ppermute(node_key, ("row", "sub"), [(i, (i + k) % group) for i in range(group)])
-        for k in range(1, group)
+        lax.ppermute(node_key, ("row", "sub"), step(r, c)) for r in range(1, rows) for c in range(subs)
     ]
     half = node_query.shape[0] // subs
     query_weight, key_weight, bias_weight = query_weight.T, key_weight.T, bias_weight.T
-    packed, late_pairs = prepare(
-        point_gain, chain_gain, key_weight, query_weight, bias_weight, pair_features, half
-    )
-    packed = swap(packed)
-    other_pairs = swap(late_pairs)
+    packed = pack(point_gain, chain_gain, key_weight, query_weight, bias_weight, node_key)
+    packed, late_pairs = lax.optimization_barrier((swap(packed), pair_features))
+    far_pairs, key_blocks = lax.optimization_barrier((slice_pairs(late_pairs, half), key_blocks))
+    other_pairs = swap(far_pairs)
+    place = jnp.stack([sub, lax.axis_index("row"), col]).astype(jnp.int32)
 
     share = half // cols
-    place = jnp.stack([sub, lax.axis_index(("row", "sub"))]).astype(jnp.int32)
+    assert cols & (cols - 1) == 0
+    spare = -share % ROWS
     base_scores, values, bias_spread, frames, edge_keys = project(
         place,
         [point_gain, chain_gain],
@@ -755,27 +777,33 @@
         key_blocks,
         half,
     )
-    part = attend(place, pair_features, other_pairs, base_scores, pair_mask, values, bias_spread, frames)
+    targets = 1 if spare else cols
+    pieces = attend(
+        place, pair_features, other_pairs, base_scores, pair_mask, values, bias_spread, frames, targets
+    )
     other_out = swap(lax.optimization_barrier((out_weight, base_scores))[0])
-
-    def piece(k):
-        return lax.dynamic_slice_in_dim(part, lax.rem(col + k, cols) * share, share, 1)
-
-    pieces = [piece(k) for k in range(cols)]
-    parts = [pieces[0]] + [
-        lax.ppermute(pieces[k], "col", [(i, (i + k) % cols) for i in range(cols)]) for k in range(1, cols)
-    ]
-    spare = -share % ROWS
-    own_nodes = lax.dynamic_slice_in_dim(node_query, sub * half + col * share, share, 0)
     if spare:
+        pieces = [
+            lax.dynamic_slice_in_dim(pieces[0], jnp.bitwise_xor(col, k) * share, share, 1) for k in range(cols)
+        ]
+    def meet(values, k):
+        return lax.ppermute(values, "col", [(i, i ^ k) for i in range(cols)])
+
+    order = range(cols - 1, 0, -1)
+    met = {k: meet(pieces[k], k) for k in order}
+    parts = [pieces[0]] + [met[k] for k in order]
+    own_nodes, begin = node_query, sub * half + col * share
+    if spare:
+        own_nodes, begin = lax.dynamic_slice_in_dim(node_query, begin, share, 0), 0 * begin
         parts = [jnp.pad(p, ((0, 0), (0, spare), (0, 0))) for p in parts]
         own_nodes = jnp.pad(own_nodes, ((0, spare), (0, 0)))
     turn_place, _ = lax.optimization_barrier((place, pieces))
     turned, in_left, out_left = turn_pairs(
-        turn_place, pair_features, other_pairs, edge_in_weight, edge_out_weight
+        turn_place, pair_features, other_pairs, edge_in_weight, edge_out_weight, half
     )
     own_nodes, turned = lax.optimization_barrier((own_nodes, turned))
     fresh_nodes = update_nodes(
+        begin.astype(jnp.int32).reshape(1),
         parts,
         own_nodes,
         out_weight,
@@ -786,19 +814,16 @@
         up_weight,
         down_weight,
     )[:share]
-    ring = [fresh_nodes] + [
-        lax.ppermute(fresh_nodes, "col", [(i, (i - k) % cols) for i in range(cols)]) for k in range(1, cols)
-    ]
-    near_nodes = jnp.concatenate(ring, axis=0)
+    met = {k: meet(fresh_nodes, k) for k in order}
+    ring = [fresh_nodes] + [met[k] for k in range(1, cols)]
+    per_share = max(share // ROWS, 1)
+    turn = col * per_share
     if spare:
-        near_nodes = jnp.roll(near_nodes, col * share, axis=0)
+        ring = [jnp.stack(ring)[jnp.bitwise_xor(jnp.arange(cols), col)].reshape(half, node_query.shape[1])]
         turn = 0 * col
-    else:
-        turn = lax.rem(cols - col, cols) * (share // ROWS)
-    near_nodes = near_nodes.reshape(half // ROWS, ROWS, near_nodes.shape[1])
     edge_place = jnp.stack([sub, turn]).astype(jnp.int32)
     kept, sent, new_nodes = update_pairs(
-        edge_place, pair_features.shape[1], turned, near_nodes, edge_keys, in_left, out_left, edge_query_weight
+        edge_place, pair_features.shape[1], turned, ring, edge_keys, in_left, out_left, edge_query_weight
     )
     updated_pairs, updated_nodes = finish(swap(sent), kept, new_nodes)
     return (updated_nodes, updated_pairs)

time: 66.8 us -> 56.5 us (0.85)
  Pallas kernels: 37.1 us -> 31.1 us
  starting transfers between devices: 15.5 us -> 12.5 us
  local copies, waits for them, and re-layouts: 3.91 us -> 2.25 us
  waiting for transfers between devices: 7.23 us -> 8.78 us
  other arithmetic: 1.75 us -> 0.67 us
    ppermute x9 -> x8, starting transfers between devices: 14.7 us -> 11.5 us  [the longest x6 8.86 us: meet(): return lax.ppermute(values, 'col', [(i, i ^ k) for i in range(cols)])]
    pallas_call x5 -> x6, Pallas kernels: 27.2 us -> 24.1 us  [the longest x1 8.2 us: attend(): pl.pallas_call(functools.partial(attend_kernel, targets), grid_spec=pltpu...]
    pallas_call x1, Pallas kernels: 5.97 us -> 3.14 us  [turn_pairs(): pl.pallas_call(turn_kernel, grid_spec=pltpu.PrefetchScalarGridSpec(num_sc...]
    ppermute x9 -> x8, waiting for transfers between devices: 2.68 us -> 4.57 us  [the longest x6 3.74 us: meet(): return lax.ppermute(values, 'col', [(i, i ^ k) for i in range(cols)])]
    dynamic_slice x2 -> x0, local copies, waits for them, and re-layouts: 1.84 us -> none  [the longest x1 1.14 us: piece(): lax.dynamic_slice_in_dim(part, lax.rem(col + k, cols) * share, share, 1)]
    unnamed x24 -> x34, local copies, waits for them, and re-layouts: 2.07 us -> 2.25 us
  transfers between devices with their start and end apart: 13 -> 12, of which waited for: 4 -> 5; matrix products, arithmetic and copies ran while one was open for 5% -> 1% of each run, Pallas kernels for 30% -> 32%
where the time goes in v3:
time: 56.5 us; the launch traced here: 56.1 us
  Pallas kernels  31.1 us (55%)
  starting transfers between devices  12.5 us (22%)
  waiting for transfers between devices  8.78 us (16%)
  local copies, waits for them, and re-layouts  2.25 us (4%)
  between operations  0.81 us (1%)
  other arithmetic  0.67 us (1%)
    ppermute x6, starting transfers between devices, meet(): return lax.ppermute(values, 'col', [(i, i ^ k) for i in range(cols)])  8.86 us
    pallas_call x1, Pallas kernels, attend(): pl.pallas_call(functools.partial(attend_kernel, targets), grid_spec=pltpu...  8.2 us
    pallas_call x1, Pallas kernels, update_pairs(): pl.pallas_call(functools.partial(edge_kernel, len(ring)), grid_spec=pltpu...  7.33 us
    ppermute x4, waiting for transfers between devices, swap(): lax.ppermute(values, 'sub', [(i, (i + 1) % subs) for i in range(subs)])  4.21 us
    pallas_call x1, Pallas kernels, project(): pl.pallas_call(functools.partial(project_kernel, len(key_blocks)), in_spe...  3.92 us
    ppermute x6, waiting for transfers between devices, meet(): return lax.ppermute(values, 'col', [(i, i ^ k) for i in range(cols)])  3.74 us
    pallas_call x1, Pallas kernels, turn_pairs(): pl.pallas_call(turn_kernel, grid_spec=pltpu.PrefetchScalarGridSpec(num_sc...  3.14 us
    pallas_call x1, Pallas kernels, update_nodes(): pl.pallas_call(functools.partial(node_kernel, len(parts)), in_specs=[SMEM...  2.84 us
  transfers between devices with their start and end apart: 12, of which 5 were waited for; matrix products, arithmetic and copies ran while one was open for 1% of the time, Pallas kernels for 32%

profile of v3, /device:TPU:0, one launch (start us, length us, event | category | flops | bytes accessed | tf_op | source)
XLA Modules:
  0.0 56.1 jit_solution(4183841195522095904)
XLA Ops:
  0.6 0.0 copy-start.1
  0.6 1.8 %pack.1 = bf16[672,256]{1,0:T(8,128)(2,1)} custom-call(f32[6]{0:T(128)} %point_own.1, f32[6]{0:T(128)} %chain_own.1, bf16[408,256]{1,0:T(8,128)(2,1)} %bitcast.13, bf16[168,256]{1,0:T(8,128)(2,1)} %bitcast.15, bf16[6,128]{1,0:T(8,128)(2,1)} %bitcast.17, bf16[64,256]{1,0:T(8,128)(2,1)} %rest_0_), custom_call_target="tpu_custom_call" | custom-call | bytes 6000000 | tf_op jit(solution)/shard_map/pack/pallas_call | solution.py:114
  2.4 0.5 collective-permute-start
  2.9 2.5 %collective-permute-start.1 = (bf16[64,256]{1,0:T(8,128)(2,1)}, bf16[64,256]{1,0:T(8,128)(2,1)S(1)}, u32[]{:S(2)}, u32[]{:S(2)}) collective-permute-start(bf16[64,256]{1,0:T(8,128)(2,1)} %rest_0_), channel_id=1, source_target_pairs={{0,2},{1,3},{2,0},{3,1},{4,6},{5,7},{6,4},{7,5},{8,10},{9,11},{10,... | collective-permute-start | bytes 98312 | tf_op jit(solution)/shard_map/ppermute | solution.py:754
  5.4 0.1 collective-permute-start.2
  5.5 0.0 collective-permute-done.packed
  5.5 2.5 %slice_pairs.1 = bf16[64,64,256]{2,1,0:T(8,128)(2,1)} custom-call(bf16[64,128,256]{2,1,0:T(8,128)(2,1)} %own_pairs.3), custom_call_target="tpu_custom_call" | custom-call | bytes 9000000 | tf_op jit(solution)/shard_map/slice_pairs/pallas_call | solution.py:145
  8.1 0.0 collective-permute-done.1.rest_1_
  8.1 0.0 copy-start.15
  8.1 0.8 %collective-permute-done.2.rest_2_ = bf16[64,256]{1,0:T(8,128)(2,1)S(1)} collective-permute-done((bf16[64,256]{1,0:T(8,128)(2,1)}, bf16[64,256]{1,0:T(8,128)(2,1)S(1)}, u32[]{:S(2)}, u32[]{:S(2)}) %collective-permute-start.2) | collective-permute-done | bytes 32800 | tf_op jit(solution)/shard_map/ppermute | solution.py:754
  8.9 0.2 collective-permute-start.3
  9.2 0.6 %pad_add_fusion.1.place = s32[3]{0:T(128)} fusion(s32[1]{0:T(128)} %bitcast.1, s32[1]{0:T(128)} %bitcast.2, s32[1]{0:T(128)} %bitcast), kind=kLoop, calls=%fused_computation.1 | loop fusion | flops 6 | bytes 24 | tf_op jit(solution)/shard_map/stack | solution.py:762
  9.8 0.0 copy-done.14
  9.8 0.0 copy-done.15
  9.8 0.0 copy-done.16
  9.8 3.9 %project.1 = (f32[12,64,256]{2,1,0:T(8,128)}, bf16[12,64,256]{2,1,0:T(8,128)(2,1)}, bf16[192,2048]{1,0:T(8,128)(2,1)}, f32[128,16]{1,0:T(8,128)}, f32[256,256]{1,0:T(8,128)}) custom-call(s32[3]{0:T(128)} %pad_add_fusion.1.place, f32[6]{0:T(128)} %point_own.1, f32[6]{0:T(128)} %chain_own.1, bf16[128,256]{1,0:T(8,128)(2,1)} %nodes.4, f32[3,128]{1,0:T(4,128)} %query_angles.1, ...), custom_call_target="tpu_custom_call" | custom-call | bytes 36000000 | tf_op jit(solution)/shard_map/project/pallas_call | solution.py:298
  13.7 0.0 copy-done.1
  13.7 0.3 collective-permute-start.4
  14.1 0.0 collective-permute-done.3.other_pairs
  14.1 0.0 copy-start.6
  14.1 8.2 %attend.1 = (bf16[18,16,128]{2,1,0:T(8,128)(2,1)}, bf16[18,16,128]{2,1,0:T(8,128)(2,1)}, bf16[18,16,128]{2,1,0:T(8,128)(2,1)}, bf16[18,16,128]{2,1,0:T(8,128)(2,1)}) custom-call(s32[3]{0:T(128)} %pad_add_fusion.1.place, f32[12,64,256]{2,1,0:T(8,128)} %get-tuple-element.34.base_scores, bf16[12,64,256]{2,1,0:T(8,128)(2,1)} %get-tuple-element.35.values, ...), custom_call_target="tpu_custom_call" | custom-call | bytes 27000000 | tf_op jit(solution)/shard_map/attend/pallas_call | solution.py:431
  22.3 1.6 %collective-permute-start.7 = (bf16[18,16,128]{2,1,0:T(8,128)(2,1)}, bf16[18,16,128]{2,1,0:T(8,128)(2,1)S(1)}, u32[]{:S(2)}, u32[]{:S(2)}) collective-permute-start(bf16[18,16,128]{2,1,0:T(8,128)(2,1)} %get-tuple-element.40), channel_id=1, source_target_pairs={{0,4},{4,0},{8,12},{12,8},{1,5},{5,1},{9,13},{13,9},{2,6},{6,2},{1... | collective-permute-start | bytes 221192 | tf_op jit(solution)/shard_map/ppermute | solution.py:790
  23.9 2.6 %collective-permute-start.6 = (bf16[18,16,128]{2,1,0:T(8,128)(2,1)}, bf16[18,16,128]{2,1,0:T(8,128)(2,1)S(1)}, u32[]{:S(2)}, u32[]{:S(2)}) collective-permute-start(bf16[18,16,128]{2,1,0:T(8,128)(2,1)} %get-tuple-element.41), channel_id=1, source_target_pairs={{0,8},{4,12},{8,0},{12,4},{1,9},{5,13},{9,1},{13,5},{2,10},{6,14},... | collective-permute-start | bytes 221192 | tf_op jit(solution)/shard_map/ppermute | solution.py:790
  26.5 0.2 collective-permute-start.5
  26.7 0.0 copy-done.9
  26.8 0.0 copy-done.10
  26.8 0.0 copy-done.11
  26.8 2.2 %copy-done = bf16[64,128,256]{2,1,0:T(8,128)(2,1)S(1)} copy-done((bf16[64,128,256]{2,1,0:T(8,128)(2,1)S(1)}, bf16[64,128,256]{2,1,0:T(8,128)(2,1)}, u32[]{:S(2)}) %copy-start) | copy-done | bytes 4194328
  29.0 0.0 copy-start.7
  29.0 3.1 %turn_pairs.1 = (bf16[64,128,256]{2,1,0:T(8,128)(2,1)S(1)}, bf16[256,128]{1,0:T(8,128)(2,1)S(1)}, bf16[128,256]{1,0:T(8,128)(2,1)S(1)}) custom-call(s32[3]{0:T(128)S(1)} %copy-done.11, bf16[64,128,256]{2,1,0:T(8,128)(2,1)S(1)} %copy-done, bf16[64,64,256]{2,1,0:T(8,128)(2,1)} %collective-permute-done.3.other_pairs, bf16[128,256]{1,0:T(8,128)(2,1)S(1)} %copy-done.9, ...), custom_call_target="tpu_custom_call" | custom-call | bytes 12000000 | tf_op jit(solution)/shard_map/turn_pairs/pallas_call | solution.py:571
  32.1 0.0 collective-permute-done.4.out_other
  32.1 0.0 collective-permute-done.7.rest_3_
  32.2 0.9 %collective-permute-done.6.rest_2_ = bf16[18,16,128]{2,1,0:T(8,128)(2,1)S(1)} collective-permute-done((bf16[18,16,128]{2,1,0:T(8,128)(2,1)}, bf16[18,16,128]{2,1,0:T(8,128)(2,1)S(1)}, u32[]{:S(2)}, u32[]{:S(2)}) %collective-permute-start.6) | collective-permute-done | bytes 73760 | tf_op jit(solution)/shard_map/ppermute | solution.py:790
  33.1 0.0 collective-permute-done.5.rest_1_
  33.1 0.0 copy-done.6
  33.1 2.8 %nodes.3.rest_0_ = bf16[16,256]{1,0:T(8,128)(2,1)S(1)} custom-call(s32[1]{0:T(128)} %bitcast.8.place, bf16[128,256]{1,0:T(8,128)(2,1)S(1)} %copy-done.6, bf16[1056,256]{1,0:T(8,128)(2,1)S(1)} %copy-done.1, bf16[1056,256]{1,0:T(8,128)(2,1)} %collective-permute-done.4.out_other, f32[1,256]{1,0:T(1,128)S(1)} %bitcast.11, f32[1,256]{1,0:T(1,128)S(1)} %bitcast.12, ...), custom_call_target="tpu_custom_call" | custom-call | bytes 6000000 | tf_op jit(solution)/shard_map/nodes/pallas_call | solution.py:538
  36.0 2.8 %collective-permute-start.10 = (bf16[16,256]{1,0:T(8,128)(2,1)S(1)}, bf16[16,256]{1,0:T(8,128)(2,1)S(1)}, u32[]{:S(2)}, u32[]{:S(2)}) collective-permute-start(bf16[16,256]{1,0:T(8,128)(2,1)S(1)} %nodes.3.rest_0_), channel_id=1, source_target_pairs={{0,12},{4,8},{8,4},{12,0},{1,13},{5,9},{9,5},{13,1},{2,14},{6,10},... | collective-permute-start | bytes 24584 | tf_op jit(solution)/shard_map/ppermute | solution.py:790
  38.7 0.2 collective-permute-start.9
  38.9 1.4 %collective-permute-start.8 = (bf16[16,256]{1,0:T(8,128)(2,1)S(1)}, bf16[16,256]{1,0:T(8,128)(2,1)S(1)}, u32[]{:S(2)}, u32[]{:S(2)}) collective-permute-start(bf16[16,256]{1,0:T(8,128)(2,1)S(1)} %nodes.3.rest_0_), channel_id=1, source_target_pairs={{0,4},{4,0},{8,12},{12,8},{1,5},{5,1},{9,13},{13,9},{2,6},{6,2},{1... | collective-permute-start | bytes 24584 | tf_op jit(solution)/shard_map/ppermute | solution.py:790
  40.4 0.1 pad_add_fusion.place
  40.4 1.0 %collective-permute-done.10.rest_3_ = bf16[16,256]{1,0:T(8,128)(2,1)S(1)} collective-permute-done((bf16[16,256]{1,0:T(8,128)(2,1)S(1)}, bf16[16,256]{1,0:T(8,128)(2,1)S(1)}, u32[]{:S(2)}, u32[]{:S(2)}) %collective-permute-start.10) | collective-permute-done | bytes 8224 | tf_op jit(solution)/shard_map/ppermute | solution.py:790
  41.5 1.8 %collective-permute-done.9.rest_2_ = bf16[16,256]{1,0:T(8,128)(2,1)S(1)} collective-permute-done((bf16[16,256]{1,0:T(8,128)(2,1)S(1)}, bf16[16,256]{1,0:T(8,128)(2,1)S(1)}, u32[]{:S(2)}, u32[]{:S(2)}) %collective-permute-start.9) | collective-permute-done | bytes 8224 | tf_op jit(solution)/shard_map/ppermute | solution.py:790
  43.3 0.0 collective-permute-done.8.rest_1_
  43.3 0.0 copy-done.7
  43.3 7.3 %edges.1 = (bf16[64,128,256]{2,1,0:T(8,128)(2,1)}, bf16[65,64,256]{2,1,0:T(8,128)(2,1)S(1)}, bf16[128,256]{1,0:T(8,128)(2,1)}) custom-call(s32[2]{0:T(128)S(1)} %pad_add_fusion.place, bf16[64,128,256]{2,1,0:T(8,128)(2,1)S(1)} %get-tuple-element.45.turned, bf16[16,256]{1,0:T(8,128)(2,1)S(1)} %nodes.3.rest_0_, ...), custom_call_target="tpu_custom_call" | custom-call | bytes 24000000 | tf_op jit(solution)/shard_map/edges/pallas_call | solution.py:646
  50.6 0.0 collective-permute-start.11
  50.6 4.2 %collective-permute-done.11.arrived = bf16[65,64,256]{2,1,0:T(8,128)(2,1)S(1)} collective-permute-done((bf16[65,64,256]{2,1,0:T(8,128)(2,1)S(1)}, bf16[65,64,256]{2,1,0:T(8,128)(2,1)S(1)}, u32[]{:S(2)}, u32[]{:S(2)}) %collective-permute-start.11) | collective-permute-done | bytes 2129952 | tf_op jit(solution)/shard_map/ppermute | solution.py:746
  54.8 1.3 %finish.1 = (bf16[64,128,256]{2,1,0:T(8,128)(2,1)}, bf16[128,256]{1,0:T(8,128)(2,1)}) custom-call(bf16[65,64,256]{2,1,0:T(8,128)(2,1)S(1)} %collective-permute-done.11.arrived, bf16[64,128,256]{2,1,0:T(8,128)(2,1)} %get-tuple-element.52.pairs_in, bf16[128,256]{1,0:T(8,128)(2,1)} %get-tuple-element.53.nodes_in), custom_call_target="tpu_custom_call", output_to_operand_aliasing={{0}: (1, {}), {1}: (2, {})} | custom-call | bytes 3000000 | tf_op jit(solution)/shard_map/finish/pallas_call | solution.py:699
  (20 shorter events, 0.0 us)
Async XLA Ops:
  0.6 13.1 %copy-start.1 = (bf16[1056,256]{1,0:T(8,128)(2,1)S(1)}, bf16[1056,256]{1,0:T(8,128)(2,1)}, u32[]{:S(2)}) copy-start(bf16[1056,256]{1,0:T(8,128)(2,1)} %out_own.1) | copy-start | bytes 1622020
  2.4 3.1 %collective-permute-start = (bf16[672,256]{1,0:T(8,128)(2,1)}, bf16[672,256]{1,0:T(8,128)(2,1)S(1)}, u32[]{:S(2)}, u32[]{:S(2)}) collective-permute-start(bf16[672,256]{1,0:T(8,128)(2,1)} %pack.1), channel_id=1, source_target_pairs={{0,1},{1,0},{2,3},{3,2},{4,5},{5,4},{6,7},{7,6},{8,9},{9,8},{10,11... | collective-permute-start | bytes 1032200 | tf_op jit(solution)/shard_map/ppermute | solution.py:746
  2.9 5.2 %collective-permute-start.1 = (bf16[64,256]{1,0:T(8,128)(2,1)}, bf16[64,256]{1,0:T(8,128)(2,1)S(1)}, u32[]{:S(2)}, u32[]{:S(2)}) collective-permute-start(bf16[64,256]{1,0:T(8,128)(2,1)} %rest_0_), channel_id=1, source_target_pairs={{0,2},{1,3},{2,0},{3,1},{4,6},{5,7},{6,4},{7,5},{8,10},{9,11},{10,... | collective-permute-start | bytes 98312 | tf_op jit(solution)/shard_map/ppermute | solution.py:754
  5.4 3.6 %collective-permute-start.2 = (bf16[64,256]{1,0:T(8,128)(2,1)}, bf16[64,256]{1,0:T(8,128)(2,1)S(1)}, u32[]{:S(2)}, u32[]{:S(2)}) collective-permute-start(bf16[64,256]{1,0:T(8,128)(2,1)} %rest_0_), channel_id=1, source_target_pairs={{0,3},{1,2},{2,1},{3,0},{4,7},{5,6},{6,5},{7,4},{8,11},{9,10},{10,... | collective-permute-start | bytes 98312 | tf_op jit(solution)/shard_map/ppermute | solution.py:754
  5.5 4.2 %copy-start.14 = (bf16[672,256]{1,0:T(8,128)(2,1)}, bf16[672,256]{1,0:T(8,128)(2,1)S(1)}, u32[]{:S(2)}) copy-start(bf16[672,256]{1,0:T(8,128)(2,1)S(1)} %collective-permute-done.packed) | copy-start | bytes 1032196
  8.1 1.7 %copy-start.15 = (bf16[64,256]{1,0:T(8,128)(2,1)}, bf16[64,256]{1,0:T(8,128)(2,1)S(1)}, u32[]{:S(2)}) copy-start(bf16[64,256]{1,0:T(8,128)(2,1)S(1)} %collective-permute-done.1.rest_1_) | copy-start | bytes 98308
  8.9 0.8 %copy-start.16 = (bf16[64,256]{1,0:T(8,128)(2,1)}, bf16[64,256]{1,0:T(8,128)(2,1)S(1)}, u32[]{:S(2)}) copy-start(bf16[64,256]{1,0:T(8,128)(2,1)S(1)} %collective-permute-done.2.rest_2_) | copy-start | bytes 98308
  8.9 5.1 %collective-permute-start.3 = (bf16[64,64,256]{2,1,0:T(8,128)(2,1)}, bf16[64,64,256]{2,1,0:T(8,128)(2,1)}, u32[]{:S(2)}, u32[]{:S(2)}) collective-permute-start(bf16[64,64,256]{2,1,0:T(8,128)(2,1)} %slice_pairs.1), channel_id=1, source_target_pairs={{0,1},{1,0},{2,3},{3,2},{4,5},{5,4},{6,7},{7,6},{8,9},{9,8},{10,11... | collective-permute-start | bytes 6291464 | tf_op jit(solution)/shard_map/ppermute | solution.py:746
  13.7 18.4 %collective-permute-start.4 = (bf16[1056,256]{1,0:T(8,128)(2,1)S(1)}, bf16[1056,256]{1,0:T(8,128)(2,1)}, u32[]{:S(2)}, u32[]{:S(2)}) collective-permute-start(bf16[1056,256]{1,0:T(8,128)(2,1)S(1)} %copy-done.1), channel_id=1, source_target_pairs={{0,1},{1,0},{2,3},{3,2},{4,5},{5,4},{6,7},{7,6},{8,9},{9,8},{10,11... | collective-permute-start | bytes 1622024 | tf_op jit(solution)/shard_map/ppermute | solution.py:746
  14.1 12.7 %copy-start.9 = (bf16[128,256]{1,0:T(8,128)(2,1)S(1)}, bf16[128,256]{1,0:T(8,128)(2,1)}, u32[]{:S(2)}) copy-start(bf16[128,256]{1,0:T(8,128)(2,1)} %in_weight.1) | copy-start | bytes 196612
  14.1 12.7 %copy-start.10 = (bf16[256,128]{1,0:T(8,128)(2,1)S(1)}, bf16[256,128]{1,0:T(8,128)(2,1)}, u32[]{:S(2)}) copy-start(bf16[256,128]{1,0:T(8,128)(2,1)} %out_weight.1) | copy-start | bytes 196612
  14.1 12.7 %copy-start.11 = (s32[3]{0:T(128)S(1)}, s32[3]{0:T(128)}, u32[]{:S(2)}) copy-start(s32[3]{0:T(128)} %pad_add_fusion.1.place) | copy-start | bytes 40
  14.1 19.0 %copy-start.6 = (bf16[128,256]{1,0:T(8,128)(2,1)S(1)}, bf16[128,256]{1,0:T(8,128)(2,1)}, u32[]{:S(2)}) copy-start(bf16[128,256]{1,0:T(8,128)(2,1)} %nodes.4) | copy-start | bytes 196612
  22.3 10.8 %copy-start.12 = (f32[256]{0:T(256)S(1)}, f32[256]{0:T(256)}, u32[]{:S(2)}) copy-start(f32[256]{0:T(256)} %param.41) | copy-start | bytes 3076
  22.3 10.8 %copy-start.13 = (f32[256]{0:T(256)S(1)}, f32[256]{0:T(256)}, u32[]{:S(2)}) copy-start(f32[256]{0:T(256)} %param.42) | copy-start | bytes 3076
  22.3 9.8 %collective-permute-start.7 = (bf16[18,16,128]{2,1,0:T(8,128)(2,1)}, bf16[18,16,128]{2,1,0:T(8,128)(2,1)S(1)}, u32[]{:S(2)}, u32[]{:S(2)}) collective-permute-start(bf16[18,16,128]{2,1,0:T(8,128)(2,1)} %get-tuple-element.40), channel_id=1, source_target_pairs={{0,4},{4,0},{8,12},{12,8},{1,5},{5,1},{9,13},{13,9},{2,6},{6,2},{1... | collective-permute-start | bytes 221192 | tf_op jit(solution)/shard_map/ppermute | solution.py:790
  23.9 9.1 %collective-permute-start.6 = (bf16[18,16,128]{2,1,0:T(8,128)(2,1)}, bf16[18,16,128]{2,1,0:T(8,128)(2,1)S(1)}, u32[]{:S(2)}, u32[]{:S(2)}) collective-permute-start(bf16[18,16,128]{2,1,0:T(8,128)(2,1)} %get-tuple-element.41), channel_id=1, source_target_pairs={{0,8},{4,12},{8,0},{12,4},{1,9},{5,13},{9,1},{13,5},{2,10},{6,14},... | collective-permute-start | bytes 221192 | tf_op jit(solution)/shard_map/ppermute | solution.py:790
  26.5 6.5 %collective-permute-start.5 = (bf16[18,16,128]{2,1,0:T(8,128)(2,1)}, bf16[18,16,128]{2,1,0:T(8,128)(2,1)S(1)}, u32[]{:S(2)}, u32[]{:S(2)}) collective-permute-start(bf16[18,16,128]{2,1,0:T(8,128)(2,1)} %get-tuple-element.42), channel_id=1, source_target_pairs={{0,12},{4,8},{8,4},{12,0},{1,13},{5,9},{9,5},{13,1},{2,14},{6,10},... | collective-permute-start | bytes 221192 | tf_op jit(solution)/shard_map/ppermute | solution.py:790
  26.8 2.2 %copy-start = (bf16[64,128,256]{2,1,0:T(8,128)(2,1)S(1)}, bf16[64,128,256]{2,1,0:T(8,128)(2,1)}, u32[]{:S(2)}) copy-start(bf16[64,128,256]{2,1,0:T(8,128)(2,1)} %own_pairs.3) | copy-start | bytes 12582916
  28.9 4.1 %copy-start.2 = (bf16[256,1024]{1,0:T(8,128)(2,1)S(1)}, bf16[256,1024]{1,0:T(8,128)(2,1)}, u32[]{:S(2)}) copy-start(bf16[256,1024]{1,0:T(8,128)(2,1)} %gate_weight.1) | copy-start | bytes 1572868
  28.9 4.1 %copy-start.3 = (bf16[256,1024]{1,0:T(8,128)(2,1)S(1)}, bf16[256,1024]{1,0:T(8,128)(2,1)}, u32[]{:S(2)}) copy-start(bf16[256,1024]{1,0:T(8,128)(2,1)} %up_weight.1) | copy-start | bytes 1572868
  28.9 4.1 %copy-start.4 = (bf16[1024,256]{1,0:T(8,128)(2,1)S(1)}, bf16[1024,256]{1,0:T(8,128)(2,1)}, u32[]{:S(2)}) copy-start(bf16[1024,256]{1,0:T(8,128)(2,1)} %down_weight.1) | copy-start | bytes 1572868
  29.0 4.2 %copy-start.8 = (bf16[18,16,128]{2,1,0:T(8,128)(2,1)S(1)}, bf16[18,16,128]{2,1,0:T(8,128)(2,1)}, u32[]{:S(2)}) copy-start(bf16[18,16,128]{2,1,0:T(8,128)(2,1)} %get-tuple-element.39.rest_0_) | copy-start | bytes 221188
  29.0 14.3 %copy-start.5 = (f32[256,256]{1,0:T(8,128)S(1)}, f32[256,256]{1,0:T(8,128)}, u32[]{:S(2)}) copy-start(f32[256,256]{1,0:T(8,128)} %get-tuple-element.48.rest_4_) | copy-start | bytes 786436
  29.0 14.3 %copy-start.7 = (bf16[256,256]{1,0:T(8,128)(2,1)S(1)}, bf16[256,256]{1,0:T(8,128)(2,1)}, u32[]{:S(2)}) copy-start(bf16[256,256]{1,0:T(8,128)(2,1)} %rest_7_.1) | copy-start | bytes 393220
  36.0 5.5 %collective-permute-start.10 = (bf16[16,256]{1,0:T(8,128)(2,1)S(1)}, bf16[16,256]{1,0:T(8,128)(2,1)S(1)}, u32[]{:S(2)}, u32[]{:S(2)}) collective-permute-start(bf16[16,256]{1,0:T(8,128)(2,1)S(1)} %nodes.3.rest_0_), channel_id=1, source_target_pairs={{0,12},{4,8},{8,4},{12,0},{1,13},{5,9},{9,5},{13,1},{2,14},{6,10},... | collective-permute-start | bytes 24584 | tf_op jit(solution)/shard_map/ppermute | solution.py:790
  38.7 4.5 %collective-permute-start.9 = (bf16[16,256]{1,0:T(8,128)(2,1)S(1)}, bf16[16,256]{1,0:T(8,128)(2,1)S(1)}, u32[]{:S(2)}, u32[]{:S(2)}) collective-permute-start(bf16[16,256]{1,0:T(8,128)(2,1)S(1)} %nodes.3.rest_0_), channel_id=1, source_target_pairs={{0,8},{4,12},{8,0},{12,4},{1,9},{5,13},{9,1},{13,5},{2,10},{6,14},... | collective-permute-start | bytes 24584 | tf_op jit(solution)/shard_map/ppermute | solution.py:790
  38.9 4.3 %collective-permute-start.8 = (bf16[16,256]{1,0:T(8,128)(2,1)S(1)}, bf16[16,256]{1,0:T(8,128)(2,1)S(1)}, u32[]{:S(2)}, u32[]{:S(2)}) collective-permute-start(bf16[16,256]{1,0:T(8,128)(2,1)S(1)} %nodes.3.rest_0_), channel_id=1, source_target_pairs={{0,4},{4,0},{8,12},{12,8},{1,5},{5,1},{9,13},{13,9},{2,6},{6,2},{1... | collective-permute-start | bytes 24584 | tf_op jit(solution)/shard_map/ppermute | solution.py:790
  50.6 4.2 %collective-permute-start.11 = (bf16[65,64,256]{2,1,0:T(8,128)(2,1)S(1)}, bf16[65,64,256]{2,1,0:T(8,128)(2,1)S(1)}, u32[]{:S(2)}, u32[]{:S(2)}) collective-permute-start(bf16[65,64,256]{2,1,0:T(8,128)(2,1)S(1)} %get-tuple-element.51), channel_id=1, source_target_pairs={{0,1},{1,0},{2,3},{3,2},{4,5},{5,4},{6,7},{7,6},{8,9},{9,8},{10,11... | collective-permute-start | bytes 6389768 | tf_op jit(solution)/shard_map/ppermute | solution.py:746

commit v4 on v3

--- a/solution.py
+++ b/solution.py
@@ -17,10 +17,9 @@
 SLOT = 64
 ROWS = 16
 VMEM_MIB = 60
-CHUNKS = 4
 ATTEND_ROWS = 32
 TURN_ROWS = 32
-EDGE_ROWS = 16
+EDGE_ROWS = 32
 
 linear_scale = math.sqrt(1.0 / 3.0)
 masked_score = -1000000000.0
@@ -117,45 +116,9 @@
         out_shape=jax.ShapeDtypeStruct((total, key_weight.shape[1]), bf16),
         scratch_shapes=[pltpu.VMEM((16, key_weight.shape[1]), f32)],
         compiler_params=params(63),
-        cost_estimate=cost(2),
+        cost_estimate=cost(10),
         name="pack",
     )(point_gain, chain_gain, *operands)
-
-
-def slice_kernel(pairs, sliced, buffer, arrivals, departures):
-    half = sliced.shape[1]
-    begin = pl.multiple_of((1 - lax.axis_index("sub")) * half, half)
-    span = sliced.shape[0] // CHUNKS
-    copies = []
-    for chunk in range(CHUNKS):
-        at = slice(chunk * span, (chunk + 1) * span)
-        load = pltpu.make_async_copy(pairs.at[at, pl.ds(begin, half), :], buffer.at[at], arrivals.at[chunk])
-        load.start()
-        copies.append((load, pltpu.make_async_copy(buffer.at[at], sliced.at[at], departures.at[chunk])))
-    for load, store in copies:
-        load.wait()
-        store.start()
-    for _, store in copies:
-        store.wait()
-
-
-def slice_pairs(pairs, half):
-    shape = (pairs.shape[0], half, pairs.shape[2])
-    hbm = pl.BlockSpec(memory_space=pl.ANY)
-    return pl.pallas_call(
-        slice_kernel,
-        in_specs=[hbm],
-        out_specs=hbm,
-        out_shape=jax.ShapeDtypeStruct(shape, bf16),
-        scratch_shapes=[
-            pltpu.VMEM(shape, bf16),
-            pltpu.SemaphoreType.DMA((CHUNKS,)),
-            pltpu.SemaphoreType.DMA((CHUNKS,)),
-        ],
-        compiler_params=params(63),
-        cost_estimate=cost(3),
-        name="slice_pairs",
-    )(pairs)
 
 
 def project_kernel(
@@ -286,62 +249,24 @@
         scores[head] = linear_scale * score
 
 
-def project(
-    place, gains, query_side, key_side, query_weight, key_weight, bias_weight, packed, edge_key_weight, key_blocks, half
-):
-    query_count = query_side[0].shape[0]
-    key_count = key_side[0].shape[1]
-    local_heads = gains[0].shape[0]
-    heads = 2 * local_heads
-    channels, hidden = bias_weight.shape[1], edge_key_weight.shape[1]
-    operands = [*query_side, *key_side, query_weight, key_weight, bias_weight, packed, edge_key_weight, *key_blocks]
-    return pl.pallas_call(
-        functools.partial(project_kernel, len(key_blocks)),
-        in_specs=[SMEM] * 3 + [whole(a) for a in operands],
-        out_shape=(
-            jax.ShapeDtypeStruct((heads, half, key_count), f32),
-            jax.ShapeDtypeStruct((heads, SLOT, key_count), bf16),
-            jax.ShapeDtypeStruct((heads * ROWS, channels * ROWS), bf16),
-            jax.ShapeDtypeStruct((query_count, 16), f32),
-            jax.ShapeDtypeStruct((hidden, key_count), f32),
-        ),
-        scratch_shapes=[
-            pltpu.VMEM((key_count, query_side[0].shape[1]), bf16),
-            pltpu.VMEM((2, local_heads * KCOLS, key_count), f32),
-            pltpu.VMEM((2, local_heads * QCOLS, query_count), f32),
-            pltpu.VMEM((heads, SLOT, key_count), f32),
-            pltpu.VMEM((heads, SLOT, query_count), f32),
-            pltpu.VMEM((heads, query_count, SLOT), f32),
-        ],
-        compiler_params=params(63),
-        cost_estimate=cost(12),
-        name="project",
-    )(place, *gains, *operands)
-
-
-def attend_kernel(
-    targets,
-    place,
-    base_scores,
-    values,
-    bias_spread,
-    frames,
-    mask,
-    own_pairs,
-    other_pairs,
-    *rest,
-):
-    results = rest[:targets]
-    part, weight_high, weight_low, peaks, sums, gather_own, gather_other = rest[targets:]
+def attend_kernel(operands, key_blocks, targets, place, own_pairs, other_pairs, mask, *rest):
+    inputs = rest[:operands]
+    results, edge_keys = rest[operands : operands + targets], rest[operands + targets]
+    scratch = rest[operands + targets + 1 :]
+    part, weight_high, weight_low, peaks, sums, gather_own, gather_other = scratch[:7]
+    scores, values, bias_spread, frames, *project_scratch = scratch[7:]
     step = pl.program_id(0)
     sub = place[0]
-    heads, _, keys = base_scores.shape
+    heads, half, keys = scores.shape
     channels = own_pairs.shape[0]
     spread = channels * ROWS
     lanes = 2 * channels
 
     @pl.when(step == 0)
     def _():
+        project_kernel(
+            key_blocks, place, *inputs, scores, values, bias_spread, frames, edge_keys, *project_scratch
+        )
         source = iota((spread, lanes), 0) // ROWS
         target = iota((spread, lanes), 1)
         gather_own[...] = (target == source + sub * channels).astype(f32).astype(bf16)
@@ -355,13 +280,13 @@
         own = own_pairs[:, span, :].reshape(spread, keys)
         other = other_pairs[:, span, :].reshape(spread, keys)
         bias = dot(bias_spread[:, :spread], own) + dot(bias_spread[:, spread:], other)
-        score = base_scores[:, span, :] + linear_scale * bias.reshape(heads, ROWS, keys)
+        at = pl.ds(pl.multiple_of(step * rows + begin, ROWS), ROWS)
+        score = scores[:, at, :] + linear_scale * bias.reshape(heads, ROWS, keys)
         score = jnp.where(mask[span, :][None] == 1, score, masked_score)
         peak = jnp.max(score, axis=2, keepdims=True)
         weight = jnp.exp(score - peak)
         total = jnp.sum(weight, axis=2, keepdims=True)
         high = weight.astype(bf16)
-        at = pl.ds(pl.multiple_of(step * rows + begin, ROWS), ROWS)
         weight_high[:, at, :] = high
         weight_low[:, at, :] = (weight - high.astype(f32)).astype(bf16)
         peaks[:, at, :] = jnp.broadcast_to(peak, (heads, ROWS, lanes))
@@ -375,7 +300,7 @@
 
     @pl.when(step == pl.num_programs(0) - 1)
     def _():
-        half = frames.shape[0]
+        own_frames = frames[pl.ds(pl.multiple_of(sub * half, half), half), :]
         lane = iota((half, 2 * SLOT), 1)
         first = lane < SLOT
         slot = lane % SLOT
@@ -385,7 +310,7 @@
         def on_planes(columns):
             out = jnp.zeros((half, 2 * SLOT), f32)
             for b, column in columns:
-                out = jnp.where(inside & (plane == b), frames[:, column : column + 1], out)
+                out = jnp.where(inside & (plane == b), own_frames[:, column : column + 1], out)
             return out
 
         shift = on_planes([(a, 9 + a) for a in range(3)])
@@ -421,43 +346,60 @@
             results[target][...] = part[:, pl.ds(pl.multiple_of(at, share) if targets > 1 else 0, share), :]
 
 
-def attend(place, own_pairs, other_pairs, base_scores, mask, values, bias_spread, frames, targets):
-    heads, half, keys = base_scores.shape
-    channels = own_pairs.shape[0]
+def attend(place, gains, inputs, key_blocks, own_pairs, other_pairs, mask, half, hidden, targets):
+    channels, query_count, keys = own_pairs.shape
+    features = inputs[0].shape[1]
+    local_heads = gains[0].shape[0]
+    heads = 2 * local_heads
+    slots, lanes = heads + local_heads, 2 * channels
     rows = math.gcd(half, ATTEND_ROWS)
     steps = half // rows
+    operands = [*inputs, *key_blocks]
     pair_block = pl.BlockSpec((channels, rows, keys), lambda g, p: (0, p[0] * steps + g, 0))
-    slots = heads + heads // 2
     return pl.pallas_call(
-        functools.partial(attend_kernel, targets),
+        functools.partial(attend_kernel, len(gains) + len(operands), len(key_blocks), targets),
         grid_spec=pltpu.PrefetchScalarGridSpec(
             num_scalar_prefetch=1,
             grid=(steps,),
             in_specs=[
-                pl.BlockSpec((heads, rows, keys), lambda g, p: (0, g, 0)),
-                whole(values),
-                whole(bias_spread),
-                pl.BlockSpec((half, frames.shape[1]), lambda g, p: (p[0], 0)),
+                pair_block,
+                pair_block,
                 pl.BlockSpec((rows, keys), lambda g, p: (p[0] * steps + g, 0)),
-                pair_block,
-                pl.BlockSpec((channels, rows, keys), lambda g, p: (0, g, 0)),
+                *[SMEM for _ in gains],
+                *[whole(a) for a in operands],
             ],
-            out_specs=[pl.BlockSpec((slots, half // targets, 2 * channels), lambda g, p: (0, 0, 0))] * targets,
+            out_specs=[
+                *[pl.BlockSpec((slots, half // targets, lanes), lambda g, p: (0, 0, 0))] * targets,
+                pl.BlockSpec((hidden, keys), lambda g, p: (0, 0)),
+            ],
             scratch_shapes=[
-                pltpu.VMEM((slots, half, 2 * channels), bf16),
+                pltpu.VMEM((slots, half, lanes), bf16),
                 pltpu.VMEM((heads, half, keys), bf16),
                 pltpu.VMEM((heads, half, keys), bf16),
-                pltpu.VMEM((heads, half, 2 * channels), f32),
-                pltpu.VMEM((heads, half, 2 * channels), f32),
-                pltpu.VMEM((channels * ROWS, 2 * channels), bf16),
-                pltpu.VMEM((channels * ROWS, 2 * channels), bf16),
+                pltpu.VMEM((heads, half, lanes), f32),
+                pltpu.VMEM((heads, half, lanes), f32),
+                pltpu.VMEM((channels * ROWS, lanes), bf16),
+                pltpu.VMEM((channels * ROWS, lanes), bf16),
+                pltpu.VMEM((heads, half, keys), f32),
+                pltpu.VMEM((heads, SLOT, keys), bf16),
+                pltpu.VMEM((heads * ROWS, lanes * ROWS), bf16),
+                pltpu.VMEM((query_count, 16), f32),
+                pltpu.VMEM((keys, features), bf16),
+                pltpu.VMEM((2, local_heads * KCOLS, keys), f32),
+                pltpu.VMEM((2, local_heads * QCOLS, query_count), f32),
+                pltpu.VMEM((heads, SLOT, keys), f32),
+                pltpu.VMEM((heads, SLOT, query_count), f32),
+                pltpu.VMEM((heads, query_count, SLOT), f32),
             ],
         ),
-        out_shape=[jax.ShapeDtypeStruct((slots, half // targets, 2 * channels), bf16)] * targets,
+        out_shape=[
+            *[jax.ShapeDtypeStruct((slots, half // targets, lanes), bf16)] * targets,
+            jax.ShapeDtypeStruct((hidden, keys), f32),
+        ],
         compiler_params=params(63),
         cost_estimate=cost(9),
         name="attend",
-    )(place, base_scores, values, bias_spread, frames, mask, own_pairs, other_pairs)
+    )(place, own_pairs, other_pairs, mask, *gains, *operands)
 
 
 def norm(values, gain):
@@ -480,6 +422,12 @@
     *rest,
 ):
     parts, result = rest[:count], rest[count]
+    *held, sems = rest[count + 1 :]
+    sources = (out_own, out_other, gate_weight, up_weight, down_weight)
+    loads = [pltpu.make_async_copy(a, b, sems.at[i]) for i, (a, b) in enumerate(zip(sources, held))]
+    for load in loads:
+        load.start()
+    out_own, out_other, gate_weight, up_weight, down_weight = held
     heads = parts[0].shape[0] * 2 // 3
     rows, lanes = parts[0].shape[1:]
     local_heads = heads // 2
@@ -512,6 +460,8 @@
         1.0 + pltpu.roll(squares, PV, 1) + pltpu.roll(squares, 2 * PV, 1) + pltpu.roll(squares, 3 * PV, 1)
     )
     merged = jnp.where(slot < at, merged, norms).astype(bf16)
+    for load in loads[:2]:
+        load.wait()
     projected = jnp.zeros((rows, nodes.shape[1]), f32)
     for head in range(heads):
         pair, odd = divmod(head, 2)
@@ -528,6 +478,8 @@
     own = nodes[pl.ds(pl.multiple_of(place[0], ROWS), rows), :]
     first_nodes = norm(own.astype(f32) + projected, first_gain[...])
     first_rounded = first_nodes.astype(bf16)
+    for load in loads[2:]:
+        load.wait()
     gate = dot(first_rounded, gate_weight[...])
     hidden = (gate / (1.0 + jnp.exp(-gate)) * dot(first_rounded, up_weight[...])).astype(bf16)
     result[...] = norm(first_nodes + dot(hidden, down_weight[...]), second_gain[...]).astype(bf16)
@@ -535,9 +487,13 @@
 
 def update_nodes(place, parts, nodes, out_own, out_other, first_gain, second_gain, gate_weight, up_weight, down_weight):
     operands = [nodes, out_own, out_other, first_gain, second_gain, gate_weight, up_weight, down_weight, *parts]
+    weights = [out_own, out_other, gate_weight, up_weight, down_weight]
+    late = {1, 2, 5, 6, 7}
+    hbm = pl.BlockSpec(memory_space=pl.ANY)
     return pl.pallas_call(
         functools.partial(node_kernel, len(parts)),
-        in_specs=[SMEM] + [whole(a) for a in operands],
+        in_specs=[SMEM] + [hbm if i in late else whole(a) for i, a in enumerate(operands)],
+        scratch_shapes=[pltpu.VMEM(a.shape, bf16) for a in weights] + [pltpu.SemaphoreType.DMA((len(weights),))],
         out_shape=jax.ShapeDtypeStruct((parts[0].shape[1], nodes.shape[1]), bf16),
         compiler_params=params(16),
         cost_estimate=cost(2),
@@ -575,7 +531,7 @@
             grid=(steps,),
             in_specs=[
                 pl.BlockSpec((channels, rows, keys), lambda g, p: (0, p[0] * steps + g, 0)),
-                pl.BlockSpec((channels, rows, keys), lambda g, p: (0, g, 0)),
+                pl.BlockSpec((channels, rows, keys), lambda g, p: (0, p[0] * steps + g, 0)),
                 whole(in_weight),
                 whole(out_weight),
             ],
@@ -674,7 +630,7 @@
             jax.ShapeDtypeStruct((channels + extra, half, keys), bf16),
             jax.ShapeDtypeStruct((count, features), bf16),
         ),
-        compiler_params=params(20),
+        compiler_params=params(36),
         cost_estimate=cost(8),
         name="edges",
     )(place, turned, *ring, edge_keys, in_left, out_left, query_weight)
@@ -756,32 +712,40 @@
     half = node_query.shape[0] // subs
     query_weight, key_weight, bias_weight = query_weight.T, key_weight.T, bias_weight.T
     packed = pack(point_gain, chain_gain, key_weight, query_weight, bias_weight, node_key)
-    packed, late_pairs = lax.optimization_barrier((swap(packed), pair_features))
-    far_pairs, key_blocks = lax.optimization_barrier((slice_pairs(late_pairs, half), key_blocks))
-    other_pairs = swap(far_pairs)
+    packed = swap(packed)
+    other_pairs = swap(pair_features)
     place = jnp.stack([sub, lax.axis_index("row"), col]).astype(jnp.int32)
 
     share = half // cols
     assert cols & (cols - 1) == 0
     spare = -share % ROWS
-    base_scores, values, bias_spread, frames, edge_keys = project(
+    targets = 1 if spare else cols
+    *pieces, edge_keys = attend(
         place,
         [point_gain, chain_gain],
-        [node_query, query_angles, query_trans, query_chain[None, :]],
-        [key_angles, key_trans, key_chain[None, :]],
-        query_weight,
-        key_weight,
-        bias_weight,
-        packed,
-        edge_key_weight,
+        [
+            node_query,
+            query_angles,
+            query_trans,
+            query_chain[None, :],
+            key_angles,
+            key_trans,
+            key_chain[None, :],
+            query_weight,
+            key_weight,
+            bias_weight,
+            packed,
+            edge_key_weight,
+        ],
         key_blocks,
+        pair_features,
+        other_pairs,
+        pair_mask,
         half,
+        edge_key_weight.shape[1],
+        targets,
     )
-    targets = 1 if spare else cols
-    pieces = attend(
-        place, pair_features, other_pairs, base_scores, pair_mask, values, bias_spread, frames, targets
-    )
-    other_out = swap(lax.optimization_barrier((out_weight, base_scores))[0])
+    other_out = swap(lax.optimization_barrier((out_weight, edge_keys))[0])
     if spare:
         pieces = [
             lax.dynamic_slice_in_dim(pieces[0], jnp.bitwise_xor(col, k) * share, share, 1) for k in range(cols)

time: 56.5 us -> 53.9 us (0.954)
  Pallas kernels: 31.1 us -> 25.2 us
  waiting for transfers between devices: 8.78 us -> 11.3 us
  local copies, waits for them, and re-layouts: 2.25 us -> 2.98 us
    pallas_call x3 -> x1, Pallas kernels: 14.7 us -> 9.85 us  [attend(): pl.pallas_call(functools.partial(attend_kernel, len(gains) + len(operands...]
    ppermute x2, waiting for transfers between devices: 0.83 us -> 3.15 us  [shards(): lax.ppermute(node_key, ('row', 'sub'), step(r, c))]
    unnamed x34, local copies, waits for them, and re-layouts: 2.25 us -> 2.98 us
  transfers between devices with their start and end apart: 12 -> 12, of which waited for: 5 -> 6; matrix products, arithmetic and copies ran while one was open for 1% -> 1% of each run, Pallas kernels for 32% -> 9%
where the time goes in v4:
time: 53.9 us; the launch traced here: 53.7 us
  Pallas kernels  25.2 us (47%)
  starting transfers between devices  12.6 us (23%)
  waiting for transfers between devices  11.3 us (21%)
  local copies, waits for them, and re-layouts  2.98 us (6%)
  between operations  0.83 us (2%)
  other arithmetic  0.75 us (1%)
    pallas_call x1, Pallas kernels, attend(): pl.pallas_call(functools.partial(attend_kernel, len(gains) + len(operands...  9.85 us
    ppermute x6, starting transfers between devices, meet(): return lax.ppermute(values, 'col', [(i, i ^ k) for i in range(cols)])  9.03 us
    pallas_call x1, Pallas kernels, update_pairs(): pl.pallas_call(functools.partial(edge_kernel, len(ring)), grid_spec=pltpu...  6.77 us
    ppermute x4, waiting for transfers between devices, swap(): lax.ppermute(values, 'sub', [(i, (i + 1) % subs) for i in range(subs)])  4.21 us
    ppermute x6, waiting for transfers between devices, meet(): return lax.ppermute(values, 'col', [(i, i ^ k) for i in range(cols)])  3.93 us
    ppermute x2, waiting for transfers between devices, shards(): lax.ppermute(node_key, ('row', 'sub'), step(r, c))  3.15 us
    pallas_call x1, Pallas kernels, turn_pairs(): pl.pallas_call(turn_kernel, grid_spec=pltpu.PrefetchScalarGridSpec(num_sc...  3.14 us
    unnamed x34, local copies, waits for them, and re-layouts  2.98 us
  transfers between devices with their start and end apart: 12, of which 6 were waited for; matrix products, arithmetic and copies ran while one was open for 1% of the time, Pallas kernels for 9%

profile of v4, /device:TPU:0, one launch (start us, length us, event | category | flops | bytes accessed | tf_op | source)
XLA Modules:
  0.0 53.7 jit_solution(11974901058780461261)
XLA Ops:
  0.6 0.5 collective-permute-start
  1.1 1.7 %pack.1 = bf16[672,256]{1,0:T(8,128)(2,1)} custom-call(f32[6]{0:T(128)} %rest_0_.1, f32[6]{0:T(128)} %rest_1_.1, bf16[408,256]{1,0:T(8,128)(2,1)} %bitcast.13, bf16[168,256]{1,0:T(8,128)(2,1)} %bitcast.15, bf16[6,128]{1,0:T(8,128)(2,1)} %bitcast.17, bf16[64,256]{1,0:T(8,128)(2,1)} %rest_14_.1), custom_call_target="tpu_custom_call" | custom-call | bytes 30000000 | tf_op jit(solution)/shard_map/pack/pallas_call | solution.py:113
  2.9 0.1 collective-permute-start.1
  3.0 2.9 %collective-permute-start.2 = (bf16[64,256]{1,0:T(8,128)(2,1)}, bf16[64,256]{1,0:T(8,128)(2,1)S(1)}, u32[]{:S(2)}, u32[]{:S(2)}) collective-permute-start(bf16[64,256]{1,0:T(8,128)(2,1)} %rest_14_.1), channel_id=1, source_target_pairs={{0,2},{1,3},{2,0},{3,1},{4,6},{5,7},{6,4},{7,5},{8,10},{9,11},{10,... | collective-permute-start | bytes 98312 | tf_op jit(solution)/shard_map/ppermute | solution.py:710
  5.9 0.0 collective-permute-start.3
  5.9 0.7 %pad_add_fusion.1.place = s32[3]{0:T(128)} fusion(s32[1]{0:T(128)} %bitcast.1, s32[1]{0:T(128)} %bitcast.2, s32[1]{0:T(128)} %bitcast), kind=kLoop, calls=%fused_computation.1 | loop fusion | flops 6 | bytes 24 | tf_op jit(solution)/shard_map/stack | solution.py:717
  6.6 1.4 %collective-permute-done.2.rest_15_ = bf16[64,256]{1,0:T(8,128)(2,1)S(1)} collective-permute-done((bf16[64,256]{1,0:T(8,128)(2,1)}, bf16[64,256]{1,0:T(8,128)(2,1)S(1)}, u32[]{:S(2)}, u32[]{:S(2)}) %collective-permute-start.2) | collective-permute-done | bytes 32800 | tf_op jit(solution)/shard_map/ppermute | solution.py:710
  8.0 1.7 %collective-permute-done.3.rest_16_ = bf16[64,256]{1,0:T(8,128)(2,1)S(1)} collective-permute-done((bf16[64,256]{1,0:T(8,128)(2,1)}, bf16[64,256]{1,0:T(8,128)(2,1)S(1)}, u32[]{:S(2)}, u32[]{:S(2)}) %collective-permute-start.3) | collective-permute-done | bytes 32800 | tf_op jit(solution)/shard_map/ppermute | solution.py:710
  9.7 0.0 collective-permute-done.1.rest_12_
  9.7 0.0 collective-permute-done.other_pairs
  9.7 0.7 %copy-done.14 = bf16[672,256]{1,0:T(8,128)(2,1)} copy-done((bf16[672,256]{1,0:T(8,128)(2,1)}, bf16[672,256]{1,0:T(8,128)(2,1)S(1)}, u32[]{:S(2)}) %copy-start.14) | copy-done | bytes 344088
  10.5 0.0 copy-done.15
  10.5 0.0 copy-done.16
  10.5 0.0 copy-start.10
  10.5 0.0 copy-start.11
  10.5 9.8 %attend.1 = (bf16[18,16,128]{2,1,0:T(8,128)(2,1)}, bf16[18,16,128]{2,1,0:T(8,128)(2,1)}, bf16[18,16,128]{2,1,0:T(8,128)(2,1)}, bf16[18,16,128]{2,1,0:T(8,128)(2,1)}, f32[256,256]{1,0:T(8,128)}) custom-call(s32[3]{0:T(128)} %pad_add_fusion.1.place, bf16[64,128,256]{2,1,0:T(8,128)(2,1)} %own_pairs.3, bf16[64,128,256]{2,1,0:T(8,128)(2,1)} %collective-permute-done.other_pairs, ...), custom_call_target="tpu_custom_call" | custom-call | bytes 27000000 | tf_op jit(solution)/shard_map/attend/pallas_call | solution.py:359
  20.3 0.0 copy-done.1
  20.4 0.1 collective-permute-start.4
  20.4 2.0 %collective-permute-start.7 = (bf16[18,16,128]{2,1,0:T(8,128)(2,1)}, bf16[18,16,128]{2,1,0:T(8,128)(2,1)S(1)}, u32[]{:S(2)}, u32[]{:S(2)}) collective-permute-start(bf16[18,16,128]{2,1,0:T(8,128)(2,1)} %get-tuple-element.20), channel_id=1, source_target_pairs={{0,4},{4,0},{8,12},{12,8},{1,5},{5,1},{9,13},{13,9},{2,6},{6,2},{1... | collective-permute-start | bytes 221192 | tf_op jit(solution)/shard_map/ppermute | solution.py:754
  22.4 2.6 %collective-permute-start.6 = (bf16[18,16,128]{2,1,0:T(8,128)(2,1)}, bf16[18,16,128]{2,1,0:T(8,128)(2,1)S(1)}, u32[]{:S(2)}, u32[]{:S(2)}) collective-permute-start(bf16[18,16,128]{2,1,0:T(8,128)(2,1)} %get-tuple-element.21), channel_id=1, source_target_pairs={{0,8},{4,12},{8,0},{12,4},{1,9},{5,13},{9,1},{13,5},{2,10},{6,14},... | collective-permute-start | bytes 221192 | tf_op jit(solution)/shard_map/ppermute | solution.py:754
  25.0 0.0 collective-permute-start.5
  25.0 0.0 copy-done.9
  25.0 0.0 copy-done.10
  25.0 0.0 copy-done.11
  25.0 0.0 copy-start
  25.1 2.2 %copy-done = bf16[64,128,256]{2,1,0:T(8,128)(2,1)S(1)} copy-done((bf16[64,128,256]{2,1,0:T(8,128)(2,1)S(1)}, bf16[64,128,256]{2,1,0:T(8,128)(2,1)}, u32[]{:S(2)}) %copy-start) | copy-done | bytes 4194328
  27.2 0.0 copy-start.8
  27.3 0.0 copy-start.12
  27.3 0.0 copy-start.13
  27.3 0.0 copy-start.6
  27.3 0.0 copy-start.7
  27.3 3.1 %turn_pairs.1 = (bf16[64,128,256]{2,1,0:T(8,128)(2,1)S(1)}, bf16[256,128]{1,0:T(8,128)(2,1)S(1)}, bf16[128,256]{1,0:T(8,128)(2,1)S(1)}) custom-call(s32[3]{0:T(128)S(1)} %copy-done.11, bf16[64,128,256]{2,1,0:T(8,128)(2,1)S(1)} %copy-done, bf16[64,128,256]{2,1,0:T(8,128)(2,1)} %collective-permute-done.other_pairs, bf16[128,256]{1,0:T(8,128)(2,1)S(1)} %copy-done.9, ...), custom_call_target="tpu_custom_call" | custom-call | bytes 12000000 | tf_op jit(solution)/shard_map/turn_pairs/pallas_call | solution.py:527
  30.4 0.0 collective-permute-done.7.rest_3_
  30.5 1.2 %collective-permute-done.6.rest_2_ = bf16[18,16,128]{2,1,0:T(8,128)(2,1)S(1)} collective-permute-done((bf16[18,16,128]{2,1,0:T(8,128)(2,1)}, bf16[18,16,128]{2,1,0:T(8,128)(2,1)S(1)}, u32[]{:S(2)}, u32[]{:S(2)}) %collective-permute-start.6) | collective-permute-done | bytes 73760 | tf_op jit(solution)/shard_map/ppermute | solution.py:754
  31.6 0.0 collective-permute-done.5.rest_1_
  31.6 0.0 collective-permute-done.4.out_other
  31.7 2.3 %nodes.3.rest_0_ = bf16[16,256]{1,0:T(8,128)(2,1)S(1)} custom-call(s32[1]{0:T(128)} %bitcast.8.place, bf16[128,256]{1,0:T(8,128)(2,1)S(1)} %copy-done.5, bf16[1056,256]{1,0:T(8,128)(2,1)S(1)} %copy-done.1, bf16[1056,256]{1,0:T(8,128)(2,1)S(1)} %collective-permute-done.4.out_other, f32[1,256]{1,0:T(1,128)S(1)} %bitcast.11, f32[1,256]{1,0:T(1,128)S(1)} %bitcast.12, ...), custom_call_target="tpu_custom_call" | custom-call | bytes 6000000 | tf_op jit(solution)/shard_map/nodes/pallas_call | solution.py:493
  34.0 2.7 %collective-permute-start.10 = (bf16[16,256]{1,0:T(8,128)(2,1)S(1)}, bf16[16,256]{1,0:T(8,128)(2,1)S(1)}, u32[]{:S(2)}, u32[]{:S(2)}) collective-permute-start(bf16[16,256]{1,0:T(8,128)(2,1)S(1)} %nodes.3.rest_0_), channel_id=1, source_target_pairs={{0,12},{4,8},{8,4},{12,0},{1,13},{5,9},{9,5},{13,1},{2,14},{6,10},... | collective-permute-start | bytes 24584 | tf_op jit(solution)/shard_map/ppermute | solution.py:754
  36.8 0.3 collective-permute-start.9
  37.1 1.4 %collective-permute-start.8 = (bf16[16,256]{1,0:T(8,128)(2,1)S(1)}, bf16[16,256]{1,0:T(8,128)(2,1)S(1)}, u32[]{:S(2)}, u32[]{:S(2)}) collective-permute-start(bf16[16,256]{1,0:T(8,128)(2,1)S(1)} %nodes.3.rest_0_), channel_id=1, source_target_pairs={{0,4},{4,0},{8,12},{12,8},{1,5},{5,1},{9,13},{13,9},{2,6},{6,2},{1... | collective-permute-start | bytes 24584 | tf_op jit(solution)/shard_map/ppermute | solution.py:754
  38.5 0.1 pad_add_fusion.place
  38.6 1.0 %collective-permute-done.10.rest_3_ = bf16[16,256]{1,0:T(8,128)(2,1)S(1)} collective-permute-done((bf16[16,256]{1,0:T(8,128)(2,1)S(1)}, bf16[16,256]{1,0:T(8,128)(2,1)S(1)}, u32[]{:S(2)}, u32[]{:S(2)}) %collective-permute-start.10) | collective-permute-done | bytes 8224 | tf_op jit(solution)/shard_map/ppermute | solution.py:754
  39.6 1.8 %collective-permute-done.9.rest_2_ = bf16[16,256]{1,0:T(8,128)(2,1)S(1)} collective-permute-done((bf16[16,256]{1,0:T(8,128)(2,1)S(1)}, bf16[16,256]{1,0:T(8,128)(2,1)S(1)}, u32[]{:S(2)}, u32[]{:S(2)}) %collective-permute-start.9) | collective-permute-done | bytes 8224 | tf_op jit(solution)/shard_map/ppermute | solution.py:754
  41.3 0.0 collective-permute-done.8.rest_1_
  41.3 6.8 %edges.1 = (bf16[64,128,256]{2,1,0:T(8,128)(2,1)}, bf16[65,64,256]{2,1,0:T(8,128)(2,1)S(1)}, bf16[128,256]{1,0:T(8,128)(2,1)}) custom-call(s32[2]{0:T(128)S(1)} %pad_add_fusion.place, bf16[64,128,256]{2,1,0:T(8,128)(2,1)S(1)} %get-tuple-element.25.turned, bf16[16,256]{1,0:T(8,128)(2,1)S(1)} %nodes.3.rest_0_, ...), custom_call_target="tpu_custom_call" | custom-call | bytes 24000000 | tf_op jit(solution)/shard_map/edges/pallas_call | solution.py:602
  48.1 0.0 collective-permute-start.11
  48.1 4.2 %collective-permute-done.11.arrived = bf16[65,64,256]{2,1,0:T(8,128)(2,1)S(1)} collective-permute-done((bf16[65,64,256]{2,1,0:T(8,128)(2,1)S(1)}, bf16[65,64,256]{2,1,0:T(8,128)(2,1)S(1)}, u32[]{:S(2)}, u32[]{:S(2)}) %collective-permute-start.11) | collective-permute-done | bytes 2129952 | tf_op jit(solution)/shard_map/ppermute | solution.py:702
  52.3 1.3 %finish.1 = (bf16[64,128,256]{2,1,0:T(8,128)(2,1)}, bf16[128,256]{1,0:T(8,128)(2,1)}) custom-call(bf16[65,64,256]{2,1,0:T(8,128)(2,1)S(1)} %collective-permute-done.11.arrived, bf16[64,128,256]{2,1,0:T(8,128)(2,1)} %get-tuple-element.32.pairs_in, bf16[128,256]{1,0:T(8,128)(2,1)} %get-tuple-element.33.nodes_in), custom_call_target="tpu_custom_call", output_to_operand_aliasing={{0}: (1, {}), {1}: (2, {})} | custom-call | bytes 3000000 | tf_op jit(solution)/shard_map/finish/pallas_call | solution.py:655
  (18 shorter events, 0.0 us)
Async XLA Ops:
  0.6 9.1 %collective-permute-start = (bf16[64,128,256]{2,1,0:T(8,128)(2,1)}, bf16[64,128,256]{2,1,0:T(8,128)(2,1)}, u32[]{:S(2)}, u32[]{:S(2)}) collective-permute-start(bf16[64,128,256]{2,1,0:T(8,128)(2,1)} %own_pairs.3), channel_id=1, source_target_pairs={{0,1},{1,0},{2,3},{3,2},{4,5},{5,4},{6,7},{7,6},{8,9},{9,8},{10,11... | collective-permute-start | bytes 12582920 | tf_op jit(solution)/shard_map/ppermute | solution.py:702
  2.9 6.8 %collective-permute-start.1 = (bf16[672,256]{1,0:T(8,128)(2,1)}, bf16[672,256]{1,0:T(8,128)(2,1)S(1)}, u32[]{:S(2)}, u32[]{:S(2)}) collective-permute-start(bf16[672,256]{1,0:T(8,128)(2,1)} %pack.1), channel_id=1, source_target_pairs={{0,1},{1,0},{2,3},{3,2},{4,5},{5,4},{6,7},{7,6},{8,9},{9,8},{10,11... | collective-permute-start | bytes 1032200 | tf_op jit(solution)/shard_map/ppermute | solution.py:702
  3.0 5.0 %collective-permute-start.2 = (bf16[64,256]{1,0:T(8,128)(2,1)}, bf16[64,256]{1,0:T(8,128)(2,1)S(1)}, u32[]{:S(2)}, u32[]{:S(2)}) collective-permute-start(bf16[64,256]{1,0:T(8,128)(2,1)} %rest_14_.1), channel_id=1, source_target_pairs={{0,2},{1,3},{2,0},{3,1},{4,6},{5,7},{6,4},{7,5},{8,10},{9,11},{10,... | collective-permute-start | bytes 98312 | tf_op jit(solution)/shard_map/ppermute | solution.py:710
  5.9 3.8 %collective-permute-start.3 = (bf16[64,256]{1,0:T(8,128)(2,1)}, bf16[64,256]{1,0:T(8,128)(2,1)S(1)}, u32[]{:S(2)}, u32[]{:S(2)}) collective-permute-start(bf16[64,256]{1,0:T(8,128)(2,1)} %rest_14_.1), channel_id=1, source_target_pairs={{0,3},{1,2},{2,1},{3,0},{4,7},{5,6},{6,5},{7,4},{8,11},{9,10},{10,... | collective-permute-start | bytes 98312 | tf_op jit(solution)/shard_map/ppermute | solution.py:710
  8.0 2.5 %copy-start.15 = (bf16[64,256]{1,0:T(8,128)(2,1)}, bf16[64,256]{1,0:T(8,128)(2,1)S(1)}, u32[]{:S(2)}) copy-start(bf16[64,256]{1,0:T(8,128)(2,1)S(1)} %collective-permute-done.2.rest_15_) | copy-start | bytes 98308
  9.7 0.7 %copy-start.16 = (bf16[64,256]{1,0:T(8,128)(2,1)}, bf16[64,256]{1,0:T(8,128)(2,1)S(1)}, u32[]{:S(2)}) copy-start(bf16[64,256]{1,0:T(8,128)(2,1)S(1)} %collective-permute-done.3.rest_16_) | copy-start | bytes 98308
  9.7 0.7 %copy-start.14 = (bf16[672,256]{1,0:T(8,128)(2,1)}, bf16[672,256]{1,0:T(8,128)(2,1)S(1)}, u32[]{:S(2)}) copy-start(bf16[672,256]{1,0:T(8,128)(2,1)S(1)} %collective-permute-done.1.rest_12_) | copy-start | bytes 1032196
  10.5 9.9 %copy-start.1 = (bf16[1056,256]{1,0:T(8,128)(2,1)S(1)}, bf16[1056,256]{1,0:T(8,128)(2,1)}, u32[]{:S(2)}) copy-start(bf16[1056,256]{1,0:T(8,128)(2,1)} %out_own.1) | copy-start | bytes 1622020
  10.5 14.6 %copy-start.9 = (bf16[128,256]{1,0:T(8,128)(2,1)S(1)}, bf16[128,256]{1,0:T(8,128)(2,1)}, u32[]{:S(2)}) copy-start(bf16[128,256]{1,0:T(8,128)(2,1)} %in_weight.1) | copy-start | bytes 196612
  10.5 14.6 %copy-start.10 = (bf16[256,128]{1,0:T(8,128)(2,1)S(1)}, bf16[256,128]{1,0:T(8,128)(2,1)}, u32[]{:S(2)}) copy-start(bf16[256,128]{1,0:T(8,128)(2,1)} %out_weight.1) | copy-start | bytes 196612
  10.5 14.6 %copy-start.11 = (s32[3]{0:T(128)S(1)}, s32[3]{0:T(128)}, u32[]{:S(2)}) copy-start(s32[3]{0:T(128)} %pad_add_fusion.1.place) | copy-start | bytes 40
  20.4 11.3 %collective-permute-start.4 = (bf16[1056,256]{1,0:T(8,128)(2,1)S(1)}, bf16[1056,256]{1,0:T(8,128)(2,1)S(1)}, u32[]{:S(2)}, u32[]{:S(2)}) collective-permute-start(bf16[1056,256]{1,0:T(8,128)(2,1)S(1)} %copy-done.1), channel_id=1, source_target_pairs={{0,1},{1,0},{2,3},{3,2},{4,5},{5,4},{6,7},{7,6},{8,9},{9,8},{10,11... | collective-permute-start | bytes 1622024 | tf_op jit(solution)/shard_map/ppermute | solution.py:702
  20.4 10.0 %collective-permute-start.7 = (bf16[18,16,128]{2,1,0:T(8,128)(2,1)}, bf16[18,16,128]{2,1,0:T(8,128)(2,1)S(1)}, u32[]{:S(2)}, u32[]{:S(2)}) collective-permute-start(bf16[18,16,128]{2,1,0:T(8,128)(2,1)} %get-tuple-element.20), channel_id=1, source_target_pairs={{0,4},{4,0},{8,12},{12,8},{1,5},{5,1},{9,13},{13,9},{2,6},{6,2},{1... | collective-permute-start | bytes 221192 | tf_op jit(solution)/shard_map/ppermute | solution.py:754
  22.4 9.2 %collective-permute-start.6 = (bf16[18,16,128]{2,1,0:T(8,128)(2,1)}, bf16[18,16,128]{2,1,0:T(8,128)(2,1)S(1)}, u32[]{:S(2)}, u32[]{:S(2)}) collective-permute-start(bf16[18,16,128]{2,1,0:T(8,128)(2,1)} %get-tuple-element.21), channel_id=1, source_target_pairs={{0,8},{4,12},{8,0},{12,4},{1,9},{5,13},{9,1},{13,5},{2,10},{6,14},... | collective-permute-start | bytes 221192 | tf_op jit(solution)/shard_map/ppermute | solution.py:754
  25.0 6.6 %collective-permute-start.5 = (bf16[18,16,128]{2,1,0:T(8,128)(2,1)}, bf16[18,16,128]{2,1,0:T(8,128)(2,1)S(1)}, u32[]{:S(2)}, u32[]{:S(2)}) collective-permute-start(bf16[18,16,128]{2,1,0:T(8,128)(2,1)} %get-tuple-element.22), channel_id=1, source_target_pairs={{0,12},{4,8},{8,4},{12,0},{1,13},{5,9},{9,5},{13,1},{2,14},{6,10},... | collective-permute-start | bytes 221192 | tf_op jit(solution)/shard_map/ppermute | solution.py:754
  25.0 2.2 %copy-start = (bf16[64,128,256]{2,1,0:T(8,128)(2,1)S(1)}, bf16[64,128,256]{2,1,0:T(8,128)(2,1)}, u32[]{:S(2)}) copy-start(bf16[64,128,256]{2,1,0:T(8,128)(2,1)} %own_pairs.3) | copy-start | bytes 12582916
  27.2 4.4 %copy-start.2 = (bf16[256,1024]{1,0:T(8,128)(2,1)S(1)}, bf16[256,1024]{1,0:T(8,128)(2,1)}, u32[]{:S(2)}) copy-start(bf16[256,1024]{1,0:T(8,128)(2,1)} %gate_weight.1) | copy-start | bytes 1572868
  27.2 4.4 %copy-start.3 = (bf16[256,1024]{1,0:T(8,128)(2,1)S(1)}, bf16[256,1024]{1,0:T(8,128)(2,1)}, u32[]{:S(2)}) copy-start(bf16[256,1024]{1,0:T(8,128)(2,1)} %up_weight.1) | copy-start | bytes 1572868
  27.2 4.4 %copy-start.4 = (bf16[1024,256]{1,0:T(8,128)(2,1)S(1)}, bf16[1024,256]{1,0:T(8,128)(2,1)}, u32[]{:S(2)}) copy-start(bf16[1024,256]{1,0:T(8,128)(2,1)} %down_weight.1) | copy-start | bytes 1572868
  27.2 4.4 %copy-start.5 = (bf16[128,256]{1,0:T(8,128)(2,1)S(1)}, bf16[128,256]{1,0:T(8,128)(2,1)}, u32[]{:S(2)}) copy-start(bf16[128,256]{1,0:T(8,128)(2,1)} %nodes.4) | copy-start | bytes 196612
  27.2 4.4 %copy-start.8 = (bf16[18,16,128]{2,1,0:T(8,128)(2,1)S(1)}, bf16[18,16,128]{2,1,0:T(8,128)(2,1)}, u32[]{:S(2)}) copy-start(bf16[18,16,128]{2,1,0:T(8,128)(2,1)} %get-tuple-element.19.rest_0_) | copy-start | bytes 221188
  27.3 4.4 %copy-start.12 = (f32[256]{0:T(256)S(1)}, f32[256]{0:T(256)}, u32[]{:S(2)}) copy-start(f32[256]{0:T(256)} %param.41) | copy-start | bytes 3076
  27.3 4.4 %copy-start.13 = (f32[256]{0:T(256)S(1)}, f32[256]{0:T(256)}, u32[]{:S(2)}) copy-start(f32[256]{0:T(256)} %param.42) | copy-start | bytes 3076
  27.3 14.1 %copy-start.6 = (f32[256,256]{1,0:T(8,128)S(1)}, f32[256,256]{1,0:T(8,128)}, u32[]{:S(2)}) copy-start(f32[256,256]{1,0:T(8,128)} %get-tuple-element.27.rest_4_) | copy-start | bytes 786436
  27.3 14.1 %copy-start.7 = (bf16[256,256]{1,0:T(8,128)(2,1)S(1)}, bf16[256,256]{1,0:T(8,128)(2,1)}, u32[]{:S(2)}) copy-start(bf16[256,256]{1,0:T(8,128)(2,1)} %rest_7_.3) | copy-start | bytes 393220
  34.0 5.5 %collective-permute-start.10 = (bf16[16,256]{1,0:T(8,128)(2,1)S(1)}, bf16[16,256]{1,0:T(8,128)(2,1)S(1)}, u32[]{:S(2)}, u32[]{:S(2)}) collective-permute-start(bf16[16,256]{1,0:T(8,128)(2,1)S(1)} %nodes.3.rest_0_), channel_id=1, source_target_pairs={{0,12},{4,8},{8,4},{12,0},{1,13},{5,9},{9,5},{13,1},{2,14},{6,10},... | collective-permute-start | bytes 24584 | tf_op jit(solution)/shard_map/ppermute | solution.py:754
  36.8 4.5 %collective-permute-start.9 = (bf16[16,256]{1,0:T(8,128)(2,1)S(1)}, bf16[16,256]{1,0:T(8,128)(2,1)S(1)}, u32[]{:S(2)}, u32[]{:S(2)}) collective-permute-start(bf16[16,256]{1,0:T(8,128)(2,1)S(1)} %nodes.3.rest_0_), channel_id=1, source_target_pairs={{0,8},{4,12},{8,0},{12,4},{1,9},{5,13},{9,1},{13,5},{2,10},{6,14},... | collective-permute-start | bytes 24584 | tf_op jit(solution)/shard_map/ppermute | solution.py:754
  37.1 4.2 %collective-permute-start.8 = (bf16[16,256]{1,0:T(8,128)(2,1)S(1)}, bf16[16,256]{1,0:T(8,128)(2,1)S(1)}, u32[]{:S(2)}, u32[]{:S(2)}) collective-permute-start(bf16[16,256]{1,0:T(8,128)(2,1)S(1)} %nodes.3.rest_0_), channel_id=1, source_target_pairs={{0,4},{4,0},{8,12},{12,8},{1,5},{5,1},{9,13},{13,9},{2,6},{6,2},{1... | collective-permute-start | bytes 24584 | tf_op jit(solution)/shard_map/ppermute | solution.py:754
  48.1 4.2 %collective-permute-start.11 = (bf16[65,64,256]{2,1,0:T(8,128)(2,1)S(1)}, bf16[65,64,256]{2,1,0:T(8,128)(2,1)S(1)}, u32[]{:S(2)}, u32[]{:S(2)}) collective-permute-start(bf16[65,64,256]{2,1,0:T(8,128)(2,1)S(1)} %get-tuple-element.31), channel_id=1, source_target_pairs={{0,1},{1,0},{2,3},{3,2},{4,5},{5,4},{6,7},{7,6},{8,9},{9,8},{10,11... | collective-permute-start | bytes 6389768 | tf_op jit(solution)/shard_map/ppermute | solution.py:702
